TPU v7x, 512 devices: a whole 4x4x16 slice. The times are simulated.
512 devices in a mesh: band: 32 (over z, y_lo), grid: 16 (over x, y_hi, core).
Axes of the slice: x: 4, y: 4 (y_hi: 2, y_lo: 2; y = y_hi * 2 + y_lo), z: 16, core: 2. Of those that a mesh axis runs over, the one named last changes fastest.
Arguments:
- orbitals: float32 [128, 128, 128, 128], P('band', 'grid'), may hold values from -6 to 6
- spin_channel: int32 [128], replicated, may hold values from 0 to 1
Outputs:
- exchange_action: float32 [128, 128, 128, 128], P('band', 'grid')
All inputs are finite; a program needn't handle non-finite values.
Results may differ from a plain program's by a relative error of at most 0.0003.
Values sent between devices are 32-bit elements; how exact they have to be, the bound alone decides.
No kernel may reach another device: no remote copies, remote signals or barrier semaphores. Data moves between devices by JAX's collectives and lax.ppermute only.
A program may use at most 64 MiB of HBM per device.

v0:
```python
import math

import jax
import jax.numpy as jnp
import numpy as np
from jax import lax
from jax.experimental import pallas as pl
from jax.experimental.pallas import tpu as pltpu
from jax.sharding import PartitionSpec as P

PARTNER_BIT = 2
ORBITALS = 4
LANES = 128
PLANES = 8
VMEM_BYTES = 40 * 2**20


def fourier_tables(length, planes):
    number = np.arange(length)
    angles = (number[:, None] * number[None, :] % length) * (2.0 * math.pi / length)
    cosine, sine = np.cos(angles), np.sin(angles)
    plus = np.block([[cosine, -sine], [sine, cosine]])
    minus = plus.T
    blocks = length // planes
    order = np.arange(2 * length).reshape(2, blocks, planes).transpose(1, 0, 2).reshape(-1)
    return plus, plus[:, order], minus, minus[order, :]


def two_parts(table):
    exact = jnp.asarray(table.astype(np.float32))
    high = exact.astype(jnp.bfloat16)
    low = (exact - high.astype(jnp.float32)).astype(jnp.bfloat16)
    return jnp.stack([high, low])


def split(value):
    high = value.astype(jnp.bfloat16)
    return high, (value - high.astype(jnp.float32)).astype(jnp.bfloat16)


def dot(a, b):
    return jnp.dot(a, b, preferred_element_type=jnp.float32)


def from_left(table_ref, value):
    high, low = split(value)
    return dot(table_ref[0], high) + dot(table_ref[0], low) + dot(table_ref[1], high)


def from_right(value, table_ref):
    high, low = split(value)
    return dot(high, table_ref[0]) + dot(low, table_ref[0]) + dot(high, table_ref[1])


def forward_kernel(choice, spin, u_ref, vw_ref, right_ref, left_ref, out_ref):
    planes = u_ref.shape[0]
    size = u_ref.shape[1]
    s0, s1 = spin[0], spin[1]
    rows = []
    for x in range(planes):
        u = u_ref[x]
        rows.append(jnp.concatenate([u * vw_ref[0, x] * s0, u * vw_ref[1, x] * s1], axis=1))
    along_z = from_right(jnp.concatenate(rows, axis=0), right_ref)
    columns = []
    for x in range(planes):
        part = along_z[x * size:(x + 1) * size]
        columns.append(jnp.concatenate([part[:, :LANES], part[:, LANES:]], axis=0))
    along_y = from_left(left_ref, jnp.concatenate(columns, axis=1))
    blocks = out_ref.shape[0]
    for x in range(planes):
        for c in range(2):
            block = along_y[c * size:(c + 1) * size, x * LANES:(x + 1) * LANES]
            out_ref[:, c, x] = block.reshape(blocks, size // blocks, LANES)


def solve_kernel(in_ref, kernel_ref, left_ref, right_ref, out_ref):
    columns = kernel_ref.shape[0]
    rows = in_ref.shape[0] // columns
    for y in range(0, columns, 2):
        value = jnp.concatenate([in_ref[pl.ds(y + k, rows, stride=columns), :] for k in range(2)], axis=1)
        weight = jnp.concatenate([kernel_ref[y], kernel_ref[y + 1]], axis=1)
        spectrum = from_left(left_ref, value) * jnp.concatenate([weight, weight], axis=0)
        solved = from_left(right_ref, spectrum)
        for k in range(2):
            out_ref[pl.ds(y + k, rows, stride=columns), :] = solved[:, k * LANES:(k + 1) * LANES]


def inverse_kernel(
    choice, spin, in_ref, u_ref, vw_ref, before_ref, sum_ref, left_ref, right_ref, total_ref, back_ref
):
    planes = u_ref.shape[0]
    size = u_ref.shape[1]
    s0, s1, keep = spin[0], spin[1], spin[2]
    columns = []
    for x in range(planes):
        parts = [in_ref[:, c, x].reshape(size, LANES) for c in range(2)]
        columns.append(jnp.concatenate(parts, axis=0))
    along_y = from_left(left_ref, jnp.concatenate(columns, axis=1))
    rows = []
    for x in range(planes):
        part = along_y[:, x * LANES:(x + 1) * LANES]
        rows.append(jnp.concatenate([part[:size], part[size:]], axis=1))
    potential = from_right(jnp.concatenate(rows, axis=0), right_ref)
    for x in range(planes):
        part = potential[x * size:(x + 1) * size]
        v0 = part[:, :LANES] * s0
        v1 = part[:, LANES:] * s1
        u = u_ref[x]
        total_ref[0, x] = sum_ref[0, x] - v0 * u
        total_ref[1, x] = sum_ref[1, x] - v1 * u
        back_ref[x] = before_ref[x] * keep - (v0 * vw_ref[0, x] + v1 * vw_ref[1, x])


def add_kernel(choice, more_ref, sum_ref, total_ref):
    total_ref[0] = sum_ref[0] + more_ref[...]


def params():
    return pltpu.CompilerParams(dimension_semantics=("arbitrary",), vmem_limit_bytes=VMEM_BYTES)


STEP = 2


def forward(choice, spin, u, orbitals, right, left, blocks):
    planes, size, lanes = u.shape
    table = pl.BlockSpec((2, 2 * size, 2 * size), lambda i, c, s: (0, 0, 0))
    return pl.pallas_call(
        forward_kernel,
        grid_spec=pltpu.PrefetchScalarGridSpec(
            num_scalar_prefetch=2,
            grid=(planes // STEP,),
            in_specs=[
                pl.BlockSpec((STEP, size, lanes), lambda i, c, s: (i, 0, 0)),
                pl.BlockSpec((2, STEP, size, lanes), lambda i, c, s: (c[0], i, 0, 0)),
                table,
                table,
            ],
            out_specs=pl.BlockSpec((blocks, 2, STEP, size // blocks, lanes), lambda i, c, s: (0, 0, i, 0, 0)),
        ),
        out_shape=jax.ShapeDtypeStruct((blocks, 2, planes, size // blocks, lanes), jnp.float32),
        compiler_params=params(),
        name="forward_planes",
    )(choice, spin, u, orbitals, right, left)


def solve(field, kernel, left, right):
    blocks, two, planes, columns, lanes = field.shape
    flat = (blocks * two * planes * columns, lanes)
    solved = pl.pallas_call(
        solve_kernel,
        out_shape=jax.ShapeDtypeStruct(flat, jnp.float32),
        compiler_params=pltpu.CompilerParams(vmem_limit_bytes=VMEM_BYTES),
        name="solve_columns",
    )(field.reshape(flat), kernel, left, right)
    return solved.reshape(field.shape)


def inverse(choice, spin, field, u, orbitals, before, total, left, right):
    planes, size, lanes = u.shape
    blocks = field.shape[0]
    table = pl.BlockSpec((2, 2 * size, 2 * size), lambda i, c, s: (0, 0, 0))
    plane = pl.BlockSpec((STEP, size, lanes), lambda i, c, s: (i, 0, 0))
    pair = pl.BlockSpec((2, STEP, size, lanes), lambda i, c, s: (c[0], i, 0, 0))
    return pl.pallas_call(
        inverse_kernel,
        grid_spec=pltpu.PrefetchScalarGridSpec(
            num_scalar_prefetch=2,
            grid=(planes // STEP,),
            in_specs=[
                pl.BlockSpec((blocks, 2, STEP, size // blocks, lanes), lambda i, c, s: (0, 0, i, 0, 0)),
                plane,
                pair,
                plane,
                pair,
                table,
                table,
            ],
            out_specs=[pair, plane],
        ),
        out_shape=[
            jax.ShapeDtypeStruct(total.shape, jnp.float32),
            jax.ShapeDtypeStruct(u.shape, jnp.float32),
        ],
        input_output_aliases={6: 0},
        compiler_params=params(),
        name="inverse_planes",
    )(choice, spin, field, u, orbitals, before, total, left, right)


def add_into(choice, total, more):
    planes, size, lanes = more.shape
    one = pl.BlockSpec((1, STEP, size, lanes), lambda i, c: (c[0], i, 0, 0))
    return pl.pallas_call(
        add_kernel,
        grid_spec=pltpu.PrefetchScalarGridSpec(
            num_scalar_prefetch=1,
            grid=(planes // STEP,),
            in_specs=[pl.BlockSpec((STEP, size, lanes), lambda i, c: (i, 0, 0)), one],
            out_specs=one,
        ),
        out_shape=jax.ShapeDtypeStruct(total.shape, jnp.float32),
        input_output_aliases={2: 0},
        compiler_params=params(),
        name="add_received",
    )(choice, more, total)


def signed(number, length):
    return jnp.where(number < length // 2, number, number - length)


def coulomb_block(size, column_count, first_column):
    strength = math.sqrt(size**3) / 4.0
    along_x = signed(jnp.arange(size, dtype=jnp.int32), size)
    along_y = signed(first_column + jnp.arange(column_count, dtype=jnp.int32), size)
    squared = along_y[:, None, None] ** 2 + along_x[None, :, None] ** 2 + along_x[None, None, :] ** 2
    bounded = jnp.maximum(squared, 1).astype(jnp.float32)
    kernel = jnp.where(squared == 0, jnp.float32(0.0), jnp.float32(strength) / bounded)
    return kernel * jnp.float32(1.0 / size**3)


def role_of(group):
    return ((group >> PARTNER_BIT) ^ (group >> (PARTNER_BIT - 1))) & 1


def exchange(field):
    return lax.all_to_all(field, "grid", split_axis=0, concat_axis=0, tiled=True)


def shards(orbitals, spin_channel):
    count, planes, size, lanes = orbitals.shape
    grid_size = lax.axis_size("grid")
    groups = lax.axis_size("band")
    band = lax.axis_index("band")
    partner = band ^ (1 << PARTNER_BIT)
    role = role_of(band)
    first = role == 0
    every = [(g, g ^ (1 << PARTNER_BIT)) for g in range(groups)]
    to_first = [(g, p) for g, p in every if role_of(p) == 0]
    to_second = [(g, p) for g, p in every if role_of(p) == 1]

    own_spin = lax.dynamic_slice_in_dim(spin_channel, band * count, count)
    other_spin = lax.dynamic_slice_in_dim(spin_channel, partner * count, count)

    plus, plus_x, minus, minus_x = (two_parts(t) for t in fourier_tables(size, planes))
    kernel = coulomb_block(size, size // grid_size, lax.axis_index("grid") * (size // grid_size))

    def index(a, b):
        return jnp.where(first, a, b).astype(jnp.int32)

    def orbital(number):
        return lax.dynamic_index_in_dim(orbitals, number, 0, keepdims=False)

    received = []
    for k in range(ORBITALS):
        if k % 2 == 0:
            sent = orbital(index(2 + k // 2, k))
        else:
            sent = orbitals[k]
        if received:
            sent, received[-1] = lax.optimization_barrier((sent, received[-1]))
        received.append(lax.ppermute(sent, "band", every if k % 2 == 0 else to_first))

    chosen, spins, us = [], [], []
    for k in range(ORBITALS):
        pair = index(0, k % 2)
        chosen.append(pair.reshape(1))
        far = other_spin[index(k, 2 + k // 2)]
        near = lax.dynamic_slice_in_dim(own_spin, 2 * pair, 2)
        same = (near == far).astype(jnp.float32)
        keep = index(0, k % 2).astype(jnp.float32)
        spins.append(jnp.concatenate([same, keep.reshape(1)]))
        us.append(received[k] if k % 2 == 0 else jnp.where(first, received[k], received[k - 1]))

    def planes_of(k):
        return forward(chosen[k], spins[k], us[k], orbitals, minus, plus, grid_size)

    total = jnp.zeros_like(orbitals)
    before = jnp.zeros_like(us[0])
    returned = []
    ahead = planes_of(0)
    arrived = exchange(ahead)
    for k in range(ORBITALS):
        solved = solve(arrived, kernel, plus_x, minus_x)
        if k + 1 < ORBITALS:
            both = exchange(jnp.concatenate([planes_of(k + 1), solved], axis=1))
            arrived, back = both[:, :2], both[:, 2:]
        else:
            back = exchange(solved)
        total, before = inverse(
            chosen[k], spins[k], back, us[k], orbitals, before, total, minus, plus
        )
        returned.append(lax.ppermute(before, "band", every if k % 2 == 1 else to_second))
    for k in range(ORBITALS):
        place = index(2 + k // 2, k)
        total = add_into(place.reshape(1), total, returned[k])
    return total


def solution(mesh):
    return jax.shard_map(
        shards,
        mesh=mesh,
        in_specs=(P("band", "grid", None, None), P()),
        out_specs=P("band", "grid", None, None),
        check_vma=False,
    )
```

profile of v0, /device:TPU:1, one launch (start us, length us, event | category | flops | bytes accessed | tf_op | source)
XLA Modules:
  0.0 284.8 jit_solution(1986773588762034100)
XLA Ops:
  0.0 3.0 %slice_bitcast_fusion.1 = (f32[8,128,128]{2,1,0:T(8,128)}, f32[8,128,128]{2,1,0:T(8,128)}, f32[8,128,128]{2,1,0:T(8,128)}, f32[8,128,128]{2,1,0:T(8,128)}) fusion(f32[4,8,128,128]{3,2,1,0:T(8,128)} %vw_ref.15, s32[]{:T(128)} %select_n.110, s32[]{:T(128)} %select_n.109), kind=kLoop, calls=%fused_computation.12 | loop fusion | bytes 4194312 | tf_op jit(solution)/shard_map/squeeze | solution.py:260
  3.0 5.7 %collective-permute-start = (f32[8,128,128]{2,1,0:T(8,128)}, f32[8,128,128]{2,1,0:T(8,128)S(1)}, u32[]{:S(2)}, u32[]{:S(2)}) collective-permute-start(f32[8,128,128]{2,1,0:T(8,128)} %get-tuple-element.40), channel_id=1, source_target_pairs={{0,64},{16,80},{32,96},{48,112},{64,0},{80,16},{96,32},{112,48},{1... | collective-permute-start | bytes 1572872 | tf_op jit(solution)/shard_map/ppermute | solution.py:263
  8.8 0.7 fusion.11
  9.5 0.1 fusion.12
  9.6 1.2 slice_compare_fusion.1
  10.8 0.1 fusion.5.spin
  10.9 20.3 %collective-permute-done.u_ref = f32[8,128,128]{2,1,0:T(8,128)S(1)} collective-permute-done((f32[8,128,128]{2,1,0:T(8,128)}, f32[8,128,128]{2,1,0:T(8,128)S(1)}, u32[]{:S(2)}, u32[]{:S(2)}) %collective-permute-start) | collective-permute-done | bytes 524320 | tf_op jit(solution)/shard_map/ppermute | solution.py:263
  31.2 3.5 %forward_planes.7 = f32[16,2,8,8,128]{4,3,2,1,0:T(8,128)S(1)} custom-call(s32[1]{0:T(128)} %constant.78.clone.1.choice, f32[3]{0:T(128)S(1)} %fusion.5.spin, f32[8,128,128]{2,1,0:T(8,128)S(1)} %collective-permute-done.u_ref, f32[4,8,128,128]{3,2,1,0:T(8,128)S(1)} %copy-done, bf16[2,256,256]{2,1,0:T(8,128)(2,1)S(1)} %copy-done.2, ...), custom_call_target="tpu_custom_call" | custom-call | tf_op jit(solution)/shard_map/forward_planes/pallas_call | solution.py:128
  34.7 1.0 copy-done.15
  35.7 8.9 %all-to-all-start = ((f32[16,2,8,8,128]{4,3,2,1,0:T(8,128)}), f32[16,2,8,8,128]{4,3,2,1,0:T(8,128)}, u32[]{:S(2)}, u32[]{:S(2)}) async-start(f32[16,2,8,8,128]{4,3,2,1,0:T(8,128)} %copy-done.15), calls=%async_computation | async-start | bytes 2097152 | tf_op jit(solution)/shard_map/all_to_all | solution.py:228
  44.6 0.6 dynamic_slice.44
  45.2 1.4 compare_convert_fusion
  46.5 1.3 collective-permute-start.1
  47.8 0.1 pad_maximum_fusion.4.spin
  47.9 0.1 broadcast_add_fusion
  48.0 0.2 fusion.3.kernel_ref
  48.2 14.7 %collective-permute-done.1 = f32[8,128,128]{2,1,0:T(8,128)S(1)} collective-permute-done((f32[8,128,128]{2,1,0:T(8,128)}, f32[8,128,128]{2,1,0:T(8,128)S(1)}, u32[]{:S(2)}, u32[]{:S(2)}) %collective-permute-start.1) | collective-permute-done | bytes 524320 | tf_op jit(solution)/shard_map/ppermute | solution.py:263
  63.0 3.5 %forward_planes.6 = f32[16,2,8,8,128]{4,3,2,1,0:T(8,128)S(1)} custom-call(s32[1]{0:T(128)} %bitcast.choice, f32[3]{0:T(128)S(1)} %pad_maximum_fusion.4.spin, f32[8,128,128]{2,1,0:T(8,128)S(1)} %broadcast_select_fusion.u_ref, f32[4,8,128,128]{3,2,1,0:T(8,128)S(1)} %copy-done, bf16[2,256,256]{2,1,0:T(8,128)(2,1)S(1)} %copy-done.2, ...), custom_call_target="tpu_custom_call" | custom-call | tf_op jit(solution)/shard_map/forward_planes/pallas_call | solution.py:128
  66.5 0.8 copy-done.5
  67.3 1.0 copy-done.21
  68.3 0.9 copy-done.12
  69.3 2.6 solve_columns.4
  71.9 1.6 pad_maximum_fusion
  73.4 7.8 %all-to-all-start.1 = ((f32[16,4,8,8,128]{4,3,2,1,0:T(8,128)}), f32[16,4,8,8,128]{4,3,2,1,0:T(8,128)}, u32[]{:S(2)}, u32[]{:S(2)}) async-start(f32[16,4,8,8,128]{4,3,2,1,0:T(8,128)} %pad_maximum_fusion), calls=%async_computation.1 | async-start | bytes 4194304 | tf_op jit(solution)/shard_map/all_to_all | solution.py:228
  81.3 2.3 collective-permute-start.2
  83.6 0.1 fusion.4.spin
  83.7 25.3 %collective-permute-done.2.u_ref = f32[8,128,128]{2,1,0:T(8,128)S(1)} collective-permute-done((f32[8,128,128]{2,1,0:T(8,128)}, f32[8,128,128]{2,1,0:T(8,128)S(1)}, u32[]{:S(2)}, u32[]{:S(2)}) %collective-permute-start.2) | collective-permute-done | bytes 524320 | tf_op jit(solution)/shard_map/ppermute | solution.py:263
  109.0 3.5 %forward_planes.5 = f32[16,2,8,8,128]{4,3,2,1,0:T(8,128)S(1)} custom-call(s32[1]{0:T(128)} %constant.78.clone.1.choice, f32[3]{0:T(128)S(1)} %fusion.4.spin, f32[8,128,128]{2,1,0:T(8,128)S(1)} %collective-permute-done.2.u_ref, f32[4,8,128,128]{3,2,1,0:T(8,128)S(1)} %copy-done, bf16[2,256,256]{2,1,0:T(8,128)(2,1)S(1)} %copy-done.2, ...), custom_call_target="tpu_custom_call" | custom-call | tf_op jit(solution)/shard_map/forward_planes/pallas_call | solution.py:128
  112.5 0.8 copy-done.7
  113.3 1.0 copy-done.17
  114.3 2.8 fusion.8
  117.1 1.3 solve_columns.5
  118.4 1.6 pad_maximum_fusion.1
  120.0 7.7 %all-to-all-start.2 = ((f32[16,4,8,8,128]{4,3,2,1,0:T(8,128)}), f32[16,4,8,8,128]{4,3,2,1,0:T(8,128)}, u32[]{:S(2)}, u32[]{:S(2)}) async-start(f32[16,4,8,8,128]{4,3,2,1,0:T(8,128)} %pad_maximum_fusion.1), calls=%async_computation.2 | async-start | bytes 4194304 | tf_op jit(solution)/shard_map/all_to_all | solution.py:228
  127.7 1.3 collective-permute-start.3
  129.0 0.1 pad_maximum_fusion.3.spin
  129.0 15.1 %collective-permute-done.3 = f32[8,128,128]{2,1,0:T(8,128)S(1)} collective-permute-done((f32[8,128,128]{2,1,0:T(8,128)}, f32[8,128,128]{2,1,0:T(8,128)S(1)}, u32[]{:S(2)}, u32[]{:S(2)}) %collective-permute-start.3) | collective-permute-done | bytes 524320 | tf_op jit(solution)/shard_map/ppermute | solution.py:263
  144.2 3.5 %forward_planes.4 = f32[16,2,8,8,128]{4,3,2,1,0:T(8,128)S(1)} custom-call(s32[1]{0:T(128)} %bitcast.choice, f32[3]{0:T(128)S(1)} %pad_maximum_fusion.3.spin, f32[8,128,128]{2,1,0:T(8,128)S(1)} %broadcast_select_fusion.1.u_ref, f32[4,8,128,128]{3,2,1,0:T(8,128)S(1)} %copy-done, bf16[2,256,256]{2,1,0:T(8,128)(2,1)S(1)} %copy-done.2, ...), custom_call_target="tpu_custom_call" | custom-call | tf_op jit(solution)/shard_map/forward_planes/pallas_call | solution.py:128
  147.7 0.8 copy-done.9
  148.5 1.0 copy-done.19
  149.5 6.7 %all-to-all-done.2 = f32[16,4,8,8,128]{4,3,2,1,0:T(8,128)} async-done(((f32[16,4,8,8,128]{4,3,2,1,0:T(8,128)}), f32[16,4,8,8,128]{4,3,2,1,0:T(8,128)}, u32[]{:S(2)}, u32[]{:S(2)}) %all-to-all-start.2) | async-done | bytes 2097184 | tf_op jit(solution)/shard_map/all_to_all | solution.py:228
  156.2 2.8 fusion.9
  159.1 1.3 solve_columns.6
  160.4 0.2 pad_maximum_fusion.2
  160.6 33.5 %all_to_all.25 = f32[16,4,8,8,128]{4,3,2,1,0:T(8,128)S(1)} all-to-all(f32[16,4,8,8,128]{4,3,2,1,0:T(8,128)S(1)} %pad_maximum_fusion.2), channel_id=1, replica_groups=mesh['band'=32,'grid'=16] {'grid'}, dimensions={0} | all-to-all | bytes 4194304 | tf_op jit(solution)/shard_map/all_to_all | solution.py:228
  194.1 1.2 fusion.10
  195.3 1.3 solve_columns.7
  196.6 1.0 copy-done.16
  197.6 5.5 %all-to-all-start.4 = ((f32[16,2,8,8,128]{4,3,2,1,0:T(8,128)}), f32[16,2,8,8,128]{4,3,2,1,0:T(8,128)}, u32[]{:S(2)}, u32[]{:S(2)}) async-start(f32[16,2,8,8,128]{4,3,2,1,0:T(8,128)} %bitcast.25), calls=%async_computation.4 | async-start | bytes 2097152 | tf_op jit(solution)/shard_map/all_to_all | solution.py:228
  203.1 1.6 broadcast_in_dim.12.sum_ref
  204.7 5.5 %inverse_planes.4 = (f32[4,8,128,128]{3,2,1,0:T(8,128)}, f32[8,128,128]{2,1,0:T(8,128)}) custom-call(s32[1]{0:T(128)} %constant.78.clone.1.choice, f32[3]{0:T(128)S(1)} %fusion.5.spin, f32[16,2,8,8,128]{4,3,2,1,0:T(8,128)S(1)} %copy-done.23, f32[8,128,128]{2,1,0:T(8,128)S(1)} %copy-done.4, ...), custom_call_target="tpu_custom_call", output_to_operand_aliasing={{0}: (6, {})} | custom-call | tf_op jit(solution)/shard_map/inverse_planes/pallas_call | solution.py:165
  210.3 2.1 collective-permute-start.7
  212.4 5.6 %inverse_planes.5 = (f32[4,8,128,128]{3,2,1,0:T(8,128)}, f32[8,128,128]{2,1,0:T(8,128)}) custom-call(s32[1]{0:T(128)} %bitcast.choice, f32[3]{0:T(128)S(1)} %pad_maximum_fusion.4.spin, f32[16,2,8,8,128]{4,3,2,1,0:T(8,128)S(1)} %copy-done.25, f32[8,128,128]{2,1,0:T(8,128)S(1)} %copy-done.6, ...), custom_call_target="tpu_custom_call", output_to_operand_aliasing={{0}: (6, {})} | custom-call | tf_op jit(solution)/shard_map/inverse_planes/pallas_call | solution.py:165
  218.0 1.9 collective-permute-start.6
  219.9 5.7 %inverse_planes.6 = (f32[4,8,128,128]{3,2,1,0:T(8,128)}, f32[8,128,128]{2,1,0:T(8,128)}) custom-call(s32[1]{0:T(128)} %constant.78.clone.1.choice, f32[3]{0:T(128)S(1)} %fusion.4.spin, f32[16,2,8,8,128]{4,3,2,1,0:T(8,128)S(1)} %copy-done.24, f32[8,128,128]{2,1,0:T(8,128)S(1)} %copy-done.8, ...), custom_call_target="tpu_custom_call", output_to_operand_aliasing={{0}: (6, {})} | custom-call | tf_op jit(solution)/shard_map/inverse_planes/pallas_call | solution.py:165
  225.6 5.1 %collective-permute-start.5 = (f32[8,128,128]{2,1,0:T(8,128)}, f32[8,128,128]{2,1,0:T(8,128)}, u32[]{:S(2)}, u32[]{:S(2)}) collective-permute-start(f32[8,128,128]{2,1,0:T(8,128)} %get-tuple-element.29.before_ref), channel_id=1, source_target_pairs={{0,64},{16,80},{96,32},{112,48},{128,192},{144,208},{224,160},{240... | collective-permute-start | bytes 1572872 | tf_op jit(solution)/shard_map/ppermute | solution.py:294
  230.7 5.7 %inverse_planes.7 = (f32[4,8,128,128]{3,2,1,0:T(8,128)}, f32[8,128,128]{2,1,0:T(8,128)}) custom-call(s32[1]{0:T(128)} %bitcast.choice, f32[3]{0:T(128)S(1)} %pad_maximum_fusion.3.spin, f32[16,2,8,8,128]{4,3,2,1,0:T(8,128)} %all-to-all-done.4.in_ref, f32[8,128,128]{2,1,0:T(8,128)S(1)} %copy-done.10, ...), custom_call_target="tpu_custom_call", output_to_operand_aliasing={{0}: (6, {})} | custom-call | tf_op jit(solution)/shard_map/inverse_planes/pallas_call | solution.py:165
  236.4 1.9 collective-permute-start.4
  238.3 3.3 %add_received.4.sum_ref = f32[4,8,128,128]{3,2,1,0:T(8,128)} custom-call(s32[1]{0:T(128)} %bitcast.20.choice, f32[8,128,128]{2,1,0:T(8,128)} %collective-permute-done.7.more_ref, f32[4,8,128,128]{3,2,1,0:T(8,128)} %get-tuple-element.32.sum_ref), custom_call_target="tpu_custom_call", output_to_operand_aliasing={{}: (2, {})} | custom-call | tf_op jit(solution)/shard_map/add_received/pallas_call | solution.py:194
  241.7 28.8 %collective-permute-done.6.more_ref = f32[8,128,128]{2,1,0:T(8,128)} collective-permute-done((f32[8,128,128]{2,1,0:T(8,128)}, f32[8,128,128]{2,1,0:T(8,128)}, u32[]{:S(2)}, u32[]{:S(2)}) %collective-permute-start.6) | collective-permute-done | bytes 524320 | tf_op jit(solution)/shard_map/ppermute | solution.py:294
  270.5 3.3 %add_received.5.sum_ref = f32[4,8,128,128]{3,2,1,0:T(8,128)} custom-call(s32[1]{0:T(128)} %bitcast.19.choice, f32[8,128,128]{2,1,0:T(8,128)} %collective-permute-done.6.more_ref, f32[4,8,128,128]{3,2,1,0:T(8,128)} %add_received.4.sum_ref), custom_call_target="tpu_custom_call", output_to_operand_aliasing={{}: (2, {})} | custom-call | tf_op jit(solution)/shard_map/add_received/pallas_call | solution.py:194
  273.8 3.3 %add_received.6.sum_ref = f32[4,8,128,128]{3,2,1,0:T(8,128)} custom-call(s32[1]{0:T(128)} %bitcast.18.choice, f32[8,128,128]{2,1,0:T(8,128)} %collective-permute-done.5.more_ref, f32[4,8,128,128]{3,2,1,0:T(8,128)} %add_received.5.sum_ref), custom_call_target="tpu_custom_call", output_to_operand_aliasing={{}: (2, {})} | custom-call | tf_op jit(solution)/shard_map/add_received/pallas_call | solution.py:194
  277.1 4.5 %collective-permute-done.4.more_ref = f32[8,128,128]{2,1,0:T(8,128)S(1)} collective-permute-done((f32[8,128,128]{2,1,0:T(8,128)}, f32[8,128,128]{2,1,0:T(8,128)S(1)}, u32[]{:S(2)}, u32[]{:S(2)}) %collective-permute-start.4) | collective-permute-done | bytes 524320 | tf_op jit(solution)/shard_map/ppermute | solution.py:294
  281.6 3.2 %add_received.7 = f32[4,8,128,128]{3,2,1,0:T(8,128)} custom-call(s32[1]{0:T(128)} %constant.68.clone.1.choice, f32[8,128,128]{2,1,0:T(8,128)S(1)} %collective-permute-done.4.more_ref, f32[4,8,128,128]{3,2,1,0:T(8,128)} %add_received.6.sum_ref), custom_call_target="tpu_custom_call", output_to_operand_aliasing={{}: (2, {})} | custom-call | tf_op jit(solution)/shard_map/add_received/pallas_call | solution.py:194
  (55 shorter events, 0.3 us)
Async XLA Ops:
  0.0 8.8 %copy-start.26 = (s32[128]{0:T(128)S(1)}, s32[128]{0:T(128)}, u32[]{:S(2)}) copy-start(s32[128]{0:T(128)} %param.7) | copy-start | bytes 1540
  0.0 31.2 %copy-start = (f32[4,8,128,128]{3,2,1,0:T(8,128)S(1)}, f32[4,8,128,128]{3,2,1,0:T(8,128)}, u32[]{:S(2)}) copy-start(f32[4,8,128,128]{3,2,1,0:T(8,128)} %vw_ref.15) | copy-start | bytes 6291460
  0.0 31.2 %copy-start.1 = (bf16[2,256,256]{2,1,0:T(8,128)(2,1)S(1)}, bf16[2,256,256]{2,1,0:T(8,128)(2,1)}, u32[]{:S(2)}) copy-start(bf16[2,256,256]{2,1,0:T(8,128)(2,1)} %constant.105.left_ref.right_ref) | copy-start | bytes 786436
  0.0 31.2 %copy-start.2 = (bf16[2,256,256]{2,1,0:T(8,128)(2,1)S(1)}, bf16[2,256,256]{2,1,0:T(8,128)(2,1)}, u32[]{:S(2)}) copy-start(bf16[2,256,256]{2,1,0:T(8,128)(2,1)} %constant.98.right_ref.left_ref) | copy-start | bytes 786436
  3.0 28.1 %collective-permute-start = (f32[8,128,128]{2,1,0:T(8,128)}, f32[8,128,128]{2,1,0:T(8,128)S(1)}, u32[]{:S(2)}, u32[]{:S(2)}) collective-permute-start(f32[8,128,128]{2,1,0:T(8,128)} %get-tuple-element.40), channel_id=1, source_target_pairs={{0,64},{16,80},{32,96},{48,112},{64,0},{80,16},{96,32},{112,48},{1... | collective-permute-start | bytes 1572872 | tf_op jit(solution)/shard_map/ppermute | solution.py:263
  31.2 3.5 %copy-start.3 = (f32[8,128,128]{2,1,0:T(8,128)}, f32[8,128,128]{2,1,0:T(8,128)S(1)}, u32[]{:S(2)}) copy-start(f32[8,128,128]{2,1,0:T(8,128)S(1)} %collective-permute-done.u_ref) | copy-start | bytes 1572868
  34.7 1.0 copy-start.15
  35.7 32.6 %all-to-all-start = ((f32[16,2,8,8,128]{4,3,2,1,0:T(8,128)}), f32[16,2,8,8,128]{4,3,2,1,0:T(8,128)}, u32[]{:S(2)}, u32[]{:S(2)}) async-start(f32[16,2,8,8,128]{4,3,2,1,0:T(8,128)} %copy-done.15), calls=%async_computation | async-start | bytes 2097152 | tf_op jit(solution)/shard_map/all_to_all | solution.py:228
  46.5 16.4 %collective-permute-start.1 = (f32[8,128,128]{2,1,0:T(8,128)}, f32[8,128,128]{2,1,0:T(8,128)S(1)}, u32[]{:S(2)}, u32[]{:S(2)}) collective-permute-start(f32[8,128,128]{2,1,0:T(8,128)} %get-tuple-element.19), channel_id=1, source_target_pairs={{32,96},{48,112},{64,0},{80,16},{160,224},{176,240},{192,128},{208... | collective-permute-start | bytes 1572872 | tf_op jit(solution)/shard_map/ppermute | solution.py:263
  63.0 5.3 %copy-start.11 = (bf16[2,256,256]{2,1,0:T(8,128)(2,1)S(1)}, bf16[2,256,256]{2,1,0:T(8,128)(2,1)}, u32[]{:S(2)}) copy-start(bf16[2,256,256]{2,1,0:T(8,128)(2,1)} %constant.112.left_ref) | copy-start | bytes 786436
  66.5 0.8 copy-start.5
  67.3 1.0 copy-start.21
  68.3 1.0 copy-start.12
  69.2 2.6 copy-start.22
  73.4 40.8 %all-to-all-start.1 = ((f32[16,4,8,8,128]{4,3,2,1,0:T(8,128)}), f32[16,4,8,8,128]{4,3,2,1,0:T(8,128)}, u32[]{:S(2)}, u32[]{:S(2)}) async-start(f32[16,4,8,8,128]{4,3,2,1,0:T(8,128)} %pad_maximum_fusion), calls=%async_computation.1 | async-start | bytes 4194304 | tf_op jit(solution)/shard_map/all_to_all | solution.py:228
  81.3 27.7 %collective-permute-start.2 = (f32[8,128,128]{2,1,0:T(8,128)}, f32[8,128,128]{2,1,0:T(8,128)S(1)}, u32[]{:S(2)}, u32[]{:S(2)}) collective-permute-start(f32[8,128,128]{2,1,0:T(8,128)} %get-tuple-element.20), channel_id=1, source_target_pairs={{0,64},{16,80},{32,96},{48,112},{64,0},{80,16},{96,32},{112,48},{1... | collective-permute-start | bytes 1572872 | tf_op jit(solution)/shard_map/ppermute | solution.py:263
  112.5 0.8 copy-start.7
  113.3 1.0 copy-start.17
  114.3 2.8 copy-start.13
  117.1 1.3 copy-start.18
  120.0 36.3 %all-to-all-start.2 = ((f32[16,4,8,8,128]{4,3,2,1,0:T(8,128)}), f32[16,4,8,8,128]{4,3,2,1,0:T(8,128)}, u32[]{:S(2)}, u32[]{:S(2)}) async-start(f32[16,4,8,8,128]{4,3,2,1,0:T(8,128)} %pad_maximum_fusion.1), calls=%async_computation.2 | async-start | bytes 4194304 | tf_op jit(solution)/shard_map/all_to_all | solution.py:228
  127.7 16.5 %collective-permute-start.3 = (f32[8,128,128]{2,1,0:T(8,128)}, f32[8,128,128]{2,1,0:T(8,128)S(1)}, u32[]{:S(2)}, u32[]{:S(2)}) collective-permute-start(f32[8,128,128]{2,1,0:T(8,128)} %get-tuple-element.21), channel_id=1, source_target_pairs={{32,96},{48,112},{64,0},{80,16},{160,224},{176,240},{192,128},{208... | collective-permute-start | bytes 1572872 | tf_op jit(solution)/shard_map/ppermute | solution.py:263
  147.7 0.8 copy-start.9
  148.5 1.0 copy-start.19
  156.2 2.8 copy-start.14
  159.1 1.3 copy-start.20
  196.6 1.0 copy-start.16
  197.6 7.1 %copy-start.4 = (f32[8,128,128]{2,1,0:T(8,128)S(1)}, f32[8,128,128]{2,1,0:T(8,128)}, u32[]{:S(2)}) copy-start(f32[8,128,128]{2,1,0:T(8,128)} %copy-done.3) | copy-start | bytes 1572868
  197.6 33.1 %all-to-all-start.4 = ((f32[16,2,8,8,128]{4,3,2,1,0:T(8,128)}), f32[16,2,8,8,128]{4,3,2,1,0:T(8,128)}, u32[]{:S(2)}, u32[]{:S(2)}) async-start(f32[16,2,8,8,128]{4,3,2,1,0:T(8,128)} %bitcast.25), calls=%async_computation.4 | async-start | bytes 2097152 | tf_op jit(solution)/shard_map/all_to_all | solution.py:228
  203.1 1.6 copy-start.23
  204.7 7.6 %copy-start.6 = (f32[8,128,128]{2,1,0:T(8,128)S(1)}, f32[8,128,128]{2,1,0:T(8,128)}, u32[]{:S(2)}) copy-start(f32[8,128,128]{2,1,0:T(8,128)} %copy-done.5) | copy-start | bytes 1572868
  204.7 7.6 %copy-start.25 = (f32[16,2,8,8,128]{4,3,2,1,0:T(8,128)S(1)}, f32[16,2,8,8,128]{4,3,2,1,0:T(8,128)}, u32[]{:S(2)}) copy-start(f32[16,2,8,8,128]{4,3,2,1,0:T(8,128)} %get-tuple-element.35.in_ref) | copy-start | bytes 3145732
  210.3 28.1 %collective-permute-start.7 = (f32[8,128,128]{2,1,0:T(8,128)}, f32[8,128,128]{2,1,0:T(8,128)}, u32[]{:S(2)}, u32[]{:S(2)}) collective-permute-start(f32[8,128,128]{2,1,0:T(8,128)} %get-tuple-element.25.before_ref), channel_id=1, source_target_pairs={{0,64},{16,80},{96,32},{112,48},{128,192},{144,208},{224,160},{240... | collective-permute-start | bytes 1572872 | tf_op jit(solution)/shard_map/ppermute | solution.py:294
  212.3 7.6 %copy-start.8 = (f32[8,128,128]{2,1,0:T(8,128)S(1)}, f32[8,128,128]{2,1,0:T(8,128)}, u32[]{:S(2)}) copy-start(f32[8,128,128]{2,1,0:T(8,128)} %copy-done.7) | copy-start | bytes 1572868
  212.4 7.6 %copy-start.24 = (f32[16,2,8,8,128]{4,3,2,1,0:T(8,128)S(1)}, f32[16,2,8,8,128]{4,3,2,1,0:T(8,128)}, u32[]{:S(2)}) copy-start(f32[16,2,8,8,128]{4,3,2,1,0:T(8,128)} %get-tuple-element.37.in_ref) | copy-start | bytes 3145732
  218.0 52.5 %collective-permute-start.6 = (f32[8,128,128]{2,1,0:T(8,128)}, f32[8,128,128]{2,1,0:T(8,128)}, u32[]{:S(2)}, u32[]{:S(2)}) collective-permute-start(f32[8,128,128]{2,1,0:T(8,128)} %get-tuple-element.27.before_ref), channel_id=1, source_target_pairs={{0,64},{16,80},{32,96},{48,112},{64,0},{80,16},{96,32},{112,48},{1... | collective-permute-start | bytes 1572872 | tf_op jit(solution)/shard_map/ppermute | solution.py:294
  219.9 10.7 %copy-start.10 = (f32[8,128,128]{2,1,0:T(8,128)S(1)}, f32[8,128,128]{2,1,0:T(8,128)}, u32[]{:S(2)}) copy-start(f32[8,128,128]{2,1,0:T(8,128)} %copy-done.9) | copy-start | bytes 1572868
  225.6 48.2 %collective-permute-start.5 = (f32[8,128,128]{2,1,0:T(8,128)}, f32[8,128,128]{2,1,0:T(8,128)}, u32[]{:S(2)}, u32[]{:S(2)}) collective-permute-start(f32[8,128,128]{2,1,0:T(8,128)} %get-tuple-element.29.before_ref), channel_id=1, source_target_pairs={{0,64},{16,80},{96,32},{112,48},{128,192},{144,208},{224,160},{240... | collective-permute-start | bytes 1572872 | tf_op jit(solution)/shard_map/ppermute | solution.py:294
  236.4 45.2 %collective-permute-start.4 = (f32[8,128,128]{2,1,0:T(8,128)}, f32[8,128,128]{2,1,0:T(8,128)S(1)}, u32[]{:S(2)}, u32[]{:S(2)}) collective-permute-start(f32[8,128,128]{2,1,0:T(8,128)} %get-tuple-element.31), channel_id=1, source_target_pairs={{0,64},{16,80},{32,96},{48,112},{64,0},{80,16},{96,32},{112,48},{1... | collective-permute-start | bytes 1572872 | tf_op jit(solution)/shard_map/ppermute | solution.py:294
where the time goes:
time: 286 us; the launch traced here: 285 us
  waiting for transfers between devices  115 us (40%)
  Pallas kernels  56.2 us (20%)
  starting transfers between devices  51.5 us (18%)
  blocking collectives  33.5 us (12%)
  local copies, waits for them, and re-layouts  21.1 us (7%)
  other arithmetic  6.73 us (2%)
    ppermute x4, waiting for transfers between devices, shards(): lax.ppermute(sent, 'band', every if k % 2 == 0 else to_first)  75.4 us
    all_to_all x1, blocking collectives, exchange(): lax.all_to_all(field, 'grid', split_axis=0, concat_axis=0, tiled=True)  33.5 us
    ppermute x4, waiting for transfers between devices, shards(): lax.ppermute(before, 'band', every if k % 2 == 1 else to_second)  33.3 us
    all_to_all x4, starting transfers between devices, exchange(): lax.all_to_all(field, 'grid', split_axis=0, concat_axis=0, tiled=True)  29.9 us
    pallas_call x4, Pallas kernels, inverse(): pl.pallas_call(inverse_kernel, grid_spec=pltpu.PrefetchScalarGridSpec(num...  22.5 us
    pallas_call x4, Pallas kernels, forward(): pl.pallas_call(forward_kernel, grid_spec=pltpu.PrefetchScalarGridSpec(num...  14.1 us
    pallas_call x4, Pallas kernels, add_into(): pl.pallas_call(add_kernel, grid_spec=pltpu.PrefetchScalarGridSpec(num_sca...  13.1 us
    ppermute x4, starting transfers between devices, shards(): lax.ppermute(before, 'band', every if k % 2 == 1 else to_second)  11 us
  transfers between devices with their start and end apart: 12, of which 7 were waited for; matrix products, arithmetic and copies ran while one was open for 2% of the time, Pallas kernels for 15%

commit v1 on v0

v1 whole, which is shorter than its diff:
```python
import math

import jax
import jax.numpy as jnp
import numpy as np
from jax import lax
from jax.experimental import pallas as pl
from jax.experimental.pallas import tpu as pltpu
from jax.sharding import PartitionSpec as P

PARTNER_BIT = 2
ORBITALS = 4
LANES = 128
VMEM_BYTES = 40 * 2**20
EARLY = pl.CostEstimate(flops=0, bytes_accessed=200 * 10**6, transcendentals=0)
ROUNDS = 3
ENTRY = 8


def cover(rows, columns, rounds):
    cells = [
        (i, j) for i in range(ORBITALS) for j in range(ORBITALS) if (i < rows) == (j < columns)
    ]

    def search(left, first, second):
        if not left:
            return first, second
        i, j = left[0]
        below = [r for r, c in left if c == j and r != i]
        beside = [c for r, c in left if r == i and c != j]
        options = [(0, r) for r in below] + [(1, c) for c in beside] + [(0, None), (1, None)]
        for side, other in options:
            if len((first, second)[side]) == rounds:
                continue
            taken = {(i, j)}
            if other is not None:
                taken.add((other, j) if side == 0 else (i, other))
            own, far = (i, j) if side == 0 else (j, i)
            entry = (far, own, (own + 1) % ORBITALS if other is None else other, int(other is not None))
            rest = [c for c in left if c not in taken]
            found = search(
                rest,
                first + [entry] if side == 0 else first,
                second + [entry] if side == 1 else second,
            )
            if found is not None:
                return found
        return None

    return search(cells, [], [])


def plan_table():
    patterns = 2**ORBITALS
    bits = [[(p >> i) & 1 for i in range(ORBITALS)] for p in range(patterns)]
    order = [sorted(range(ORBITALS), key=lambda i: b[i]) for b in bits]
    zeros = [b.count(0) for b in bits]
    found = {}
    for rows in range(ORBITALS + 1):
        for columns in range(ORBITALS + 1):
            found[rows, columns] = cover(rows, columns, ROUNDS) or cover(rows, columns, ROUNDS + 1)
    table = np.zeros((2, patterns, patterns, ROUNDS + 1, ENTRY), np.int32)
    table[..., 1] = 1
    for side in range(2):
        for own in range(patterns):
            for other in range(patterns):
                first, second = (own, other) if side == 0 else (other, own)
                both = found[zeros[first], zeros[second]]
                for number, (_, a, b, mask) in enumerate(both[side]):
                    table[side, own, other, number, :4] = (order[own][a], order[own][b], 1, mask)
                for number, (u, *_) in enumerate(both[1 - side]):
                    table[side, own, other, number, 4] = order[own][u]
    rows = np.zeros((2 * patterns * patterns, 1, LANES), np.int32)
    rows[:, 0, :(ROUNDS + 1) * ENTRY] = table.reshape(2 * patterns * patterns, -1)
    return rows


def plan_kernel(spin, table_ref, orbitals_ref, plan_ref, sent_ref, row_ref, sems):
    band = lax.axis_index("band")
    partner = band ^ (1 << PARTNER_BIT)
    row = (band >> PARTNER_BIT) & 1
    for group in (band, partner):
        own = jnp.int32(0)
        for i in range(ORBITALS):
            own = own + spin[group * ORBITALS + i] * (1 << i)
        row = row * 2**ORBITALS + own
    copy = pltpu.make_async_copy(table_ref.at[row], row_ref, sems.at[0])
    copy.start()
    copy.wait()
    copy = pltpu.make_async_copy(orbitals_ref.at[row_ref[0, 4]], sent_ref, sems.at[1])
    copy.start()
    for i in range((ROUNDS + 1) * ENTRY):
        plan_ref[i] = row_ref[0, i]
    copy.wait()


def make_plan(spin_channel, orbitals):
    smem = pl.BlockSpec(memory_space=pltpu.SMEM)
    hbm = pl.BlockSpec(memory_space=pl.ANY)
    return pl.pallas_call(
        plan_kernel,
        in_specs=[smem, hbm, hbm],
        out_specs=[smem, pl.BlockSpec(memory_space=pltpu.VMEM)],
        out_shape=[
            jax.ShapeDtypeStruct(((ROUNDS + 1) * ENTRY,), jnp.int32),
            jax.ShapeDtypeStruct(orbitals.shape[1:], jnp.float32),
        ],
        scratch_shapes=[pltpu.SMEM((1, LANES), jnp.int32), pltpu.SemaphoreType.DMA((2,))],
        name="plan_rounds",
    )(spin_channel, jnp.asarray(plan_table()), orbitals)


def needs_more(spin_channel):
    flip = 1 << PARTNER_BIT
    ones = jnp.sum(spin_channel.reshape(-1, 2, flip, ORBITALS), axis=(1, 3))
    return jnp.any((ones == 0) | (ones == 2 * ORBITALS))


def fourier_tables(length, planes):
    number = np.arange(length)
    angles = (number[:, None] * number[None, :] % length) * (2.0 * math.pi / length)
    cosine, sine = np.cos(angles), np.sin(angles)
    plus = np.block([[cosine, -sine], [sine, cosine]])
    minus = plus.T
    blocks = length // planes
    order = np.arange(2 * length).reshape(2, blocks, planes).transpose(1, 0, 2).reshape(-1)
    return plus, plus[:, order], minus, minus[order, :]


def two_parts(table):
    exact = table.astype(np.float32)
    high = exact.astype(jnp.bfloat16)
    low = (exact - high.astype(np.float32)).astype(jnp.bfloat16)
    return jnp.asarray(np.stack([high, low]))


def split(value):
    high = value.astype(jnp.bfloat16)
    return high, (value - high.astype(jnp.float32)).astype(jnp.bfloat16)


def dot(a, b):
    return jnp.dot(a, b, preferred_element_type=jnp.float32)


def from_left(table_ref, value):
    high, low = split(value)
    return dot(table_ref[0], high) + dot(table_ref[0], low) + dot(table_ref[1], high)


def from_right(value, table_ref):
    high, low = split(value)
    return dot(high, table_ref[0]) + dot(low, table_ref[0]) + dot(high, table_ref[1])


def forward_kernel(number, plan, u_ref, v_ref, w_ref, right_ref, left_ref, out_ref):
    planes, size = u_ref.shape[:2]
    blocks = out_ref.shape[0]
    s0 = plan[number * ENTRY + 2].astype(jnp.float32)
    s1 = plan[number * ENTRY + 3].astype(jnp.float32)
    for first in range(0, planes, 2):
        rows = []
        for x in range(first, first + 2):
            u = u_ref[x]
            rows.append(jnp.concatenate([u * v_ref[0, x] * s0, u * w_ref[0, x] * s1], axis=1))
        along_z = from_right(jnp.concatenate(rows, axis=0), right_ref)
        columns = []
        for k in range(2):
            part = along_z[k * size:(k + 1) * size]
            columns.append(jnp.concatenate([part[:, :LANES], part[:, LANES:]], axis=0))
        along_y = from_left(left_ref, jnp.concatenate(columns, axis=1))
        for k in range(2):
            for c in range(2):
                block = along_y[c * size:(c + 1) * size, k * LANES:(k + 1) * LANES]
                out_ref[:, c, first + k] = block.reshape(blocks, size // blocks, LANES)


def solve_kernel(in_ref, kernel_ref, left_ref, right_ref, *rest):
    out_ref = rest[-1]
    columns = kernel_ref.shape[0]
    rows = math.prod(in_ref.shape[:3])
    flat_in = in_ref.reshape(rows * columns, LANES)
    flat_out = out_ref.reshape(rows * columns, LANES)
    for y in range(0, columns, 2):
        value = jnp.concatenate([flat_in[pl.ds(y + k, rows, stride=columns), :] for k in range(2)], axis=1)
        weight = jnp.concatenate([kernel_ref[y], kernel_ref[y + 1]], axis=1)
        spectrum = from_left(left_ref, value) * jnp.concatenate([weight, weight], axis=0)
        solved = from_left(right_ref, spectrum)
        for k in range(2):
            flat_out[pl.ds(y + k, rows, stride=columns), :] = solved[:, k * LANES:(k + 1) * LANES]


def inverse_kernel(number, plan, in_ref, u_ref, v_ref, w_ref, left_ref, right_ref, own_ref, back_ref):
    planes, size = u_ref.shape[:2]
    s0 = plan[number * ENTRY + 2].astype(jnp.float32)
    s1 = plan[number * ENTRY + 3].astype(jnp.float32)
    for first in range(0, planes, 2):
        columns = []
        for x in range(first, first + 2):
            columns.append(jnp.concatenate([in_ref[:, c, x].reshape(size, LANES) for c in range(2)], axis=0))
        along_y = from_left(left_ref, jnp.concatenate(columns, axis=1))
        rows = []
        for k in range(2):
            part = along_y[:, k * LANES:(k + 1) * LANES]
            rows.append(jnp.concatenate([part[:size], part[size:]], axis=1))
        potential = from_right(jnp.concatenate(rows, axis=0), right_ref)
        for k in range(2):
            x = first + k
            v0 = potential[k * size:(k + 1) * size, :LANES] * s0
            v1 = potential[k * size:(k + 1) * size, LANES:] * s1
            u = u_ref[x]
            own_ref[0, x] = -(v0 * u)
            own_ref[1, x] = -(v1 * u)
            back_ref[x] = -(v0 * v_ref[0, x] + v1 * w_ref[0, x])


def add_kernel(plan, more_ref, sum_ref, total_ref):
    total_ref[...] = sum_ref[...] + more_ref[...]


def in_hbm(value):
    return pltpu.with_memory_space_constraint(value, pltpu.HBM)


def params():
    return pltpu.CompilerParams(dimension_semantics=("arbitrary",), vmem_limit_bytes=VMEM_BYTES)


def whole(shape):
    return pl.BlockSpec(shape, lambda *_: (0,) * len(shape))


def part(shape, place):
    return pl.BlockSpec((shape[0], 2) + shape[2:], lambda *_: (0, place, 0, 0, 0))


def orbital_block(shape, number, field):
    return pl.BlockSpec((1,) + shape[1:], lambda i, plan: (plan[number * ENTRY + field], 0, 0, 0))


def forward(number, width, plan, u, orbitals, right, left):
    planes, size, lanes = u.shape
    blocks = lax.axis_size("grid")
    shape = (blocks, 2 * width, planes, size // blocks, lanes)
    return pl.pallas_call(
        lambda *refs: forward_kernel(number, *refs),
        grid_spec=pltpu.PrefetchScalarGridSpec(
            num_scalar_prefetch=1,
            grid=(1,),
            in_specs=[
                whole(u.shape),
                orbital_block(orbitals.shape, number, 0),
                orbital_block(orbitals.shape, number, 1),
                whole(right.shape),
                whole(left.shape),
            ],
            out_specs=part(shape, 0),
        ),
        out_shape=pltpu.HBM(shape, jnp.float32),
        cost_estimate=EARLY if number else None,
        compiler_params=params(),
        name="forward_planes",
    )(plan, u, orbitals, orbitals, right, left)


def solve(arrived, kernel, left, right, ahead, after):
    hbm = pl.BlockSpec(memory_space=pl.ANY)
    operands = [in_hbm(arrived), kernel, left, right]
    specs = [part(arrived.shape, 0), whole(kernel.shape), whole(left.shape), whole(right.shape)]
    if ahead is None:
        shape, place, aliases = (arrived.shape[0], 2) + arrived.shape[2:], 0, {}
    else:
        shape, place, aliases = ahead.shape, 1, {len(operands): 0}
        operands.append(in_hbm(ahead))
        specs.append(hbm)
    return pl.pallas_call(
        solve_kernel,
        grid=(1,),
        in_specs=specs + [hbm] * len(after),
        out_specs=part(shape, place),
        out_shape=pltpu.HBM(shape, jnp.float32),
        input_output_aliases=aliases,
        compiler_params=params(),
        name="solve_columns",
    )(*operands, *after)


def inverse(number, place, plan, arrived, u, orbitals, left, right):
    own = (2,) + u.shape
    return pl.pallas_call(
        lambda *refs: inverse_kernel(number, *refs),
        grid_spec=pltpu.PrefetchScalarGridSpec(
            num_scalar_prefetch=1,
            grid=(1,),
            in_specs=[
                part(arrived.shape, place),
                whole(u.shape),
                orbital_block(orbitals.shape, number, 0),
                orbital_block(orbitals.shape, number, 1),
                whole(left.shape),
                whole(right.shape),
            ],
            out_specs=[whole(own), whole(u.shape)],
        ),
        out_shape=[jax.ShapeDtypeStruct(own, jnp.float32), pltpu.HBM(u.shape, jnp.float32)],
        compiler_params=params(),
        name="inverse_planes",
    )(plan, in_hbm(arrived), u, orbitals, orbitals, left, right)


def add_into(number, field, plan, total, more):
    count = more.shape[0]
    one = (1,) + more.shape[1:]
    target = pl.BlockSpec(one, lambda i, plan: (plan[number * ENTRY + field + i], 0, 0, 0))
    return pl.pallas_call(
        add_kernel,
        grid_spec=pltpu.PrefetchScalarGridSpec(
            num_scalar_prefetch=1,
            grid=(count,),
            in_specs=[pl.BlockSpec(one, lambda i, plan: (i, 0, 0, 0)), target],
            out_specs=target,
        ),
        out_shape=jax.ShapeDtypeStruct(total.shape, jnp.float32),
        input_output_aliases={2: 0},
        compiler_params=params(),
        name="add_terms",
    )(plan, more, total)


def signed(number, length):
    return jnp.where(number < length // 2, number, number - length)


def coulomb_block(size, column_count, first_column):
    strength = math.sqrt(size**3) / 4.0
    along_x = signed(jnp.arange(size, dtype=jnp.int32), size)
    along_y = signed(first_column + jnp.arange(column_count, dtype=jnp.int32), size)
    squared = along_y[:, None, None] ** 2 + along_x[None, :, None] ** 2 + along_x[None, None, :] ** 2
    bounded = jnp.maximum(squared, 1).astype(jnp.float32)
    kernel = jnp.where(squared == 0, jnp.float32(0.0), jnp.float32(strength) / bounded)
    return kernel * jnp.float32(1.0 / size**3)


def exchange(field):
    return lax.all_to_all(field, "grid", split_axis=0, concat_axis=0, tiled=True)


def to_partner(value):
    pairs = [(g, g ^ (1 << PARTNER_BIT)) for g in range(lax.axis_size("band"))]
    return lax.ppermute(value, "band", pairs)


def sent_orbital(number, plan, orbitals):
    return lax.dynamic_index_in_dim(orbitals, plan[number * ENTRY + 4], 0, keepdims=False)


def one_round(number, plan, orbitals, kernel, total, tables):
    plus, plus_x, minus, minus_x = tables
    u = to_partner(sent_orbital(number, plan, orbitals))
    arrived = exchange(forward(number, 1, plan, u, orbitals, minus, plus))
    arrived = exchange(solve(arrived, kernel, plus_x, minus_x, None, ()))
    own, back = inverse(number, 0, plan, arrived, u, orbitals, minus, plus)
    total = add_into(number, 0, plan, total, own)
    return add_into(number, 4, plan, total, to_partner(back)[None])


def shards(orbitals, spin_channel):
    count, planes, size, lanes = orbitals.shape
    column_count = size // lax.axis_size("grid")
    plan, sent = make_plan(spin_channel, orbitals)
    us = [to_partner(sent)]
    kernel = coulomb_block(size, column_count, lax.axis_index("grid") * column_count)
    tables = tuple(two_parts(t) for t in fourier_tables(size, planes))
    plus, plus_x, minus, minus_x = tables
    total = lax.cond(
        needs_more(spin_channel),
        lambda *args: one_round(ROUNDS, *args, jnp.zeros_like(orbitals), tables),
        lambda *args: jnp.zeros_like(orbitals),
        plan, orbitals, kernel,
    )
    for number in range(1, ROUNDS):
        sent, us[-1] = lax.optimization_barrier((sent_orbital(number, plan, orbitals), us[-1]))
        us.append(to_partner(sent))

    def planes_of(number):
        return forward(number, 1 if number == 0 else 2, plan, us[number], orbitals, minus, plus)

    returned = []
    arrived = exchange(planes_of(0))
    for number in range(ROUNDS):
        ahead = planes_of(number + 1) if number + 1 < ROUNDS else None
        after = returned[:max(number - 1, 0)]
        arrived = exchange(solve(arrived, kernel, plus_x, minus_x, ahead, after))
        own, back = inverse(number, 0 if ahead is None else 1, plan, arrived, us[number], orbitals, minus, plus)
        returned.append(to_partner(back))
        total = add_into(number, 0, plan, total, own)
        if number > 0:
            total = add_into(number - 1, 4, plan, total, returned[number - 1][None])
    place = plan[(ROUNDS - 1) * ENTRY + 4]
    last = lax.dynamic_index_in_dim(total, place, 0, keepdims=False) + returned[-1]
    return lax.dynamic_update_index_in_dim(total, last, place, 0)


def solution(mesh):
    return jax.shard_map(
        shards,
        mesh=mesh,
        in_specs=(P("band", "grid", None, None), P()),
        out_specs=P("band", "grid", None, None),
        check_vma=False,
    )
```

time: 286 us -> 229 us (0.80)
  blocking collectives: 33.5 us -> 0 us
  local copies, waits for them, and re-layouts: 21.1 us -> 6.43 us
  Pallas kernels: 56.2 us -> 50.2 us
  starting transfers between devices: 51.5 us -> 46.9 us
  between operations: 0.41 us -> 4.3 us
  other arithmetic: 6.73 us -> 3.01 us
    all_to_all x1 -> x0, blocking collectives: 33.5 us -> none  [exchange(): lax.all_to_all(field, 'grid', split_axis=0, concat_axis=0, tiled=True)]
    unnamed x54 -> x24, local copies, waits for them, and re-layouts: 8.24 us -> 1.99 us
    slice x3 -> x1, local copies, waits for them, and re-layouts: 6.85 us -> 0.62 us  [sent_orbital(): plan[number * ENTRY + 4]]
    ppermute x8 -> x6, starting transfers between devices: 21.5 us -> 15.6 us  [to_partner(): return lax.ppermute(value, 'band', pairs)]
    pallas_call x12 -> x10, Pallas kernels: 43.1 us -> 37.5 us  [the longest x3 12.4 us: inverse(): pl.pallas_call(lambda *refs: inverse_kernel(number, *refs), grid_spec=plt...]
    concatenate x7 -> x0, other arithmetic: 3.69 us -> none  [the longest x3 3.38 us: shards(): both = exchange(jnp.concatenate([planes_of(k + 1), solved], axis=1))]
    all_to_all x4, waiting for transfers between devices: 6.73 us -> 10.1 us  [exchange(): lax.all_to_all(field, 'grid', split_axis=0, concat_axis=0, tiled=True)]
    ppermute x8 -> x6, waiting for transfers between devices: 109 us -> 106 us  [to_partner(): return lax.ppermute(value, 'band', pairs)]
  transfers between devices with their start and end apart: 12 -> 10, of which waited for: 7 -> 7; matrix products, arithmetic and copies ran while one was open for 2% -> 2% of each run, Pallas kernels for 15% -> 15%
where the time goes in v1:
time: 229 us; the launch traced here: 227 us
  waiting for transfers between devices  117 us (51%)
  Pallas kernels  50.2 us (22%)
  starting transfers between devices  46.9 us (20%)
  local copies, waits for them, and re-layouts  6.43 us (3%)
  between operations  4.3 us (2%)
  other arithmetic  3.01 us (1%)
    ppermute x6, waiting for transfers between devices, to_partner(): return lax.ppermute(value, 'band', pairs)  106 us
    all_to_all x4, starting transfers between devices, exchange(): lax.all_to_all(field, 'grid', split_axis=0, concat_axis=0, tiled=True)  31.4 us
    ppermute x6, starting transfers between devices, to_partner(): return lax.ppermute(value, 'band', pairs)  15.6 us
    pallas_call x5, Pallas kernels, add_into(): pl.pallas_call(add_kernel, grid_spec=pltpu.PrefetchScalarGridSpec(num_sca...  12.7 us
    pallas_call x3, Pallas kernels, inverse(): pl.pallas_call(lambda *refs: inverse_kernel(number, *refs), grid_spec=plt...  12.4 us
    pallas_call x3, Pallas kernels, forward(): pl.pallas_call(lambda *refs: forward_kernel(number, *refs), grid_spec=plt...  10.9 us
    pallas_call x3, Pallas kernels, solve(): pl.pallas_call(solve_kernel, grid=(1,), in_specs=specs + [hbm] * len(afte...  10.7 us
    all_to_all x4, waiting for transfers between devices, exchange(): lax.all_to_all(field, 'grid', split_axis=0, concat_axis=0, tiled=True)  10.1 us
  transfers between devices with their start and end apart: 10, of which 7 were waited for; matrix products, arithmetic and copies ran while one was open for 2% of the time, Pallas kernels for 15%

profile of v1, /device:TPU:1, one launch (start us, length us, event | category | flops | bytes accessed | tf_op | source)
XLA Modules:
  0.0 227.5 jit_solution(11406742198186344540)
XLA Ops:
  0.0 0.0 copy-start.6
  0.0 0.0 copy-start.4
  0.0 0.0 copy-start.7
  0.0 3.5 %plan_rounds.1 = (s32[32]{0:T(128)S(1)}, f32[8,128,128]{2,1,0:T(8,128)}) custom-call(s32[128]{0:T(128)} %spin.1, s32[512,1,128]{2,1,0:T(1,128)} %constant.60.clone.table_ref, f32[4,8,128,128]{3,2,1,0:T(8,128)} %refs_4_.8), custom_call_target="tpu_custom_call" | custom-call | tf_op jit(solution)/shard_map/plan_rounds/pallas_call | solution.py:100
  3.5 5.7 %collective-permute-start.2 = (f32[8,128,128]{2,1,0:T(8,128)}, f32[8,128,128]{2,1,0:T(8,128)S(1)}, u32[]{:S(2)}, u32[]{:S(2)}) collective-permute-start(f32[8,128,128]{2,1,0:T(8,128)} %get-tuple-element.44), channel_id=1, source_target_pairs={{0,64},{16,80},{32,96},{48,112},{64,0},{80,16},{96,32},{112,48},{1... | collective-permute-start | bytes 1572872 | tf_op jit(solution)/shard_map/ppermute | solution.py:350
  9.2 0.6 fusion.6
  13.3 0.0 copy-done.4
  13.4 1.1 dynamic-slice_bitcast_fusion.1
  14.4 17.2 %collective-permute-done.2.refs_1_.refs_2_ = f32[8,128,128]{2,1,0:T(8,128)S(1)} collective-permute-done((f32[8,128,128]{2,1,0:T(8,128)}, f32[8,128,128]{2,1,0:T(8,128)S(1)}, u32[]{:S(2)}, u32[]{:S(2)}) %collective-permute-start.2) | collective-permute-done | bytes 524320 | tf_op jit(solution)/shard_map/ppermute | solution.py:350
  31.6 0.0 copy-done.6
  31.6 0.0 copy-done.7
  31.6 2.8 %forward_planes.5 = f32[16,2,8,8,128]{4,3,2,1,0:T(8,128)} custom-call(s32[32]{0:T(128)S(1)} %get-tuple-element.43.refs_0_.plan, f32[8,128,128]{2,1,0:T(8,128)S(1)} %collective-permute-done.2.refs_1_.refs_2_, f32[4,8,128,128]{3,2,1,0:T(8,128)S(1)} %copy-done.4, f32[4,8,128,128]{3,2,1,0:T(8,128)S(1)} %copy-done.4, bf16[2,256,256]{2,1,0:T(8,128)(2,1)S(1)} %copy-done.6, ...), custom_call_target="tpu_custom_call" | custom-call | tf_op jit(solution)/shard_map/forward_planes/pallas_call | solution.py:245
  34.4 0.0 copy-start.13
  34.4 9.0 %all-to-all-start.2 = ((f32[16,2,8,8,128]{4,3,2,1,0:T(8,128)}), f32[16,2,8,8,128]{4,3,2,1,0:T(8,128)}, u32[]{:S(2)}, u32[]{:S(2)}) async-start(f32[16,2,8,8,128]{4,3,2,1,0:T(8,128)} %forward_planes.5), calls=%async_computation.2 | async-start | bytes 2097152 | tf_op jit(solution)/shard_map/all_to_all | solution.py:345
  43.4 0.0 copy-done.13
  43.4 1.9 collective-permute-start.3
  45.4 0.1 broadcast_add_fusion
  45.5 0.2 fusion.3.kernel_ref
  45.7 0.0 copy-start.8
  45.7 25.1 %collective-permute-done.3.refs_1_.refs_2_ = f32[8,128,128]{2,1,0:T(8,128)S(1)} collective-permute-done((f32[8,128,128]{2,1,0:T(8,128)S(1)}, f32[8,128,128]{2,1,0:T(8,128)S(1)}, u32[]{:S(2)}, u32[]{:S(2)}) %collective-permute-start.3) | collective-permute-done | bytes 524320 | tf_op jit(solution)/shard_map/ppermute | solution.py:350
  70.8 0.0 copy-start.10
  70.9 4.0 %forward_planes.6.rest_0_ = f32[16,4,8,8,128]{4,3,2,1,0:T(8,128)} custom-call(s32[32]{0:T(128)S(1)} %get-tuple-element.43.refs_0_.plan, f32[8,128,128]{2,1,0:T(8,128)S(1)} %collective-permute-done.3.refs_1_.refs_2_, f32[4,8,128,128]{3,2,1,0:T(8,128)} %refs_4_.8, f32[4,8,128,128]{3,2,1,0:T(8,128)} %refs_4_.8, bf16[2,256,256]{2,1,0:T(8,128)(2,1)S(1)} %copy-done.6, ...), custom_call_target="tpu_custom_call" | custom-call | bytes 200000000 | tf_op jit(solution)/shard_map/forward_planes/pallas_call | solution.py:245
  74.9 0.0 all-to-all-done.2.in_ref
  74.9 0.0 copy-done.10
  74.9 0.0 copy-done.11
  74.9 3.5 %solve_columns.5 = f32[16,4,8,8,128]{4,3,2,1,0:T(8,128)} custom-call(f32[16,2,8,8,128]{4,3,2,1,0:T(8,128)} %all-to-all-done.2.in_ref, f32[8,128,128]{2,1,0:T(8,128)S(1)} %fusion.3.kernel_ref, bf16[2,256,256]{2,1,0:T(8,128)(2,1)S(1)} %copy-done.10, bf16[2,256,256]{2,1,0:T(8,128)(2,1)S(1)} %copy-done.11, ...), custom_call_target="tpu_custom_call", output_to_operand_aliasing={{}: (4, {})} | custom-call | tf_op jit(solution)/shard_map/solve_columns/pallas_call | solution.py:276
  78.4 7.8 %all-to-all-start.3 = ((f32[16,4,8,8,128]{4,3,2,1,0:T(8,128)}), f32[16,4,8,8,128]{4,3,2,1,0:T(8,128)}, u32[]{:S(2)}, u32[]{:S(2)}) async-start(f32[16,4,8,8,128]{4,3,2,1,0:T(8,128)} %solve_columns.5), calls=%async_computation.3 | async-start | bytes 4194304 | tf_op jit(solution)/shard_map/all_to_all | solution.py:345
  86.2 1.9 collective-permute-start.4
  88.1 24.9 %collective-permute-done.4.refs_1_.refs_2_ = f32[8,128,128]{2,1,0:T(8,128)S(1)} collective-permute-done((f32[8,128,128]{2,1,0:T(8,128)}, f32[8,128,128]{2,1,0:T(8,128)S(1)}, u32[]{:S(2)}, u32[]{:S(2)}) %collective-permute-start.4) | collective-permute-done | bytes 524320 | tf_op jit(solution)/shard_map/ppermute | solution.py:350
  113.0 4.1 %forward_planes.7.rest_0_ = f32[16,4,8,8,128]{4,3,2,1,0:T(8,128)} custom-call(s32[32]{0:T(128)S(1)} %get-tuple-element.43.refs_0_.plan, f32[8,128,128]{2,1,0:T(8,128)S(1)} %collective-permute-done.4.refs_1_.refs_2_, f32[4,8,128,128]{3,2,1,0:T(8,128)} %refs_4_.8, f32[4,8,128,128]{3,2,1,0:T(8,128)} %refs_4_.8, bf16[2,256,256]{2,1,0:T(8,128)(2,1)S(1)} %copy-done.6, ...), custom_call_target="tpu_custom_call" | custom-call | bytes 200000000 | tf_op jit(solution)/shard_map/forward_planes/pallas_call | solution.py:245
  117.1 0.0 all-to-all-done.3.in_ref.refs_1_
  117.1 0.0 copy-done.8
  117.1 3.6 %solve_columns.6 = f32[16,4,8,8,128]{4,3,2,1,0:T(8,128)} custom-call(f32[16,4,8,8,128]{4,3,2,1,0:T(8,128)} %all-to-all-done.3.in_ref.refs_1_, f32[8,128,128]{2,1,0:T(8,128)S(1)} %fusion.3.kernel_ref, bf16[2,256,256]{2,1,0:T(8,128)(2,1)S(1)} %copy-done.10, bf16[2,256,256]{2,1,0:T(8,128)(2,1)S(1)} %copy-done.11, ...), custom_call_target="tpu_custom_call", output_to_operand_aliasing={{}: (4, {})} | custom-call | tf_op jit(solution)/shard_map/solve_columns/pallas_call | solution.py:276
  120.6 7.2 %all-to-all-start.4 = ((f32[16,4,8,8,128]{4,3,2,1,0:T(8,128)}), f32[16,4,8,8,128]{4,3,2,1,0:T(8,128)}, u32[]{:S(2)}, u32[]{:S(2)}) async-start(f32[16,4,8,8,128]{4,3,2,1,0:T(8,128)} %solve_columns.6), calls=%async_computation.4 | async-start | bytes 4194304 | tf_op jit(solution)/shard_map/all_to_all | solution.py:345
  127.8 4.1 %inverse_planes.6 = (f32[2,8,128,128]{3,2,1,0:T(8,128)S(1)}, f32[8,128,128]{2,1,0:T(8,128)}) custom-call(s32[32]{0:T(128)S(1)} %get-tuple-element.43.refs_0_.plan, f32[16,4,8,8,128]{4,3,2,1,0:T(8,128)} %all-to-all-done.3.in_ref.refs_1_, f32[8,128,128]{2,1,0:T(8,128)S(1)} %collective-permute-done.2.refs_1_.refs_2_, f32[4,8,128,128]{3,2,1,0:T(8,128)} %refs_4_.8, ...), custom_call_target="tpu_custom_call" | custom-call | tf_op jit(solution)/shard_map/inverse_planes/pallas_call | solution.py:290
  132.0 1.9 collective-permute-start.6
  133.9 26.2 %collective-permute-done.6.rest_0_ = f32[8,128,128]{2,1,0:T(8,128)S(1)} collective-permute-done((f32[8,128,128]{2,1,0:T(8,128)}, f32[8,128,128]{2,1,0:T(8,128)S(1)}, u32[]{:S(2)}, u32[]{:S(2)}) %collective-permute-start.6) | collective-permute-done | bytes 524320 | tf_op jit(solution)/shard_map/ppermute | solution.py:350
  160.1 0.0 all-to-all-done.4.refs_1_.in_ref
  160.1 3.7 %solve_columns.7 = f32[16,2,8,8,128]{4,3,2,1,0:T(8,128)} custom-call(f32[16,4,8,8,128]{4,3,2,1,0:T(8,128)} %all-to-all-done.4.refs_1_.in_ref, f32[8,128,128]{2,1,0:T(8,128)} %copy-done.8, bf16[2,256,256]{2,1,0:T(8,128)(2,1)S(1)} %copy-done.10, bf16[2,256,256]{2,1,0:T(8,128)(2,1)} %constant.64.clone.right_ref, f32[8,128,128]{2,1,0:T(8,128)S(1)} %collective-permute-done.6.rest_0_), custom_call_target="tpu_custom_call" | custom-call | tf_op jit(solution)/shard_map/solve_columns/pallas_call | solution.py:276
  163.8 7.3 %all-to-all-start.5 = ((f32[16,2,8,8,128]{4,3,2,1,0:T(8,128)}), f32[16,2,8,8,128]{4,3,2,1,0:T(8,128)}, u32[]{:S(2)}, u32[]{:S(2)}) async-start(f32[16,2,8,8,128]{4,3,2,1,0:T(8,128)} %solve_columns.7), calls=%async_computation.5 | async-start | bytes 2097152 | tf_op jit(solution)/shard_map/all_to_all | solution.py:345
  171.1 4.2 %inverse_planes.5 = (f32[2,8,128,128]{3,2,1,0:T(8,128)S(1)}, f32[8,128,128]{2,1,0:T(8,128)}) custom-call(s32[32]{0:T(128)S(1)} %get-tuple-element.43.refs_0_.plan, f32[16,4,8,8,128]{4,3,2,1,0:T(8,128)} %all-to-all-done.4.refs_1_.in_ref, f32[8,128,128]{2,1,0:T(8,128)S(1)} %collective-permute-done.3.refs_1_.refs_2_, f32[4,8,128,128]{3,2,1,0:T(8,128)} %refs_4_.8, ...), custom_call_target="tpu_custom_call" | custom-call | tf_op jit(solution)/shard_map/inverse_planes/pallas_call | solution.py:290
  175.2 1.0 copy-done
  176.2 2.0 collective-permute-start.5
  178.3 10.1 %all-to-all-done.5.refs_1_ = f32[16,2,8,8,128]{4,3,2,1,0:T(8,128)} async-done(((f32[16,2,8,8,128]{4,3,2,1,0:T(8,128)}), f32[16,2,8,8,128]{4,3,2,1,0:T(8,128)}, u32[]{:S(2)}, u32[]{:S(2)}) %all-to-all-start.5) | async-done | bytes 1048608 | tf_op jit(solution)/shard_map/all_to_all | solution.py:345
  188.4 4.1 %inverse_planes.7 = (f32[2,8,128,128]{3,2,1,0:T(8,128)S(1)}, f32[8,128,128]{2,1,0:T(8,128)}) custom-call(s32[32]{0:T(128)S(1)} %get-tuple-element.43.refs_0_.plan, f32[16,2,8,8,128]{4,3,2,1,0:T(8,128)} %all-to-all-done.5.refs_1_, f32[8,128,128]{2,1,0:T(8,128)S(1)} %collective-permute-done.4.refs_1_.refs_2_, f32[4,8,128,128]{3,2,1,0:T(8,128)} %refs_4_.8, ...), custom_call_target="tpu_custom_call" | custom-call | tf_op jit(solution)/shard_map/inverse_planes/pallas_call | solution.py:290
  192.5 1.0 copy-done.2
  193.5 2.1 collective-permute-start.7
  195.6 0.0 copy-done.14
  195.6 0.1 reshape.64
  195.7 0.2 reduce_sum.9
  195.9 0.6 or_reduce_fusion
  197.2 1.6 conditional.1
  197.2 1.6 broadcast.64
  198.7 2.6 %add_terms.9.sum_ref = f32[4,8,128,128]{3,2,1,0:T(8,128)} custom-call(s32[32]{0:T(128)S(1)} %get-tuple-element.43.refs_0_.plan, f32[2,8,128,128]{3,2,1,0:T(8,128)S(1)} %get-tuple-element.53.more_ref, f32[4,8,128,128]{3,2,1,0:T(8,128)} %get-tuple-element.59.sum_ref), custom_call_target="tpu_custom_call", output_to_operand_aliasing={{}: (2, {})} | custom-call | tf_op jit(solution)/shard_map/add_terms/pallas_call | solution.py:315
  201.4 0.0 copy-done.1
  201.4 2.6 %add_terms.10.sum_ref = f32[4,8,128,128]{3,2,1,0:T(8,128)} custom-call(s32[32]{0:T(128)S(1)} %get-tuple-element.43.refs_0_.plan, f32[2,8,128,128]{3,2,1,0:T(8,128)S(1)} %copy-done.1, f32[4,8,128,128]{3,2,1,0:T(8,128)} %add_terms.9.sum_ref), custom_call_target="tpu_custom_call", output_to_operand_aliasing={{}: (2, {})} | custom-call | tf_op jit(solution)/shard_map/add_terms/pallas_call | solution.py:315
  204.0 2.4 %add_terms.11.sum_ref = f32[4,8,128,128]{3,2,1,0:T(8,128)} custom-call(s32[32]{0:T(128)S(1)} %get-tuple-element.43.refs_0_.plan, f32[1,8,128,128]{3,2,1,0:T(8,128)S(1)} %bitcast.18, f32[4,8,128,128]{3,2,1,0:T(8,128)} %add_terms.10.sum_ref), custom_call_target="tpu_custom_call", output_to_operand_aliasing={{}: (2, {})} | custom-call | tf_op jit(solution)/shard_map/add_terms/pallas_call | solution.py:315
  206.4 0.0 copy-done.3
  206.4 2.6 %add_terms.12.sum_ref = f32[4,8,128,128]{3,2,1,0:T(8,128)} custom-call(s32[32]{0:T(128)S(1)} %get-tuple-element.43.refs_0_.plan, f32[2,8,128,128]{3,2,1,0:T(8,128)S(1)} %copy-done.3, f32[4,8,128,128]{3,2,1,0:T(8,128)} %add_terms.11.sum_ref), custom_call_target="tpu_custom_call", output_to_operand_aliasing={{}: (2, {})} | custom-call | tf_op jit(solution)/shard_map/add_terms/pallas_call | solution.py:315
  209.0 5.2 %collective-permute-done.5 = f32[8,128,128]{2,1,0:T(8,128)S(1)} collective-permute-done((f32[8,128,128]{2,1,0:T(8,128)}, f32[8,128,128]{2,1,0:T(8,128)S(1)}, u32[]{:S(2)}, u32[]{:S(2)}) %collective-permute-start.5) | collective-permute-done | bytes 524320 | tf_op jit(solution)/shard_map/ppermute | solution.py:350
  214.3 2.4 %add_terms.13 = f32[4,8,128,128]{3,2,1,0:T(8,128)} custom-call(s32[32]{0:T(128)S(1)} %get-tuple-element.43.refs_0_.plan, f32[1,8,128,128]{3,2,1,0:T(8,128)S(1)} %bitcast.19, f32[4,8,128,128]{3,2,1,0:T(8,128)} %add_terms.12.sum_ref), custom_call_target="tpu_custom_call", output_to_operand_aliasing={{}: (2, {})} | custom-call | tf_op jit(solution)/shard_map/add_terms/pallas_call | solution.py:315
  216.7 1.1 constant_dynamic-slice_fusion
  217.8 7.8 %collective-permute-done.7 = f32[8,128,128]{2,1,0:T(8,128)} collective-permute-done((f32[8,128,128]{2,1,0:T(8,128)}, f32[8,128,128]{2,1,0:T(8,128)}, u32[]{:S(2)}, u32[]{:S(2)}) %collective-permute-start.7) | collective-permute-done | bytes 524320 | tf_op jit(solution)/shard_map/ppermute | solution.py:350
  225.6 1.9 bitcast_dynamic-update-slice_fusion
  (8 shorter events, 0.0 us)
Async XLA Ops:
  0.0 31.6 %copy-start.6 = (bf16[2,256,256]{2,1,0:T(8,128)(2,1)S(1)}, bf16[2,256,256]{2,1,0:T(8,128)(2,1)}, u32[]{:S(2)}) copy-start(bf16[2,256,256]{2,1,0:T(8,128)(2,1)} %constant.63.clone.refs_4_.refs_5_) | copy-start | bytes 786436
  0.0 13.3 %copy-start.4 = (f32[4,8,128,128]{3,2,1,0:T(8,128)S(1)}, f32[4,8,128,128]{3,2,1,0:T(8,128)}, u32[]{:S(2)}) copy-start(f32[4,8,128,128]{3,2,1,0:T(8,128)} %refs_4_.8) | copy-start | bytes 6291460
  0.0 31.6 %copy-start.7 = (bf16[2,256,256]{2,1,0:T(8,128)(2,1)S(1)}, bf16[2,256,256]{2,1,0:T(8,128)(2,1)}, u32[]{:S(2)}) copy-start(bf16[2,256,256]{2,1,0:T(8,128)(2,1)} %constant.61.clone.refs_5_.refs_6_) | copy-start | bytes 786436
  3.5 28.1 %collective-permute-start.2 = (f32[8,128,128]{2,1,0:T(8,128)}, f32[8,128,128]{2,1,0:T(8,128)S(1)}, u32[]{:S(2)}, u32[]{:S(2)}) collective-permute-start(f32[8,128,128]{2,1,0:T(8,128)} %get-tuple-element.44), channel_id=1, source_target_pairs={{0,64},{16,80},{32,96},{48,112},{64,0},{80,16},{96,32},{112,48},{1... | collective-permute-start | bytes 1572872 | tf_op jit(solution)/shard_map/ppermute | solution.py:350
  34.4 9.0 %copy-start.13 = (f32[8,128,128]{2,1,0:T(8,128)S(1)}, f32[8,128,128]{2,1,0:T(8,128)}, u32[]{:S(2)}) copy-start(f32[8,128,128]{2,1,0:T(8,128)} %get-tuple-element.46) | copy-start | bytes 1572868
  34.4 40.4 %all-to-all-start.2 = ((f32[16,2,8,8,128]{4,3,2,1,0:T(8,128)}), f32[16,2,8,8,128]{4,3,2,1,0:T(8,128)}, u32[]{:S(2)}, u32[]{:S(2)}) async-start(f32[16,2,8,8,128]{4,3,2,1,0:T(8,128)} %forward_planes.5), calls=%async_computation.2 | async-start | bytes 2097152 | tf_op jit(solution)/shard_map/all_to_all | solution.py:345
  43.4 27.4 %collective-permute-start.3 = (f32[8,128,128]{2,1,0:T(8,128)S(1)}, f32[8,128,128]{2,1,0:T(8,128)S(1)}, u32[]{:S(2)}, u32[]{:S(2)}) collective-permute-start(f32[8,128,128]{2,1,0:T(8,128)S(1)} %copy-done.13), channel_id=1, source_target_pairs={{0,64},{16,80},{32,96},{48,112},{64,0},{80,16},{96,32},{112,48},{1... | collective-permute-start | bytes 1572872 | tf_op jit(solution)/shard_map/ppermute | solution.py:350
  45.7 71.4 %copy-start.8 = (f32[8,128,128]{2,1,0:T(8,128)}, f32[8,128,128]{2,1,0:T(8,128)S(1)}, u32[]{:S(2)}) copy-start(f32[8,128,128]{2,1,0:T(8,128)S(1)} %fusion.3.kernel_ref) | copy-start | bytes 1572868
  70.8 4.0 %copy-start.10 = (bf16[2,256,256]{2,1,0:T(8,128)(2,1)S(1)}, bf16[2,256,256]{2,1,0:T(8,128)(2,1)}, u32[]{:S(2)}) copy-start(bf16[2,256,256]{2,1,0:T(8,128)(2,1)} %constant.62.clone.left_ref) | copy-start | bytes 786436
  70.9 4.0 %copy-start.11 = (bf16[2,256,256]{2,1,0:T(8,128)(2,1)S(1)}, bf16[2,256,256]{2,1,0:T(8,128)(2,1)}, u32[]{:S(2)}) copy-start(bf16[2,256,256]{2,1,0:T(8,128)(2,1)} %constant.64.clone.right_ref) | copy-start | bytes 786436
  78.4 38.7 %all-to-all-start.3 = ((f32[16,4,8,8,128]{4,3,2,1,0:T(8,128)}), f32[16,4,8,8,128]{4,3,2,1,0:T(8,128)}, u32[]{:S(2)}, u32[]{:S(2)}) async-start(f32[16,4,8,8,128]{4,3,2,1,0:T(8,128)} %solve_columns.5), calls=%async_computation.3 | async-start | bytes 4194304 | tf_op jit(solution)/shard_map/all_to_all | solution.py:345
  86.2 26.8 %collective-permute-start.4 = (f32[8,128,128]{2,1,0:T(8,128)}, f32[8,128,128]{2,1,0:T(8,128)S(1)}, u32[]{:S(2)}, u32[]{:S(2)}) collective-permute-start(f32[8,128,128]{2,1,0:T(8,128)} %get-tuple-element.48), channel_id=1, source_target_pairs={{0,64},{16,80},{32,96},{48,112},{64,0},{80,16},{96,32},{112,48},{1... | collective-permute-start | bytes 1572872 | tf_op jit(solution)/shard_map/ppermute | solution.py:350
  120.6 39.5 %all-to-all-start.4 = ((f32[16,4,8,8,128]{4,3,2,1,0:T(8,128)}), f32[16,4,8,8,128]{4,3,2,1,0:T(8,128)}, u32[]{:S(2)}, u32[]{:S(2)}) async-start(f32[16,4,8,8,128]{4,3,2,1,0:T(8,128)} %solve_columns.6), calls=%async_computation.4 | async-start | bytes 4194304 | tf_op jit(solution)/shard_map/all_to_all | solution.py:345
  132.0 28.1 %collective-permute-start.6 = (f32[8,128,128]{2,1,0:T(8,128)}, f32[8,128,128]{2,1,0:T(8,128)S(1)}, u32[]{:S(2)}, u32[]{:S(2)}) collective-permute-start(f32[8,128,128]{2,1,0:T(8,128)} %get-tuple-element.50), channel_id=1, source_target_pairs={{0,64},{16,80},{32,96},{48,112},{64,0},{80,16},{96,32},{112,48},{1... | collective-permute-start | bytes 1572872 | tf_op jit(solution)/shard_map/ppermute | solution.py:350
  163.8 24.6 %all-to-all-start.5 = ((f32[16,2,8,8,128]{4,3,2,1,0:T(8,128)}), f32[16,2,8,8,128]{4,3,2,1,0:T(8,128)}, u32[]{:S(2)}, u32[]{:S(2)}) async-start(f32[16,2,8,8,128]{4,3,2,1,0:T(8,128)} %solve_columns.7), calls=%async_computation.5 | async-start | bytes 2097152 | tf_op jit(solution)/shard_map/all_to_all | solution.py:345
  175.2 1.0 copy-start
  176.2 19.4 %copy-start.14 = (s32[128]{0:T(128)S(1)}, s32[128]{0:T(128)}, u32[]{:S(2)}) copy-start(s32[128]{0:T(128)} %spin.1) | copy-start | bytes 1540
  176.2 38.0 %collective-permute-start.5 = (f32[8,128,128]{2,1,0:T(8,128)}, f32[8,128,128]{2,1,0:T(8,128)S(1)}, u32[]{:S(2)}, u32[]{:S(2)}) collective-permute-start(f32[8,128,128]{2,1,0:T(8,128)} %get-tuple-element.49), channel_id=1, source_target_pairs={{0,64},{16,80},{32,96},{48,112},{64,0},{80,16},{96,32},{112,48},{1... | collective-permute-start | bytes 1572872 | tf_op jit(solution)/shard_map/ppermute | solution.py:350
  192.5 1.0 copy-start.2
  193.5 32.1 %collective-permute-start.7 = (f32[8,128,128]{2,1,0:T(8,128)}, f32[8,128,128]{2,1,0:T(8,128)}, u32[]{:S(2)}, u32[]{:S(2)}) collective-permute-start(f32[8,128,128]{2,1,0:T(8,128)} %get-tuple-element.54), channel_id=1, source_target_pairs={{0,64},{16,80},{32,96},{48,112},{64,0},{80,16},{96,32},{112,48},{1... | collective-permute-start | bytes 1572872 | tf_op jit(solution)/shard_map/ppermute | solution.py:350
  198.7 2.6 %copy-start.1 = (f32[2,8,128,128]{3,2,1,0:T(8,128)S(1)}, f32[2,8,128,128]{3,2,1,0:T(8,128)}, u32[]{:S(2)}) copy-start(f32[2,8,128,128]{3,2,1,0:T(8,128)} %copy-done) | copy-start | bytes 3145732
  204.0 2.4 %copy-start.3 = (f32[2,8,128,128]{3,2,1,0:T(8,128)S(1)}, f32[2,8,128,128]{3,2,1,0:T(8,128)}, u32[]{:S(2)}) copy-start(f32[2,8,128,128]{3,2,1,0:T(8,128)} %copy-done.2) | copy-start | bytes 3145732

commit v2 on v1

--- a/solution.py
+++ b/solution.py
@@ -12,7 +12,7 @@
 ORBITALS = 4
 LANES = 128
 VMEM_BYTES = 40 * 2**20
-EARLY = pl.CostEstimate(flops=0, bytes_accessed=200 * 10**6, transcendentals=0)
+EARLY = pl.CostEstimate(flops=10**11, bytes_accessed=200 * 10**6, transcendentals=0)
 ROUNDS = 3
 ENTRY = 8
 
@@ -263,7 +263,7 @@
     )(plan, u, orbitals, orbitals, right, left)
 
 
-def solve(arrived, kernel, left, right, ahead, after):
+def solve(arrived, kernel, left, right, ahead=None):
     hbm = pl.BlockSpec(memory_space=pl.ANY)
     operands = [in_hbm(arrived), kernel, left, right]
     specs = [part(arrived.shape, 0), whole(kernel.shape), whole(left.shape), whole(right.shape)]
@@ -276,13 +276,13 @@
     return pl.pallas_call(
         solve_kernel,
         grid=(1,),
-        in_specs=specs + [hbm] * len(after),
+        in_specs=specs,
         out_specs=part(shape, place),
         out_shape=pltpu.HBM(shape, jnp.float32),
         input_output_aliases=aliases,
         compiler_params=params(),
         name="solve_columns",
-    )(*operands, *after)
+    )(*operands)
 
 
 def inverse(number, place, plan, arrived, u, orbitals, left, right):
@@ -302,7 +302,7 @@
             ],
             out_specs=[whole(own), whole(u.shape)],
         ),
-        out_shape=[jax.ShapeDtypeStruct(own, jnp.float32), pltpu.HBM(u.shape, jnp.float32)],
+        out_shape=[pltpu.HBM(own, jnp.float32), pltpu.HBM(u.shape, jnp.float32)],
         compiler_params=params(),
         name="inverse_planes",
     )(plan, in_hbm(arrived), u, orbitals, orbitals, left, right)
@@ -358,7 +358,7 @@
     plus, plus_x, minus, minus_x = tables
     u = to_partner(sent_orbital(number, plan, orbitals))
     arrived = exchange(forward(number, 1, plan, u, orbitals, minus, plus))
-    arrived = exchange(solve(arrived, kernel, plus_x, minus_x, None, ()))
+    arrived = exchange(solve(arrived, kernel, plus_x, minus_x))
     own, back = inverse(number, 0, plan, arrived, u, orbitals, minus, plus)
     total = add_into(number, 0, plan, total, own)
     return add_into(number, 4, plan, total, to_partner(back)[None])
@@ -389,8 +389,10 @@
     arrived = exchange(planes_of(0))
     for number in range(ROUNDS):
         ahead = planes_of(number + 1) if number + 1 < ROUNDS else None
-        after = returned[:max(number - 1, 0)]
-        arrived = exchange(solve(arrived, kernel, plus_x, minus_x, ahead, after))
+        leaving = solve(arrived, kernel, plus_x, minus_x, ahead)
+        if number > 1:
+            leaving, returned[number - 2] = lax.optimization_barrier((leaving, returned[number - 2]))
+        arrived = exchange(leaving)
         own, back = inverse(number, 0 if ahead is None else 1, plan, arrived, us[number], orbitals, minus, plus)
         returned.append(to_partner(back))
         total = add_into(number, 0, plan, total, own)

time: 229 us -> 212 us (0.926)
  waiting for transfers between devices: 117 us -> 96.4 us
  starting transfers between devices: 46.9 us -> 50.1 us
    ppermute x6, waiting for transfers between devices: 106 us -> 48 us  [to_partner(): return lax.ppermute(value, 'band', pairs)]
    all_to_all x4, waiting for transfers between devices: 10.1 us -> 48.4 us  [exchange(): lax.all_to_all(field, 'grid', split_axis=0, concat_axis=0, tiled=True)]
    ppermute x6, starting transfers between devices: 15.6 us -> 18.6 us  [to_partner(): return lax.ppermute(value, 'band', pairs)]
  transfers between devices with their start and end apart: 10 -> 10, of which waited for: 7 -> 10; matrix products, arithmetic and copies ran while one was open for 2% -> 3% of each run, Pallas kernels for 15% -> 21%
where the time goes in v2:
time: 212 us; the launch traced here: 211 us
  waiting for transfers between devices  96.4 us (45%)
  Pallas kernels  51.9 us (24%)
  starting transfers between devices  50.1 us (24%)
  local copies, waits for them, and re-layouts  4.51 us (2%)
  between operations  4.41 us (2%)
  other arithmetic  3.84 us (2%)
    all_to_all x4, waiting for transfers between devices, exchange(): lax.all_to_all(field, 'grid', split_axis=0, concat_axis=0, tiled=True)  48.4 us
    ppermute x6, waiting for transfers between devices, to_partner(): return lax.ppermute(value, 'band', pairs)  48 us
    all_to_all x4, starting transfers between devices, exchange(): lax.all_to_all(field, 'grid', split_axis=0, concat_axis=0, tiled=True)  31.4 us
    ppermute x6, starting transfers between devices, to_partner(): return lax.ppermute(value, 'band', pairs)  18.6 us
    pallas_call x3, Pallas kernels, inverse(): pl.pallas_call(lambda *refs: inverse_kernel(number, *refs), grid_spec=plt...  13.4 us
    pallas_call x5, Pallas kernels, add_into(): pl.pallas_call(add_kernel, grid_spec=pltpu.PrefetchScalarGridSpec(num_sca...  12.7 us
    pallas_call x3, Pallas kernels, forward(): pl.pallas_call(lambda *refs: forward_kernel(number, *refs), grid_spec=plt...  11.9 us
    pallas_call x3, Pallas kernels, solve(): pl.pallas_call(solve_kernel, grid=(1,), in_specs=specs, out_specs=part(sh...  10.6 us
  transfers between devices with their start and end apart: 10, of which 10 were waited for; matrix products, arithmetic and copies ran while one was open for 3% of the time, Pallas kernels for 21%

profile of v2, /device:TPU:1, one launch (start us, length us, event | category | flops | bytes accessed | tf_op | source)
XLA Modules:
  0.0 211.2 jit_solution(12160305760744701215)
XLA Ops:
  0.0 0.0 copy-start.7
  0.0 0.0 copy-start.4
  0.0 3.3 %plan_rounds.1 = (s32[32]{0:T(128)S(1)}, f32[8,128,128]{2,1,0:T(8,128)}) custom-call(s32[128]{0:T(128)} %spin.1, s32[512,1,128]{2,1,0:T(1,128)} %constant.60.clone.table_ref, f32[4,8,128,128]{3,2,1,0:T(8,128)} %refs_4_.8), custom_call_target="tpu_custom_call" | custom-call | tf_op jit(solution)/shard_map/plan_rounds/pallas_call | solution.py:100
  3.4 5.7 %collective-permute-start.2 = (f32[8,128,128]{2,1,0:T(8,128)}, f32[8,128,128]{2,1,0:T(8,128)S(1)}, u32[]{:S(2)}, u32[]{:S(2)}) collective-permute-start(f32[8,128,128]{2,1,0:T(8,128)} %get-tuple-element.45), channel_id=1, source_target_pairs={{0,64},{16,80},{32,96},{48,112},{64,0},{80,16},{96,32},{112,48},{1... | collective-permute-start | bytes 1572872 | tf_op jit(solution)/shard_map/ppermute | solution.py:350
  9.1 0.7 fusion.6
  13.4 0.0 copy-done.4
  13.4 1.1 dynamic-slice_bitcast_fusion.1
  14.5 17.0 %collective-permute-done.2.refs_1_.refs_2_ = f32[8,128,128]{2,1,0:T(8,128)S(1)} collective-permute-done((f32[8,128,128]{2,1,0:T(8,128)}, f32[8,128,128]{2,1,0:T(8,128)S(1)}, u32[]{:S(2)}, u32[]{:S(2)}) %collective-permute-start.2) | collective-permute-done | bytes 524320 | tf_op jit(solution)/shard_map/ppermute | solution.py:350
  31.5 1.9 collective-permute-start.3
  33.4 0.1 broadcast_add_fusion
  33.5 1.0 fusion.3.kernel_ref
  34.5 0.0 copy-done.7
  34.5 3.8 %forward_planes.5 = f32[16,2,8,8,128]{4,3,2,1,0:T(8,128)} custom-call(s32[32]{0:T(128)S(1)} %get-tuple-element.44.refs_0_.plan, f32[8,128,128]{2,1,0:T(8,128)S(1)} %collective-permute-done.2.refs_1_.refs_2_, f32[4,8,128,128]{3,2,1,0:T(8,128)S(1)} %copy-done.4, f32[4,8,128,128]{3,2,1,0:T(8,128)S(1)} %copy-done.4, bf16[2,256,256]{2,1,0:T(8,128)(2,1)S(1)} %copy-done.7, ...), custom_call_target="tpu_custom_call" | custom-call | tf_op jit(solution)/shard_map/forward_planes/pallas_call | solution.py:245
  38.3 0.0 copy-start.8
  38.3 9.0 %all-to-all-start.2 = ((f32[16,2,8,8,128]{4,3,2,1,0:T(8,128)}), f32[16,2,8,8,128]{4,3,2,1,0:T(8,128)}, u32[]{:S(2)}, u32[]{:S(2)}) async-start(f32[16,2,8,8,128]{4,3,2,1,0:T(8,128)} %forward_planes.5), calls=%async_computation.2 | async-start | bytes 2097152 | tf_op jit(solution)/shard_map/all_to_all | solution.py:345
  47.3 10.0 %collective-permute-done.3.refs_1_.refs_2_ = f32[8,128,128]{2,1,0:T(8,128)S(1)} collective-permute-done((f32[8,128,128]{2,1,0:T(8,128)}, f32[8,128,128]{2,1,0:T(8,128)S(1)}, u32[]{:S(2)}, u32[]{:S(2)}) %collective-permute-start.3) | collective-permute-done | bytes 524320 | tf_op jit(solution)/shard_map/ppermute | solution.py:350
  57.3 0.0 copy-start.6
  57.3 0.0 copy-start.9
  57.3 0.0 copy-start.10
  57.3 2.0 collective-permute-start.4
  59.4 0.0 copy-done.8
  59.4 4.0 %forward_planes.6.rest_0_ = f32[16,4,8,8,128]{4,3,2,1,0:T(8,128)} custom-call(s32[32]{0:T(128)S(1)} %get-tuple-element.44.refs_0_.plan, f32[8,128,128]{2,1,0:T(8,128)S(1)} %collective-permute-done.3.refs_1_.refs_2_, f32[4,8,128,128]{3,2,1,0:T(8,128)} %refs_4_.8, f32[4,8,128,128]{3,2,1,0:T(8,128)} %refs_4_.8, bf16[2,256,256]{2,1,0:T(8,128)(2,1)S(1)} %copy-done.7, ...), custom_call_target="tpu_custom_call" | custom-call | flops 99999997952 | bytes 200000000 | tf_op jit(solution)/shard_map/forward_planes/pallas_call | solution.py:245
  63.4 1.2 all-to-all-done.2.in_ref
  64.6 0.0 copy-done.6
  64.6 0.0 copy-done.9
  64.6 0.0 copy-done.10
  64.6 3.5 %solve_columns.5 = f32[16,4,8,8,128]{4,3,2,1,0:T(8,128)} custom-call(f32[16,2,8,8,128]{4,3,2,1,0:T(8,128)} %all-to-all-done.2.in_ref, f32[8,128,128]{2,1,0:T(8,128)S(1)} %copy-done.6, bf16[2,256,256]{2,1,0:T(8,128)(2,1)S(1)} %copy-done.9, bf16[2,256,256]{2,1,0:T(8,128)(2,1)S(1)} %copy-done.10, ...), custom_call_target="tpu_custom_call", output_to_operand_aliasing={{}: (4, {})} | custom-call | tf_op jit(solution)/shard_map/solve_columns/pallas_call | solution.py:276
  68.1 9.2 %all-to-all-start.3 = ((f32[16,4,8,8,128]{4,3,2,1,0:T(8,128)}), f32[16,4,8,8,128]{4,3,2,1,0:T(8,128)}, u32[]{:S(2)}, u32[]{:S(2)}) async-start(f32[16,4,8,8,128]{4,3,2,1,0:T(8,128)} %solve_columns.5), calls=%async_computation.3 | async-start | bytes 4194304 | tf_op jit(solution)/shard_map/all_to_all | solution.py:345
  77.3 7.4 %collective-permute-done.4.refs_1_.refs_2_ = f32[8,128,128]{2,1,0:T(8,128)S(1)} collective-permute-done((f32[8,128,128]{2,1,0:T(8,128)}, f32[8,128,128]{2,1,0:T(8,128)S(1)}, u32[]{:S(2)}, u32[]{:S(2)}) %collective-permute-start.4) | collective-permute-done | bytes 524320 | tf_op jit(solution)/shard_map/ppermute | solution.py:350
  84.7 4.1 %forward_planes.7.rest_0_ = f32[16,4,8,8,128]{4,3,2,1,0:T(8,128)} custom-call(s32[32]{0:T(128)S(1)} %get-tuple-element.44.refs_0_.plan, f32[8,128,128]{2,1,0:T(8,128)S(1)} %collective-permute-done.4.refs_1_.refs_2_, f32[4,8,128,128]{3,2,1,0:T(8,128)} %refs_4_.8, f32[4,8,128,128]{3,2,1,0:T(8,128)} %refs_4_.8, bf16[2,256,256]{2,1,0:T(8,128)(2,1)S(1)} %copy-done.7, ...), custom_call_target="tpu_custom_call" | custom-call | flops 99999997952 | bytes 200000000 | tf_op jit(solution)/shard_map/forward_planes/pallas_call | solution.py:245
  88.8 17.1 %all-to-all-done.3.in_ref.refs_1_ = f32[16,4,8,8,128]{4,3,2,1,0:T(8,128)} async-done(((f32[16,4,8,8,128]{4,3,2,1,0:T(8,128)}), f32[16,4,8,8,128]{4,3,2,1,0:T(8,128)}, u32[]{:S(2)}, u32[]{:S(2)}) %all-to-all-start.3) | async-done | bytes 2097184 | tf_op jit(solution)/shard_map/all_to_all | solution.py:345
  105.8 3.6 %solve_columns.6 = f32[16,4,8,8,128]{4,3,2,1,0:T(8,128)} custom-call(f32[16,4,8,8,128]{4,3,2,1,0:T(8,128)} %all-to-all-done.3.in_ref.refs_1_, f32[8,128,128]{2,1,0:T(8,128)S(1)} %copy-done.6, bf16[2,256,256]{2,1,0:T(8,128)(2,1)S(1)} %copy-done.9, bf16[2,256,256]{2,1,0:T(8,128)(2,1)S(1)} %copy-done.10, ...), custom_call_target="tpu_custom_call", output_to_operand_aliasing={{}: (4, {})} | custom-call | tf_op jit(solution)/shard_map/solve_columns/pallas_call | solution.py:276
  109.4 5.7 %all-to-all-start.4 = ((f32[16,4,8,8,128]{4,3,2,1,0:T(8,128)}), f32[16,4,8,8,128]{4,3,2,1,0:T(8,128)}, u32[]{:S(2)}, u32[]{:S(2)}) async-start(f32[16,4,8,8,128]{4,3,2,1,0:T(8,128)} %solve_columns.6), calls=%async_computation.4 | async-start | bytes 4194304 | tf_op jit(solution)/shard_map/all_to_all | solution.py:345
  115.1 4.5 %inverse_planes.6 = (f32[2,8,128,128]{3,2,1,0:T(8,128)}, f32[8,128,128]{2,1,0:T(8,128)}) custom-call(s32[32]{0:T(128)S(1)} %get-tuple-element.44.refs_0_.plan, f32[16,4,8,8,128]{4,3,2,1,0:T(8,128)} %all-to-all-done.3.in_ref.refs_1_, f32[8,128,128]{2,1,0:T(8,128)S(1)} %collective-permute-done.2.refs_1_.refs_2_, f32[4,8,128,128]{3,2,1,0:T(8,128)} %refs_4_.8, ...), custom_call_target="tpu_custom_call" | custom-call | tf_op jit(solution)/shard_map/inverse_planes/pallas_call | solution.py:290
  119.5 4.5 %collective-permute-start.6 = (f32[8,128,128]{2,1,0:T(8,128)}, f32[8,128,128]{2,1,0:T(8,128)S(1)}, u32[]{:S(2)}, u32[]{:S(2)}) collective-permute-start(f32[8,128,128]{2,1,0:T(8,128)} %get-tuple-element.51), channel_id=1, source_target_pairs={{0,64},{16,80},{32,96},{48,112},{64,0},{80,16},{96,32},{112,48},{1... | collective-permute-start | bytes 1572872 | tf_op jit(solution)/shard_map/ppermute | solution.py:350
  124.1 19.5 %all-to-all-done.4.refs_1_.in_ref = f32[16,4,8,8,128]{4,3,2,1,0:T(8,128)} async-done(((f32[16,4,8,8,128]{4,3,2,1,0:T(8,128)}), f32[16,4,8,8,128]{4,3,2,1,0:T(8,128)}, u32[]{:S(2)}, u32[]{:S(2)}) %all-to-all-start.4) | async-done | bytes 2097184 | tf_op jit(solution)/shard_map/all_to_all | solution.py:345
  143.6 3.5 %solve_columns.7 = f32[16,2,8,8,128]{4,3,2,1,0:T(8,128)} custom-call(f32[16,4,8,8,128]{4,3,2,1,0:T(8,128)} %all-to-all-done.4.refs_1_.in_ref, f32[8,128,128]{2,1,0:T(8,128)S(1)} %copy-done.6, bf16[2,256,256]{2,1,0:T(8,128)(2,1)S(1)} %copy-done.9, bf16[2,256,256]{2,1,0:T(8,128)(2,1)S(1)} %copy-done.10), custom_call_target="tpu_custom_call" | custom-call | tf_op jit(solution)/shard_map/solve_columns/pallas_call | solution.py:276
  147.1 0.5 collective-permute-done.6
  147.7 7.6 %all-to-all-start.5 = ((f32[16,2,8,8,128]{4,3,2,1,0:T(8,128)}), f32[16,2,8,8,128]{4,3,2,1,0:T(8,128)}, u32[]{:S(2)}, u32[]{:S(2)}) async-start(f32[16,2,8,8,128]{4,3,2,1,0:T(8,128)} %solve_columns.7), calls=%async_computation.5 | async-start | bytes 2097152 | tf_op jit(solution)/shard_map/all_to_all | solution.py:345
  155.3 4.5 %inverse_planes.5 = (f32[2,8,128,128]{3,2,1,0:T(8,128)}, f32[8,128,128]{2,1,0:T(8,128)}) custom-call(s32[32]{0:T(128)S(1)} %get-tuple-element.44.refs_0_.plan, f32[16,4,8,8,128]{4,3,2,1,0:T(8,128)} %all-to-all-done.4.refs_1_.in_ref, f32[8,128,128]{2,1,0:T(8,128)S(1)} %collective-permute-done.3.refs_1_.refs_2_, f32[4,8,128,128]{3,2,1,0:T(8,128)} %refs_4_.8, ...), custom_call_target="tpu_custom_call" | custom-call | tf_op jit(solution)/shard_map/inverse_planes/pallas_call | solution.py:290
  159.8 0.0 copy-start.12
  159.8 2.2 %collective-permute-start.5 = (f32[8,128,128]{2,1,0:T(8,128)}, f32[8,128,128]{2,1,0:T(8,128)S(1)}, u32[]{:S(2)}, u32[]{:S(2)}) collective-permute-start(f32[8,128,128]{2,1,0:T(8,128)} %get-tuple-element.50), channel_id=1, source_target_pairs={{0,64},{16,80},{32,96},{48,112},{64,0},{80,16},{96,32},{112,48},{1... | collective-permute-start | bytes 1572872 | tf_op jit(solution)/shard_map/ppermute | solution.py:350
  162.0 10.6 %all-to-all-done.5.refs_1_ = f32[16,2,8,8,128]{4,3,2,1,0:T(8,128)} async-done(((f32[16,2,8,8,128]{4,3,2,1,0:T(8,128)}), f32[16,2,8,8,128]{4,3,2,1,0:T(8,128)}, u32[]{:S(2)}, u32[]{:S(2)}) %all-to-all-start.5) | async-done | bytes 1048608 | tf_op jit(solution)/shard_map/all_to_all | solution.py:345
  172.6 4.4 %inverse_planes.7 = (f32[2,8,128,128]{3,2,1,0:T(8,128)}, f32[8,128,128]{2,1,0:T(8,128)}) custom-call(s32[32]{0:T(128)S(1)} %get-tuple-element.44.refs_0_.plan, f32[16,2,8,8,128]{4,3,2,1,0:T(8,128)} %all-to-all-done.5.refs_1_, f32[8,128,128]{2,1,0:T(8,128)S(1)} %collective-permute-done.4.refs_1_.refs_2_, f32[4,8,128,128]{3,2,1,0:T(8,128)} %refs_4_.8, ...), custom_call_target="tpu_custom_call" | custom-call | tf_op jit(solution)/shard_map/inverse_planes/pallas_call | solution.py:290
  177.0 2.2 %collective-permute-start.7 = (f32[8,128,128]{2,1,0:T(8,128)}, f32[8,128,128]{2,1,0:T(8,128)}, u32[]{:S(2)}, u32[]{:S(2)}) collective-permute-start(f32[8,128,128]{2,1,0:T(8,128)} %get-tuple-element.56), channel_id=1, source_target_pairs={{0,64},{16,80},{32,96},{48,112},{64,0},{80,16},{96,32},{112,48},{1... | collective-permute-start | bytes 1572872 | tf_op jit(solution)/shard_map/ppermute | solution.py:350
  179.3 0.0 copy-done.12
  179.3 0.1 reshape.64
  179.4 0.2 reduce_sum.9
  179.5 0.6 or_reduce_fusion
  180.8 0.0 copy-start
  180.8 1.6 conditional.1
  180.9 1.6 broadcast.64
  182.4 0.0 copy-done
  182.4 2.6 %add_terms.9.sum_ref = f32[4,8,128,128]{3,2,1,0:T(8,128)} custom-call(s32[32]{0:T(128)S(1)} %get-tuple-element.44.refs_0_.plan, f32[2,8,128,128]{3,2,1,0:T(8,128)S(1)} %copy-done, f32[4,8,128,128]{3,2,1,0:T(8,128)} %get-tuple-element.61.sum_ref), custom_call_target="tpu_custom_call", output_to_operand_aliasing={{}: (2, {})} | custom-call | tf_op jit(solution)/shard_map/add_terms/pallas_call | solution.py:315
  185.1 0.0 copy-done.1
  185.1 2.6 %add_terms.10.sum_ref = f32[4,8,128,128]{3,2,1,0:T(8,128)} custom-call(s32[32]{0:T(128)S(1)} %get-tuple-element.44.refs_0_.plan, f32[2,8,128,128]{3,2,1,0:T(8,128)S(1)} %copy-done.1, f32[4,8,128,128]{3,2,1,0:T(8,128)} %add_terms.9.sum_ref), custom_call_target="tpu_custom_call", output_to_operand_aliasing={{}: (2, {})} | custom-call | tf_op jit(solution)/shard_map/add_terms/pallas_call | solution.py:315
  187.7 2.4 %add_terms.11.sum_ref = f32[4,8,128,128]{3,2,1,0:T(8,128)} custom-call(s32[32]{0:T(128)S(1)} %get-tuple-element.44.refs_0_.plan, f32[1,8,128,128]{3,2,1,0:T(8,128)S(1)} %bitcast.18, f32[4,8,128,128]{3,2,1,0:T(8,128)} %add_terms.10.sum_ref), custom_call_target="tpu_custom_call", output_to_operand_aliasing={{}: (2, {})} | custom-call | tf_op jit(solution)/shard_map/add_terms/pallas_call | solution.py:315
  190.1 0.0 copy-done.2
  190.1 2.6 %add_terms.12.sum_ref = f32[4,8,128,128]{3,2,1,0:T(8,128)} custom-call(s32[32]{0:T(128)S(1)} %get-tuple-element.44.refs_0_.plan, f32[2,8,128,128]{3,2,1,0:T(8,128)S(1)} %copy-done.2, f32[4,8,128,128]{3,2,1,0:T(8,128)} %add_terms.11.sum_ref), custom_call_target="tpu_custom_call", output_to_operand_aliasing={{}: (2, {})} | custom-call | tf_op jit(solution)/shard_map/add_terms/pallas_call | solution.py:315
  192.7 5.2 %collective-permute-done.5 = f32[8,128,128]{2,1,0:T(8,128)S(1)} collective-permute-done((f32[8,128,128]{2,1,0:T(8,128)}, f32[8,128,128]{2,1,0:T(8,128)S(1)}, u32[]{:S(2)}, u32[]{:S(2)}) %collective-permute-start.5) | collective-permute-done | bytes 524320 | tf_op jit(solution)/shard_map/ppermute | solution.py:350
  197.9 2.4 %add_terms.13 = f32[4,8,128,128]{3,2,1,0:T(8,128)} custom-call(s32[32]{0:T(128)S(1)} %get-tuple-element.44.refs_0_.plan, f32[1,8,128,128]{3,2,1,0:T(8,128)S(1)} %bitcast.19, f32[4,8,128,128]{3,2,1,0:T(8,128)} %add_terms.12.sum_ref), custom_call_target="tpu_custom_call", output_to_operand_aliasing={{}: (2, {})} | custom-call | tf_op jit(solution)/shard_map/add_terms/pallas_call | solution.py:315
  200.4 1.1 constant_dynamic-slice_fusion
  201.5 7.8 %collective-permute-done.7 = f32[8,128,128]{2,1,0:T(8,128)} collective-permute-done((f32[8,128,128]{2,1,0:T(8,128)}, f32[8,128,128]{2,1,0:T(8,128)}, u32[]{:S(2)}, u32[]{:S(2)}) %collective-permute-start.7) | collective-permute-done | bytes 524320 | tf_op jit(solution)/shard_map/ppermute | solution.py:350
  209.3 1.9 bitcast_dynamic-update-slice_fusion
  (4 shorter events, 0.0 us)
Async XLA Ops:
  0.0 34.5 %copy-start.7 = (bf16[2,256,256]{2,1,0:T(8,128)(2,1)S(1)}, bf16[2,256,256]{2,1,0:T(8,128)(2,1)}, u32[]{:S(2)}) copy-start(bf16[2,256,256]{2,1,0:T(8,128)(2,1)} %constant.63.clone.refs_4_.refs_5_) | copy-start | bytes 786436
  0.0 13.4 %copy-start.4 = (f32[4,8,128,128]{3,2,1,0:T(8,128)S(1)}, f32[4,8,128,128]{3,2,1,0:T(8,128)}, u32[]{:S(2)}) copy-start(f32[4,8,128,128]{3,2,1,0:T(8,128)} %refs_4_.8) | copy-start | bytes 6291460
  3.4 28.1 %collective-permute-start.2 = (f32[8,128,128]{2,1,0:T(8,128)}, f32[8,128,128]{2,1,0:T(8,128)S(1)}, u32[]{:S(2)}, u32[]{:S(2)}) collective-permute-start(f32[8,128,128]{2,1,0:T(8,128)} %get-tuple-element.45), channel_id=1, source_target_pairs={{0,64},{16,80},{32,96},{48,112},{64,0},{80,16},{96,32},{112,48},{1... | collective-permute-start | bytes 1572872 | tf_op jit(solution)/shard_map/ppermute | solution.py:350
  31.5 25.8 %collective-permute-start.3 = (f32[8,128,128]{2,1,0:T(8,128)}, f32[8,128,128]{2,1,0:T(8,128)S(1)}, u32[]{:S(2)}, u32[]{:S(2)}) collective-permute-start(f32[8,128,128]{2,1,0:T(8,128)} %get-tuple-element.47), channel_id=1, source_target_pairs={{0,64},{16,80},{32,96},{48,112},{64,0},{80,16},{96,32},{112,48},{1... | collective-permute-start | bytes 1572872 | tf_op jit(solution)/shard_map/ppermute | solution.py:350
  38.3 21.1 %copy-start.8 = (bf16[2,256,256]{2,1,0:T(8,128)(2,1)S(1)}, bf16[2,256,256]{2,1,0:T(8,128)(2,1)}, u32[]{:S(2)}) copy-start(bf16[2,256,256]{2,1,0:T(8,128)(2,1)} %constant.61.clone.refs_5_.refs_6_) | copy-start | bytes 786436
  38.3 26.3 %all-to-all-start.2 = ((f32[16,2,8,8,128]{4,3,2,1,0:T(8,128)}), f32[16,2,8,8,128]{4,3,2,1,0:T(8,128)}, u32[]{:S(2)}, u32[]{:S(2)}) async-start(f32[16,2,8,8,128]{4,3,2,1,0:T(8,128)} %forward_planes.5), calls=%async_computation.2 | async-start | bytes 2097152 | tf_op jit(solution)/shard_map/all_to_all | solution.py:345
  57.3 7.3 %copy-start.6 = (f32[8,128,128]{2,1,0:T(8,128)S(1)}, f32[8,128,128]{2,1,0:T(8,128)}, u32[]{:S(2)}) copy-start(f32[8,128,128]{2,1,0:T(8,128)} %fusion.3.kernel_ref) | copy-start | bytes 1572868
  57.3 7.3 %copy-start.9 = (bf16[2,256,256]{2,1,0:T(8,128)(2,1)S(1)}, bf16[2,256,256]{2,1,0:T(8,128)(2,1)}, u32[]{:S(2)}) copy-start(bf16[2,256,256]{2,1,0:T(8,128)(2,1)} %constant.62.clone.left_ref) | copy-start | bytes 786436
  57.3 7.3 %copy-start.10 = (bf16[2,256,256]{2,1,0:T(8,128)(2,1)S(1)}, bf16[2,256,256]{2,1,0:T(8,128)(2,1)}, u32[]{:S(2)}) copy-start(bf16[2,256,256]{2,1,0:T(8,128)(2,1)} %constant.64.clone.right_ref) | copy-start | bytes 786436
  57.3 27.3 %collective-permute-start.4 = (f32[8,128,128]{2,1,0:T(8,128)}, f32[8,128,128]{2,1,0:T(8,128)S(1)}, u32[]{:S(2)}, u32[]{:S(2)}) collective-permute-start(f32[8,128,128]{2,1,0:T(8,128)} %get-tuple-element.49), channel_id=1, source_target_pairs={{0,64},{16,80},{32,96},{48,112},{64,0},{80,16},{96,32},{112,48},{1... | collective-permute-start | bytes 1572872 | tf_op jit(solution)/shard_map/ppermute | solution.py:350
  68.1 37.7 %all-to-all-start.3 = ((f32[16,4,8,8,128]{4,3,2,1,0:T(8,128)}), f32[16,4,8,8,128]{4,3,2,1,0:T(8,128)}, u32[]{:S(2)}, u32[]{:S(2)}) async-start(f32[16,4,8,8,128]{4,3,2,1,0:T(8,128)} %solve_columns.5), calls=%async_computation.3 | async-start | bytes 4194304 | tf_op jit(solution)/shard_map/all_to_all | solution.py:345
  109.4 34.2 %all-to-all-start.4 = ((f32[16,4,8,8,128]{4,3,2,1,0:T(8,128)}), f32[16,4,8,8,128]{4,3,2,1,0:T(8,128)}, u32[]{:S(2)}, u32[]{:S(2)}) async-start(f32[16,4,8,8,128]{4,3,2,1,0:T(8,128)} %solve_columns.6), calls=%async_computation.4 | async-start | bytes 4194304 | tf_op jit(solution)/shard_map/all_to_all | solution.py:345
  119.5 28.1 %collective-permute-start.6 = (f32[8,128,128]{2,1,0:T(8,128)}, f32[8,128,128]{2,1,0:T(8,128)S(1)}, u32[]{:S(2)}, u32[]{:S(2)}) collective-permute-start(f32[8,128,128]{2,1,0:T(8,128)} %get-tuple-element.51), channel_id=1, source_target_pairs={{0,64},{16,80},{32,96},{48,112},{64,0},{80,16},{96,32},{112,48},{1... | collective-permute-start | bytes 1572872 | tf_op jit(solution)/shard_map/ppermute | solution.py:350
  147.7 24.9 %all-to-all-start.5 = ((f32[16,2,8,8,128]{4,3,2,1,0:T(8,128)}), f32[16,2,8,8,128]{4,3,2,1,0:T(8,128)}, u32[]{:S(2)}, u32[]{:S(2)}) async-start(f32[16,2,8,8,128]{4,3,2,1,0:T(8,128)} %solve_columns.7), calls=%async_computation.5 | async-start | bytes 2097152 | tf_op jit(solution)/shard_map/all_to_all | solution.py:345
  159.8 19.5 %copy-start.12 = (s32[128]{0:T(128)S(1)}, s32[128]{0:T(128)}, u32[]{:S(2)}) copy-start(s32[128]{0:T(128)} %spin.1) | copy-start | bytes 1540
  159.8 38.2 %collective-permute-start.5 = (f32[8,128,128]{2,1,0:T(8,128)}, f32[8,128,128]{2,1,0:T(8,128)S(1)}, u32[]{:S(2)}, u32[]{:S(2)}) collective-permute-start(f32[8,128,128]{2,1,0:T(8,128)} %get-tuple-element.50), channel_id=1, source_target_pairs={{0,64},{16,80},{32,96},{48,112},{64,0},{80,16},{96,32},{112,48},{1... | collective-permute-start | bytes 1572872 | tf_op jit(solution)/shard_map/ppermute | solution.py:350
  177.0 32.3 %collective-permute-start.7 = (f32[8,128,128]{2,1,0:T(8,128)}, f32[8,128,128]{2,1,0:T(8,128)}, u32[]{:S(2)}, u32[]{:S(2)}) collective-permute-start(f32[8,128,128]{2,1,0:T(8,128)} %get-tuple-element.56), channel_id=1, source_target_pairs={{0,64},{16,80},{32,96},{48,112},{64,0},{80,16},{96,32},{112,48},{1... | collective-permute-start | bytes 1572872 | tf_op jit(solution)/shard_map/ppermute | solution.py:350
  180.8 1.6 copy-start
  182.4 2.6 %copy-start.1 = (f32[2,8,128,128]{3,2,1,0:T(8,128)S(1)}, f32[2,8,128,128]{3,2,1,0:T(8,128)}, u32[]{:S(2)}) copy-start(f32[2,8,128,128]{3,2,1,0:T(8,128)} %get-tuple-element.54.more_ref) | copy-start | bytes 3145732
  187.7 2.4 %copy-start.2 = (f32[2,8,128,128]{3,2,1,0:T(8,128)S(1)}, f32[2,8,128,128]{3,2,1,0:T(8,128)}, u32[]{:S(2)}) copy-start(f32[2,8,128,128]{3,2,1,0:T(8,128)} %get-tuple-element.53.more_ref) | copy-start | bytes 3145732

commit v3 on v2

--- a/solution.py
+++ b/solution.py
@@ -354,41 +354,21 @@
     return lax.dynamic_index_in_dim(orbitals, plan[number * ENTRY + 4], 0, keepdims=False)
 
 
-def one_round(number, plan, orbitals, kernel, total, tables):
+def in_rounds(rounds, plan, received, orbitals, kernel, sends, tables):
     plus, plus_x, minus, minus_x = tables
-    u = to_partner(sent_orbital(number, plan, orbitals))
-    arrived = exchange(forward(number, 1, plan, u, orbitals, minus, plus))
-    arrived = exchange(solve(arrived, kernel, plus_x, minus_x))
-    own, back = inverse(number, 0, plan, arrived, u, orbitals, minus, plus)
-    total = add_into(number, 0, plan, total, own)
-    return add_into(number, 4, plan, total, to_partner(back)[None])
-
-
-def shards(orbitals, spin_channel):
-    count, planes, size, lanes = orbitals.shape
-    column_count = size // lax.axis_size("grid")
-    plan, sent = make_plan(spin_channel, orbitals)
-    us = [to_partner(sent)]
-    kernel = coulomb_block(size, column_count, lax.axis_index("grid") * column_count)
-    tables = tuple(two_parts(t) for t in fourier_tables(size, planes))
-    plus, plus_x, minus, minus_x = tables
-    total = lax.cond(
-        needs_more(spin_channel),
-        lambda *args: one_round(ROUNDS, *args, jnp.zeros_like(orbitals), tables),
-        lambda *args: jnp.zeros_like(orbitals),
-        plan, orbitals, kernel,
-    )
-    for number in range(1, ROUNDS):
-        sent, us[-1] = lax.optimization_barrier((sent_orbital(number, plan, orbitals), us[-1]))
+    us = [received]
+    for number in range(1, rounds):
+        sent, us[-1] = lax.optimization_barrier((sends[number - 1], us[-1]))
         us.append(to_partner(sent))
 
     def planes_of(number):
         return forward(number, 1 if number == 0 else 2, plan, us[number], orbitals, minus, plus)
 
+    total = jnp.zeros_like(orbitals)
     returned = []
     arrived = exchange(planes_of(0))
-    for number in range(ROUNDS):
-        ahead = planes_of(number + 1) if number + 1 < ROUNDS else None
+    for number in range(rounds):
+        ahead = planes_of(number + 1) if number + 1 < rounds else None
         leaving = solve(arrived, kernel, plus_x, minus_x, ahead)
         if number > 1:
             leaving, returned[number - 2] = lax.optimization_barrier((leaving, returned[number - 2]))
@@ -398,9 +378,26 @@
         total = add_into(number, 0, plan, total, own)
         if number > 0:
             total = add_into(number - 1, 4, plan, total, returned[number - 1][None])
-    place = plan[(ROUNDS - 1) * ENTRY + 4]
+    place = plan[(rounds - 1) * ENTRY + 4]
     last = lax.dynamic_index_in_dim(total, place, 0, keepdims=False) + returned[-1]
     return lax.dynamic_update_index_in_dim(total, last, place, 0)
+
+
+def shards(orbitals, spin_channel):
+    count, planes, size, lanes = orbitals.shape
+    column_count = size // lax.axis_size("grid")
+    plan, sent = make_plan(spin_channel, orbitals)
+    received = to_partner(sent)
+    sends = [sent_orbital(number, plan, orbitals) for number in range(1, ROUNDS + 1)]
+    kernel = coulomb_block(size, column_count, lax.axis_index("grid") * column_count)
+    tables = tuple(two_parts(t) for t in fourier_tables(size, planes))
+    more, kernel, sends = lax.optimization_barrier((needs_more(spin_channel), kernel, sends))
+    return lax.cond(
+        more,
+        lambda *args: in_rounds(ROUNDS + 1, *args, tables),
+        lambda *args: in_rounds(ROUNDS, *args, tables),
+        plan, received, orbitals, kernel, sends,
+    )
 
 
 def solution(mesh):

time: 212 us -> 212 us (level)
  waiting for transfers between devices: 96.4 us -> 90.2 us
  between operations: 4.41 us -> 6.59 us
    ppermute x6, waiting for transfers between devices: 48 us -> 42.7 us  [to_partner(): return lax.ppermute(value, 'band', pairs)]
where the time goes in v3:
time: 212 us; the launch traced here: 211 us
  waiting for transfers between devices  90.2 us (43%)
  Pallas kernels  52.1 us (25%)
  starting transfers between devices  51.5 us (24%)
  between operations  6.59 us (3%)
  local copies, waits for them, and re-layouts  5.21 us (2%)
  other arithmetic  2.87 us (1%)
    all_to_all x4, waiting for transfers between devices, exchange(): lax.all_to_all(field, 'grid', split_axis=0, concat_axis=0, tiled=True)  47.5 us
    ppermute x6, waiting for transfers between devices, to_partner(): return lax.ppermute(value, 'band', pairs)  42.7 us
    all_to_all x4, starting transfers between devices, exchange(): lax.all_to_all(field, 'grid', split_axis=0, concat_axis=0, tiled=True)  32.2 us
    ppermute x6, starting transfers between devices, to_partner(): return lax.ppermute(value, 'band', pairs)  19.4 us
    pallas_call x3, Pallas kernels, inverse(): pl.pallas_call(lambda *refs: inverse_kernel(number, *refs), grid_spec=plt...  13.4 us
    pallas_call x5, Pallas kernels, add_into(): pl.pallas_call(add_kernel, grid_spec=pltpu.PrefetchScalarGridSpec(num_sca...  12.7 us
    pallas_call x3, Pallas kernels, solve(): pl.pallas_call(solve_kernel, grid=(1,), in_specs=specs, out_specs=part(sh...  11.3 us
    pallas_call x3, Pallas kernels, forward(): pl.pallas_call(lambda *refs: forward_kernel(number, *refs), grid_spec=plt...  11.3 us
  transfers between devices with their start and end apart: 10, of which 10 were waited for; matrix products, arithmetic and copies ran while one was open for 3% of the time, Pallas kernels for 21%

profile of v3, /device:TPU:1, one launch (start us, length us, event | category | flops | bytes accessed | tf_op | source)
XLA Modules:
  0.0 210.6 jit_solution(9281679646739871772)
XLA Ops:
  0.0 0.0 copy-start.22
  0.0 0.0 copy-start.9
  0.0 3.3 %plan_rounds.1 = (s32[32]{0:T(128)S(1)}, f32[8,128,128]{2,1,0:T(8,128)}) custom-call(s32[128]{0:T(128)} %spin.1, s32[512,1,128]{2,1,0:T(1,128)} %constant.66.clone.table_ref, f32[4,8,128,128]{3,2,1,0:T(8,128)} %orbitals_ref.1), custom_call_target="tpu_custom_call" | custom-call | tf_op jit(solution)/shard_map/plan_rounds/pallas_call | solution.py:100
  3.4 0.0 copy-start.14
  3.4 5.9 %collective-permute-start.12 = (f32[8,128,128]{2,1,0:T(8,128)}, f32[8,128,128]{2,1,0:T(8,128)S(1)}, u32[]{:S(2)}, u32[]{:S(2)}) collective-permute-start(f32[8,128,128]{2,1,0:T(8,128)} %get-tuple-element.108), channel_id=1, source_target_pairs={{0,64},{16,80},{32,96},{48,112},{64,0},{80,16},{96,32},{112,48},{1... | collective-permute-start | bytes 1572872 | tf_op jit(solution)/shard_map/ppermute | solution.py:350
  9.2 0.7 fusion.6
  13.8 0.0 copy-done.22
  13.8 0.1 reshape.64
  13.9 0.2 reduce_sum.9
  14.1 0.7 or_reduce_fusion
  16.8 0.0 copy-done.9
  16.8 1.2 dynamic-slice_bitcast_fusion
  18.0 0.1 broadcast_add_fusion
  18.0 1.0 fusion.3
  19.8 11.9 %collective-permute-done.12 = f32[8,128,128]{2,1,0:T(8,128)S(1)} collective-permute-done((f32[8,128,128]{2,1,0:T(8,128)}, f32[8,128,128]{2,1,0:T(8,128)S(1)}, u32[]{:S(2)}, u32[]{:S(2)}) %collective-permute-start.12) | collective-permute-done | bytes 524320 | tf_op jit(solution)/shard_map/ppermute | solution.py:350
  31.6 0.0 copy-done.14
  31.6 179.0 %conditional.1 = (f32[4,8,128,128]{3,2,1,0:T(8,128)}) conditional(s32[]{:T(128)} %convert_element_type.7, (f32[8,128,128]{2,1,0:T(8,128)}, f32[8,128,128]{2,1,0:T(8,128)S(1)}, s32[32]{0:T(128)S(1)}, f32[4,8,128,128]{3,2,1,0:T(8,128)S(1)}, bf16[2,256,256]{2,1,0:T(8,128)(2,1)}, /*index=5*/bf16[2,256,256]{2,1,0:T(8,128)(2,1)S(1)}, ...), branch_computations={%region_2.3_spmd, %region_3.4_spmd} | conditional | flops 300000116736 | bytes 691750784 | solution.py:395
  31.6 0.0 copy-start.19
  31.6 1.9 collective-permute-start
  33.6 3.8 %forward_planes.7 = f32[16,2,8,8,128]{4,3,2,1,0:T(8,128)} custom-call(s32[32]{0:T(128)S(1)} %get-tuple-element.50.refs_0_.plan, f32[8,128,128]{2,1,0:T(8,128)S(1)} %get-tuple-element.53.refs_1_.refs_2_, f32[4,8,128,128]{3,2,1,0:T(8,128)S(1)} %get-tuple-element.54.refs_2_.refs_3_.refs_4_, f32[4,8,128,128]{3,2,1,0:T(8,128)S(1)} %get-tuple-element.54.refs_2_.refs_3_.refs_4_, ...), custom_call_target="tpu_custom_call" | custom-call | tf_op jit(solution)/shard_map/cond/branch_0_fun/forward_planes/pallas_call | solution.py:245
  37.3 8.9 %all-to-all-start = ((f32[16,2,8,8,128]{4,3,2,1,0:T(8,128)}), f32[16,2,8,8,128]{4,3,2,1,0:T(8,128)}, u32[]{:S(2)}, u32[]{:S(2)}) async-start(f32[16,2,8,8,128]{4,3,2,1,0:T(8,128)} %forward_planes.7), calls=%async_computation | async-start | bytes 2097152 | tf_op jit(solution)/shard_map/cond/branch_0_fun/all_to_all | solution.py:345
  46.2 11.3 %collective-permute-done.refs_1_.refs_2_ = f32[8,128,128]{2,1,0:T(8,128)S(1)} collective-permute-done((f32[8,128,128]{2,1,0:T(8,128)}, f32[8,128,128]{2,1,0:T(8,128)S(1)}, u32[]{:S(2)}, u32[]{:S(2)}) %collective-permute-start) | collective-permute-done | bytes 524320 | tf_op jit(solution)/shard_map/cond/branch_0_fun/ppermute | solution.py:350
  57.5 0.0 copy-done.19
  57.5 1.9 collective-permute-start.1
  59.4 3.8 %forward_planes.8.rest_0_ = f32[16,4,8,8,128]{4,3,2,1,0:T(8,128)} custom-call(s32[32]{0:T(128)S(1)} %get-tuple-element.50.refs_0_.plan, f32[8,128,128]{2,1,0:T(8,128)S(1)} %collective-permute-done.refs_1_.refs_2_, f32[4,8,128,128]{3,2,1,0:T(8,128)S(1)} %get-tuple-element.54.refs_2_.refs_3_.refs_4_, ...), custom_call_target="tpu_custom_call" | custom-call | flops 99999997952 | bytes 200000000 | tf_op jit(solution)/shard_map/cond/branch_0_fun/forward_planes/pallas_call | solution.py:245
  63.2 0.3 all-to-all-done.in_ref
  63.5 3.8 %solve_columns.7 = f32[16,4,8,8,128]{4,3,2,1,0:T(8,128)} custom-call(f32[16,2,8,8,128]{4,3,2,1,0:T(8,128)} %all-to-all-done.in_ref, f32[8,128,128]{2,1,0:T(8,128)} %get-tuple-element.57.kernel_ref, bf16[2,256,256]{2,1,0:T(8,128)(2,1)} %get-tuple-element.58.left_ref, ...), custom_call_target="tpu_custom_call", output_to_operand_aliasing={{}: (4, {})} | custom-call | tf_op jit(solution)/shard_map/cond/branch_0_fun/solve_columns/pallas_call | solution.py:276
  67.3 10.0 %all-to-all-start.1 = ((f32[16,4,8,8,128]{4,3,2,1,0:T(8,128)}), f32[16,4,8,8,128]{4,3,2,1,0:T(8,128)}, u32[]{:S(2)}, u32[]{:S(2)}) async-start(f32[16,4,8,8,128]{4,3,2,1,0:T(8,128)} %solve_columns.7), calls=%async_computation.1 | async-start | bytes 4194304 | tf_op jit(solution)/shard_map/cond/branch_0_fun/all_to_all | solution.py:345
  77.3 7.4 %collective-permute-done.1.refs_1_.refs_2_ = f32[8,128,128]{2,1,0:T(8,128)S(1)} collective-permute-done((f32[8,128,128]{2,1,0:T(8,128)}, f32[8,128,128]{2,1,0:T(8,128)S(1)}, u32[]{:S(2)}, u32[]{:S(2)}) %collective-permute-start.1) | collective-permute-done | bytes 524320 | tf_op jit(solution)/shard_map/cond/branch_0_fun/ppermute | solution.py:350
  84.7 3.8 %forward_planes.9.rest_0_ = f32[16,4,8,8,128]{4,3,2,1,0:T(8,128)} custom-call(s32[32]{0:T(128)S(1)} %get-tuple-element.50.refs_0_.plan, f32[8,128,128]{2,1,0:T(8,128)S(1)} %collective-permute-done.1.refs_1_.refs_2_, f32[4,8,128,128]{3,2,1,0:T(8,128)S(1)} %get-tuple-element.54.refs_2_.refs_3_.refs_4_, ...), custom_call_target="tpu_custom_call" | custom-call | flops 99999997952 | bytes 200000000 | tf_op jit(solution)/shard_map/cond/branch_0_fun/forward_planes/pallas_call | solution.py:245
  88.5 17.3 %all-to-all-done.1.in_ref.refs_1_ = f32[16,4,8,8,128]{4,3,2,1,0:T(8,128)} async-done(((f32[16,4,8,8,128]{4,3,2,1,0:T(8,128)}), f32[16,4,8,8,128]{4,3,2,1,0:T(8,128)}, u32[]{:S(2)}, u32[]{:S(2)}) %all-to-all-start.1) | async-done | bytes 2097184 | tf_op jit(solution)/shard_map/cond/branch_0_fun/all_to_all | solution.py:345
  105.8 3.8 %solve_columns.8 = f32[16,4,8,8,128]{4,3,2,1,0:T(8,128)} custom-call(f32[16,4,8,8,128]{4,3,2,1,0:T(8,128)} %all-to-all-done.1.in_ref.refs_1_, f32[8,128,128]{2,1,0:T(8,128)} %get-tuple-element.57.kernel_ref, bf16[2,256,256]{2,1,0:T(8,128)(2,1)} %get-tuple-element.58.left_ref, ...), custom_call_target="tpu_custom_call", output_to_operand_aliasing={{}: (4, {})} | custom-call | tf_op jit(solution)/shard_map/cond/branch_0_fun/solve_columns/pallas_call | solution.py:276
  109.7 5.7 %all-to-all-start.2 = ((f32[16,4,8,8,128]{4,3,2,1,0:T(8,128)}), f32[16,4,8,8,128]{4,3,2,1,0:T(8,128)}, u32[]{:S(2)}, u32[]{:S(2)}) async-start(f32[16,4,8,8,128]{4,3,2,1,0:T(8,128)} %solve_columns.8), calls=%async_computation.2 | async-start | bytes 4194304 | tf_op jit(solution)/shard_map/cond/branch_0_fun/all_to_all | solution.py:345
  115.3 0.0 copy-done.10
  115.3 4.4 %inverse_planes.8 = (f32[2,8,128,128]{3,2,1,0:T(8,128)}, f32[8,128,128]{2,1,0:T(8,128)}) custom-call(s32[32]{0:T(128)S(1)} %get-tuple-element.50.refs_0_.plan, f32[16,4,8,8,128]{4,3,2,1,0:T(8,128)} %all-to-all-done.1.in_ref.refs_1_, f32[8,128,128]{2,1,0:T(8,128)} %copy-done.19, f32[4,8,128,128]{3,2,1,0:T(8,128)S(1)} %get-tuple-element.54.refs_2_.refs_3_.refs_4_, ...), custom_call_target="tpu_custom_call" | custom-call | tf_op jit(solution)/shard_map/cond/branch_0_fun/inverse_planes/pallas_call | solution.py:290
  119.7 4.5 %collective-permute-start.3 = (f32[8,128,128]{2,1,0:T(8,128)}, f32[8,128,128]{2,1,0:T(8,128)S(1)}, u32[]{:S(2)}, u32[]{:S(2)}) collective-permute-start(f32[8,128,128]{2,1,0:T(8,128)} %get-tuple-element.65), channel_id=1, source_target_pairs={{0,64},{16,80},{32,96},{48,112},{64,0},{80,16},{96,32},{112,48},{1... | collective-permute-start | bytes 1572872 | tf_op jit(solution)/shard_map/cond/branch_0_fun/ppermute | solution.py:350
  124.3 19.6 %all-to-all-done.2.refs_1_.in_ref = f32[16,4,8,8,128]{4,3,2,1,0:T(8,128)} async-done(((f32[16,4,8,8,128]{4,3,2,1,0:T(8,128)}), f32[16,4,8,8,128]{4,3,2,1,0:T(8,128)}, u32[]{:S(2)}, u32[]{:S(2)}) %all-to-all-start.2) | async-done | bytes 2097184 | tf_op jit(solution)/shard_map/cond/branch_0_fun/all_to_all | solution.py:345
  143.9 3.8 %solve_columns.9 = f32[16,2,8,8,128]{4,3,2,1,0:T(8,128)} custom-call(f32[16,4,8,8,128]{4,3,2,1,0:T(8,128)} %all-to-all-done.2.refs_1_.in_ref, f32[8,128,128]{2,1,0:T(8,128)} %get-tuple-element.57.kernel_ref, bf16[2,256,256]{2,1,0:T(8,128)(2,1)} %get-tuple-element.58.left_ref, bf16[2,256,256]{2,1,0:T(8,128)(2,1)} %get-tuple-element.59.right_ref), custom_call_target="tpu_custom_call" | custom-call | tf_op jit(solution)/shard_map/cond/branch_0_fun/solve_columns/pallas_call | solution.py:276
  147.6 0.0 copy-start.15
  147.6 0.2 collective-permute-done.3
  147.9 7.6 %all-to-all-start.3 = ((f32[16,2,8,8,128]{4,3,2,1,0:T(8,128)}), f32[16,2,8,8,128]{4,3,2,1,0:T(8,128)}, u32[]{:S(2)}, u32[]{:S(2)}) async-start(f32[16,2,8,8,128]{4,3,2,1,0:T(8,128)} %solve_columns.9), calls=%async_computation.3 | async-start | bytes 2097152 | tf_op jit(solution)/shard_map/cond/branch_0_fun/all_to_all | solution.py:345
  155.5 0.0 copy-done.15
  155.5 4.5 %inverse_planes.7 = (f32[2,8,128,128]{3,2,1,0:T(8,128)}, f32[8,128,128]{2,1,0:T(8,128)}) custom-call(s32[32]{0:T(128)S(1)} %get-tuple-element.50.refs_0_.plan, f32[16,4,8,8,128]{4,3,2,1,0:T(8,128)} %all-to-all-done.2.refs_1_.in_ref, f32[8,128,128]{2,1,0:T(8,128)S(1)} %collective-permute-done.refs_1_.refs_2_, f32[4,8,128,128]{3,2,1,0:T(8,128)} %copy-done.10, ...), custom_call_target="tpu_custom_call" | custom-call | tf_op jit(solution)/shard_map/cond/branch_0_fun/inverse_planes/pallas_call | solution.py:290
  160.0 2.5 %collective-permute-start.2 = (f32[8,128,128]{2,1,0:T(8,128)}, f32[8,128,128]{2,1,0:T(8,128)S(1)}, u32[]{:S(2)}, u32[]{:S(2)}) collective-permute-start(f32[8,128,128]{2,1,0:T(8,128)} %get-tuple-element.64), channel_id=1, source_target_pairs={{0,64},{16,80},{32,96},{48,112},{64,0},{80,16},{96,32},{112,48},{1... | collective-permute-start | bytes 1572872 | tf_op jit(solution)/shard_map/cond/branch_0_fun/ppermute | solution.py:350
  162.5 10.3 %all-to-all-done.3.refs_1_ = f32[16,2,8,8,128]{4,3,2,1,0:T(8,128)} async-done(((f32[16,2,8,8,128]{4,3,2,1,0:T(8,128)}), f32[16,2,8,8,128]{4,3,2,1,0:T(8,128)}, u32[]{:S(2)}, u32[]{:S(2)}) %all-to-all-start.3) | async-done | bytes 1048608 | tf_op jit(solution)/shard_map/cond/branch_0_fun/all_to_all | solution.py:345
  172.8 4.5 %inverse_planes.9 = (f32[2,8,128,128]{3,2,1,0:T(8,128)}, f32[8,128,128]{2,1,0:T(8,128)}) custom-call(s32[32]{0:T(128)S(1)} %get-tuple-element.50.refs_0_.plan, f32[16,2,8,8,128]{4,3,2,1,0:T(8,128)} %all-to-all-done.3.refs_1_, f32[8,128,128]{2,1,0:T(8,128)S(1)} %collective-permute-done.1.refs_1_.refs_2_, f32[4,8,128,128]{3,2,1,0:T(8,128)} %copy-done.10, ...), custom_call_target="tpu_custom_call" | custom-call | tf_op jit(solution)/shard_map/cond/branch_0_fun/inverse_planes/pallas_call | solution.py:290
  177.2 0.0 copy-start.2
  177.2 2.7 %collective-permute-start.4 = (f32[8,128,128]{2,1,0:T(8,128)}, f32[8,128,128]{2,1,0:T(8,128)S(1)}, u32[]{:S(2)}, u32[]{:S(2)}) collective-permute-start(f32[8,128,128]{2,1,0:T(8,128)} %get-tuple-element.70), channel_id=1, source_target_pairs={{0,64},{16,80},{32,96},{48,112},{64,0},{80,16},{96,32},{112,48},{1... | collective-permute-start | bytes 1572872 | tf_op jit(solution)/shard_map/cond/branch_0_fun/ppermute | solution.py:350
  179.9 0.6 slice.10
  182.4 1.6 broadcast_5_sum_ref.0.sum_ref
  184.0 0.0 copy-done.2
  184.0 0.0 copy-start.4
  184.0 2.6 %add_terms.12.sum_ref = f32[4,8,128,128]{3,2,1,0:T(8,128)} custom-call(s32[32]{0:T(128)S(1)} %get-tuple-element.50.refs_0_.plan, f32[2,8,128,128]{3,2,1,0:T(8,128)S(1)} %copy-done.2, f32[4,8,128,128]{3,2,1,0:T(8,128)} %broadcast_5_sum_ref.0.sum_ref), custom_call_target="tpu_custom_call", output_to_operand_aliasing={{}: (2, {})} | custom-call | tf_op jit(solution)/shard_map/cond/branch_0_fun/add_terms/pallas_call | solution.py:315
  186.6 0.0 copy-done.4
  186.6 2.6 %add_terms.13.sum_ref = f32[4,8,128,128]{3,2,1,0:T(8,128)} custom-call(s32[32]{0:T(128)S(1)} %get-tuple-element.50.refs_0_.plan, f32[2,8,128,128]{3,2,1,0:T(8,128)S(1)} %copy-done.4, f32[4,8,128,128]{3,2,1,0:T(8,128)} %add_terms.12.sum_ref), custom_call_target="tpu_custom_call", output_to_operand_aliasing={{}: (2, {})} | custom-call | tf_op jit(solution)/shard_map/cond/branch_0_fun/add_terms/pallas_call | solution.py:315
  189.2 0.0 copy-start.6
  189.2 2.4 %add_terms.14.sum_ref = f32[4,8,128,128]{3,2,1,0:T(8,128)} custom-call(s32[32]{0:T(128)S(1)} %get-tuple-element.50.refs_0_.plan, f32[1,8,128,128]{3,2,1,0:T(8,128)S(1)} %bitcast.30, f32[4,8,128,128]{3,2,1,0:T(8,128)} %add_terms.13.sum_ref), custom_call_target="tpu_custom_call", output_to_operand_aliasing={{}: (2, {})} | custom-call | tf_op jit(solution)/shard_map/cond/branch_0_fun/add_terms/pallas_call | solution.py:315
  191.7 0.0 copy-done.6
  191.7 2.6 %add_terms.15.sum_ref = f32[4,8,128,128]{3,2,1,0:T(8,128)} custom-call(s32[32]{0:T(128)S(1)} %get-tuple-element.50.refs_0_.plan, f32[2,8,128,128]{3,2,1,0:T(8,128)S(1)} %copy-done.6, f32[4,8,128,128]{3,2,1,0:T(8,128)} %add_terms.14.sum_ref), custom_call_target="tpu_custom_call", output_to_operand_aliasing={{}: (2, {})} | custom-call | tf_op jit(solution)/shard_map/cond/branch_0_fun/add_terms/pallas_call | solution.py:315
  194.3 4.2 %collective-permute-done.2 = f32[8,128,128]{2,1,0:T(8,128)S(1)} collective-permute-done((f32[8,128,128]{2,1,0:T(8,128)}, f32[8,128,128]{2,1,0:T(8,128)S(1)}, u32[]{:S(2)}, u32[]{:S(2)}) %collective-permute-start.2) | collective-permute-done | bytes 524320 | tf_op jit(solution)/shard_map/cond/branch_0_fun/ppermute | solution.py:350
  198.5 2.4 %add_terms.16 = f32[4,8,128,128]{3,2,1,0:T(8,128)} custom-call(s32[32]{0:T(128)S(1)} %get-tuple-element.50.refs_0_.plan, f32[1,8,128,128]{3,2,1,0:T(8,128)S(1)} %bitcast.32, f32[4,8,128,128]{3,2,1,0:T(8,128)} %add_terms.15.sum_ref), custom_call_target="tpu_custom_call", output_to_operand_aliasing={{}: (2, {})} | custom-call | tf_op jit(solution)/shard_map/cond/branch_0_fun/add_terms/pallas_call | solution.py:315
  200.9 1.1 constant_dynamic-slice_fusion
  202.0 7.7 %collective-permute-done.4 = f32[8,128,128]{2,1,0:T(8,128)S(1)} collective-permute-done((f32[8,128,128]{2,1,0:T(8,128)}, f32[8,128,128]{2,1,0:T(8,128)S(1)}, u32[]{:S(2)}, u32[]{:S(2)}) %collective-permute-start.4) | collective-permute-done | bytes 524320 | tf_op jit(solution)/shard_map/cond/branch_0_fun/ppermute | solution.py:350
  209.7 0.9 bitcast_dynamic-update-slice_fusion
  (3 shorter events, 0.0 us)
Async XLA Ops:
  0.0 13.8 %copy-start.22 = (s32[128]{0:T(128)S(1)}, s32[128]{0:T(128)}, u32[]{:S(2)}) copy-start(s32[128]{0:T(128)} %spin.1) | copy-start | bytes 1540
  0.0 16.8 %copy-start.9 = (f32[4,8,128,128]{3,2,1,0:T(8,128)S(1)}, f32[4,8,128,128]{3,2,1,0:T(8,128)}, u32[]{:S(2)}) copy-start(f32[4,8,128,128]{3,2,1,0:T(8,128)} %orbitals_ref.1) | copy-start | bytes 6291460
  3.4 28.3 %copy-start.14 = (bf16[2,256,256]{2,1,0:T(8,128)(2,1)S(1)}, bf16[2,256,256]{2,1,0:T(8,128)(2,1)}, u32[]{:S(2)}) copy-start(bf16[2,256,256]{2,1,0:T(8,128)(2,1)} %constant.67.clone) | copy-start | bytes 786436
  3.4 28.3 %collective-permute-start.12 = (f32[8,128,128]{2,1,0:T(8,128)}, f32[8,128,128]{2,1,0:T(8,128)S(1)}, u32[]{:S(2)}, u32[]{:S(2)}) collective-permute-start(f32[8,128,128]{2,1,0:T(8,128)} %get-tuple-element.108), channel_id=1, source_target_pairs={{0,64},{16,80},{32,96},{48,112},{64,0},{80,16},{96,32},{112,48},{1... | collective-permute-start | bytes 1572872 | tf_op jit(solution)/shard_map/ppermute | solution.py:350
  31.6 25.9 %copy-start.19 = (f32[8,128,128]{2,1,0:T(8,128)}, f32[8,128,128]{2,1,0:T(8,128)S(1)}, u32[]{:S(2)}) copy-start(f32[8,128,128]{2,1,0:T(8,128)S(1)} %get-tuple-element.53.refs_1_.refs_2_) | copy-start | bytes 1572868 | tf_op jit(solution)/shard_map/cond
  31.6 83.7 %copy-start.10 = (f32[4,8,128,128]{3,2,1,0:T(8,128)}, f32[4,8,128,128]{3,2,1,0:T(8,128)S(1)}, u32[]{:S(2)}) copy-start(f32[4,8,128,128]{3,2,1,0:T(8,128)S(1)} %get-tuple-element.54.refs_2_.refs_3_.refs_4_) | copy-start | bytes 6291460 | tf_op jit(solution)/shard_map/cond
  31.6 25.9 %collective-permute-start = (f32[8,128,128]{2,1,0:T(8,128)}, f32[8,128,128]{2,1,0:T(8,128)S(1)}, u32[]{:S(2)}, u32[]{:S(2)}) collective-permute-start(f32[8,128,128]{2,1,0:T(8,128)} %get-tuple-element.61), channel_id=1, source_target_pairs={{0,64},{16,80},{32,96},{48,112},{64,0},{80,16},{96,32},{112,48},{1... | collective-permute-start | bytes 1572872 | tf_op jit(solution)/shard_map/cond/branch_0_fun/ppermute | solution.py:350
  37.3 26.2 %all-to-all-start = ((f32[16,2,8,8,128]{4,3,2,1,0:T(8,128)}), f32[16,2,8,8,128]{4,3,2,1,0:T(8,128)}, u32[]{:S(2)}, u32[]{:S(2)}) async-start(f32[16,2,8,8,128]{4,3,2,1,0:T(8,128)} %forward_planes.7), calls=%async_computation | async-start | bytes 2097152 | tf_op jit(solution)/shard_map/cond/branch_0_fun/all_to_all | solution.py:345
  57.5 27.2 %collective-permute-start.1 = (f32[8,128,128]{2,1,0:T(8,128)}, f32[8,128,128]{2,1,0:T(8,128)S(1)}, u32[]{:S(2)}, u32[]{:S(2)}) collective-permute-start(f32[8,128,128]{2,1,0:T(8,128)} %get-tuple-element.63), channel_id=1, source_target_pairs={{0,64},{16,80},{32,96},{48,112},{64,0},{80,16},{96,32},{112,48},{1... | collective-permute-start | bytes 1572872 | tf_op jit(solution)/shard_map/cond/branch_0_fun/ppermute | solution.py:350
  67.3 38.6 %all-to-all-start.1 = ((f32[16,4,8,8,128]{4,3,2,1,0:T(8,128)}), f32[16,4,8,8,128]{4,3,2,1,0:T(8,128)}, u32[]{:S(2)}, u32[]{:S(2)}) async-start(f32[16,4,8,8,128]{4,3,2,1,0:T(8,128)} %solve_columns.7), calls=%async_computation.1 | async-start | bytes 4194304 | tf_op jit(solution)/shard_map/cond/branch_0_fun/all_to_all | solution.py:345
  109.7 34.2 %all-to-all-start.2 = ((f32[16,4,8,8,128]{4,3,2,1,0:T(8,128)}), f32[16,4,8,8,128]{4,3,2,1,0:T(8,128)}, u32[]{:S(2)}, u32[]{:S(2)}) async-start(f32[16,4,8,8,128]{4,3,2,1,0:T(8,128)} %solve_columns.8), calls=%async_computation.2 | async-start | bytes 4194304 | tf_op jit(solution)/shard_map/cond/branch_0_fun/all_to_all | solution.py:345
  119.7 28.1 %collective-permute-start.3 = (f32[8,128,128]{2,1,0:T(8,128)}, f32[8,128,128]{2,1,0:T(8,128)S(1)}, u32[]{:S(2)}, u32[]{:S(2)}) collective-permute-start(f32[8,128,128]{2,1,0:T(8,128)} %get-tuple-element.65), channel_id=1, source_target_pairs={{0,64},{16,80},{32,96},{48,112},{64,0},{80,16},{96,32},{112,48},{1... | collective-permute-start | bytes 1572872 | tf_op jit(solution)/shard_map/cond/branch_0_fun/ppermute | solution.py:350
  147.6 7.8 %copy-start.15 = (bf16[2,256,256]{2,1,0:T(8,128)(2,1)S(1)}, bf16[2,256,256]{2,1,0:T(8,128)(2,1)}, u32[]{:S(2)}) copy-start(bf16[2,256,256]{2,1,0:T(8,128)(2,1)} %get-tuple-element.55.refs_4_.refs_5_) | copy-start | bytes 786436 | tf_op jit(solution)/shard_map/cond
  147.9 24.9 %all-to-all-start.3 = ((f32[16,2,8,8,128]{4,3,2,1,0:T(8,128)}), f32[16,2,8,8,128]{4,3,2,1,0:T(8,128)}, u32[]{:S(2)}, u32[]{:S(2)}) async-start(f32[16,2,8,8,128]{4,3,2,1,0:T(8,128)} %solve_columns.9), calls=%async_computation.3 | async-start | bytes 2097152 | tf_op jit(solution)/shard_map/cond/branch_0_fun/all_to_all | solution.py:345
  160.0 38.5 %collective-permute-start.2 = (f32[8,128,128]{2,1,0:T(8,128)}, f32[8,128,128]{2,1,0:T(8,128)S(1)}, u32[]{:S(2)}, u32[]{:S(2)}) collective-permute-start(f32[8,128,128]{2,1,0:T(8,128)} %get-tuple-element.64), channel_id=1, source_target_pairs={{0,64},{16,80},{32,96},{48,112},{64,0},{80,16},{96,32},{112,48},{1... | collective-permute-start | bytes 1572872 | tf_op jit(solution)/shard_map/cond/branch_0_fun/ppermute | solution.py:350
  177.2 6.8 %copy-start.2 = (f32[2,8,128,128]{3,2,1,0:T(8,128)S(1)}, f32[2,8,128,128]{3,2,1,0:T(8,128)}, u32[]{:S(2)}) copy-start(f32[2,8,128,128]{3,2,1,0:T(8,128)} %get-tuple-element.69.more_ref) | copy-start | bytes 3145732 | tf_op jit(solution)/shard_map/cond
  177.2 32.5 %collective-permute-start.4 = (f32[8,128,128]{2,1,0:T(8,128)}, f32[8,128,128]{2,1,0:T(8,128)S(1)}, u32[]{:S(2)}, u32[]{:S(2)}) collective-permute-start(f32[8,128,128]{2,1,0:T(8,128)} %get-tuple-element.70), channel_id=1, source_target_pairs={{0,64},{16,80},{32,96},{48,112},{64,0},{80,16},{96,32},{112,48},{1... | collective-permute-start | bytes 1572872 | tf_op jit(solution)/shard_map/cond/branch_0_fun/ppermute | solution.py:350
  184.0 2.6 %copy-start.4 = (f32[2,8,128,128]{3,2,1,0:T(8,128)S(1)}, f32[2,8,128,128]{3,2,1,0:T(8,128)}, u32[]{:S(2)}) copy-start(f32[2,8,128,128]{3,2,1,0:T(8,128)} %get-tuple-element.68.more_ref) | copy-start | bytes 3145732 | tf_op jit(solution)/shard_map/cond
  189.2 2.4 %copy-start.6 = (f32[2,8,128,128]{3,2,1,0:T(8,128)S(1)}, f32[2,8,128,128]{3,2,1,0:T(8,128)}, u32[]{:S(2)}) copy-start(f32[2,8,128,128]{3,2,1,0:T(8,128)} %get-tuple-element.67.more_ref) | copy-start | bytes 3145732 | tf_op jit(solution)/shard_map/cond

commit v4 on v3

--- a/solution.py
+++ b/solution.py
@@ -214,6 +214,32 @@
             back_ref[x] = -(v0 * v_ref[0, x] + v1 * w_ref[0, x])
 
 
+def solve_and_inverse_kernel(
+    number, plan, in_ref, kernel_ref, left_x_ref, right_x_ref, u_ref, v_ref, w_ref, left_ref, right_ref,
+    out_ref, own_ref, back_ref,
+):
+    blocks, parts, planes, columns, lanes = in_ref.shape
+    rows = blocks * 2 * planes
+    each = 2 * planes
+    flat_in = in_ref.reshape(blocks * parts * planes * columns, lanes)
+    flat_out = out_ref.reshape(rows * columns, lanes)
+    for y in range(0, columns, 2):
+        halves = []
+        for k in range(2):
+            places = [block * parts * planes * columns + y + k for block in range(blocks)]
+            halves.append(
+                jnp.concatenate([flat_in[pl.ds(place, each, stride=columns), :] for place in places], axis=0)
+            )
+        weight = jnp.concatenate([kernel_ref[y], kernel_ref[y + 1]], axis=1)
+        spectrum = from_left(left_x_ref, jnp.concatenate(halves, axis=1))
+        solved = from_left(right_x_ref, spectrum * jnp.concatenate([weight, weight], axis=0))
+        for k in range(2):
+            flat_out[pl.ds(y + k, rows, stride=columns), :] = solved[:, k * lanes:(k + 1) * lanes]
+    inverse_kernel(
+        number, plan, in_ref.at[:, pl.ds(2, 2)], u_ref, v_ref, w_ref, left_ref, right_ref, own_ref, back_ref
+    )
+
+
 def add_kernel(plan, more_ref, sum_ref, total_ref):
     total_ref[...] = sum_ref[...] + more_ref[...]
 
@@ -308,6 +334,35 @@
     )(plan, in_hbm(arrived), u, orbitals, orbitals, left, right)
 
 
+def solve_and_inverse(number, plan, arrived, kernel, left_x, right_x, u, orbitals, left, right):
+    own = (2,) + u.shape
+    field = (arrived.shape[0], 2) + arrived.shape[2:]
+    return pl.pallas_call(
+        lambda *refs: solve_and_inverse_kernel(number, *refs),
+        grid_spec=pltpu.PrefetchScalarGridSpec(
+            num_scalar_prefetch=1,
+            grid=(1,),
+            in_specs=[
+                whole(arrived.shape),
+                whole(kernel.shape),
+                whole(left_x.shape),
+                whole(right_x.shape),
+                whole(u.shape),
+                orbital_block(orbitals.shape, number, 0),
+                orbital_block(orbitals.shape, number, 1),
+                whole(left.shape),
+                whole(right.shape),
+            ],
+            out_specs=[whole(field), whole(own), whole(u.shape)],
+        ),
+        out_shape=[
+            pltpu.HBM(field, jnp.float32), pltpu.HBM(own, jnp.float32), pltpu.HBM(u.shape, jnp.float32)
+        ],
+        compiler_params=params(),
+        name="solve_and_inverse",
+    )(plan, in_hbm(arrived), kernel, left_x, right_x, u, orbitals, orbitals, left, right)
+
+
 def add_into(number, field, plan, total, more):
     count = more.shape[0]
     one = (1,) + more.shape[1:]
@@ -365,17 +420,29 @@
         return forward(number, 1 if number == 0 else 2, plan, us[number], orbitals, minus, plus)
 
     total = jnp.zeros_like(orbitals)
-    returned = []
+    returned, owns = [], []
+
+    def give(own, back):
+        owns.append(own)
+        returned.append(to_partner(back))
+
     arrived = exchange(planes_of(0))
-    for number in range(rounds):
-        ahead = planes_of(number + 1) if number + 1 < rounds else None
-        leaving = solve(arrived, kernel, plus_x, minus_x, ahead)
+    for number in range(rounds - 1):
+        leaving = solve(arrived, kernel, plus_x, minus_x, planes_of(number + 1))
         if number > 1:
             leaving, returned[number - 2] = lax.optimization_barrier((leaving, returned[number - 2]))
         arrived = exchange(leaving)
-        own, back = inverse(number, 0 if ahead is None else 1, plan, arrived, us[number], orbitals, minus, plus)
-        returned.append(to_partner(back))
-        total = add_into(number, 0, plan, total, own)
+        if number < rounds - 2:
+            give(*inverse(number, 1, plan, arrived, us[number], orbitals, minus, plus))
+    leaving, own, back = solve_and_inverse(
+        rounds - 2, plan, arrived, kernel, plus_x, minus_x, us[rounds - 2], orbitals, minus, plus
+    )
+    leaving, returned[rounds - 3] = lax.optimization_barrier((leaving, returned[rounds - 3]))
+    arrived = exchange(leaving)
+    give(own, back)
+    give(*inverse(rounds - 1, 0, plan, arrived, us[rounds - 1], orbitals, minus, plus))
+    for number in range(rounds):
+        total = add_into(number, 0, plan, total, owns[number])
         if number > 0:
             total = add_into(number - 1, 4, plan, total, returned[number - 1][None])
     place = plan[(rounds - 1) * ENTRY + 4]

time: 212 us -> 208 us (0.981)
  waiting for transfers between devices: 90.2 us -> 85.5 us
  starting transfers between devices: 51.5 us -> 53.8 us
  Pallas kernels: 52.1 us -> 49.9 us
    ppermute x6, waiting for transfers between devices: 42.7 us -> 35.6 us  [to_partner(): return lax.ppermute(value, 'band', pairs)]
    pallas_call x0 -> x1, Pallas kernels: none -> 6.01 us  [solve_and_inverse(): pl.pallas_call(lambda *refs: solve_and_inverse_kernel(number, *refs), gri...]
    pallas_call x3 -> x2, Pallas kernels: 13.4 us -> 8.92 us  [inverse(): pl.pallas_call(lambda *refs: inverse_kernel(number, *refs), grid_spec=plt...]
    ppermute x6, starting transfers between devices: 19.4 us -> 23.4 us  [to_partner(): return lax.ppermute(value, 'band', pairs)]
    pallas_call x3 -> x2, Pallas kernels: 11.3 us -> 7.58 us  [solve(): pl.pallas_call(solve_kernel, grid=(1,), in_specs=specs, out_specs=part(sh...]
    all_to_all x4, waiting for transfers between devices: 47.5 us -> 49.9 us  [exchange(): lax.all_to_all(field, 'grid', split_axis=0, concat_axis=0, tiled=True)]
  transfers between devices with their start and end apart: 10 -> 10, of which waited for: 10 -> 8; matrix products, arithmetic and copies ran while one was open for 3% -> 3% of each run, Pallas kernels for 21% -> 21%
where the time goes in v4:
time: 208 us; the launch traced here: 207 us
  waiting for transfers between devices  85.5 us (41%)
  starting transfers between devices  53.8 us (26%)
  Pallas kernels  49.9 us (24%)
  between operations  6.53 us (3%)
  local copies, waits for them, and re-layouts  6.19 us (3%)
  other arithmetic  2.86 us (1%)
    all_to_all x4, waiting for transfers between devices, exchange(): lax.all_to_all(field, 'grid', split_axis=0, concat_axis=0, tiled=True)  49.9 us
    ppermute x6, waiting for transfers between devices, to_partner(): return lax.ppermute(value, 'band', pairs)  35.6 us
    all_to_all x4, starting transfers between devices, exchange(): lax.all_to_all(field, 'grid', split_axis=0, concat_axis=0, tiled=True)  30.4 us
    ppermute x6, starting transfers between devices, to_partner(): return lax.ppermute(value, 'band', pairs)  23.4 us
    pallas_call x5, Pallas kernels, add_into(): pl.pallas_call(add_kernel, grid_spec=pltpu.PrefetchScalarGridSpec(num_sca...  12.7 us
    pallas_call x3, Pallas kernels, forward(): pl.pallas_call(lambda *refs: forward_kernel(number, *refs), grid_spec=plt...  11.4 us
    pallas_call x2, Pallas kernels, inverse(): pl.pallas_call(lambda *refs: inverse_kernel(number, *refs), grid_spec=plt...  8.92 us
    pallas_call x2, Pallas kernels, solve(): pl.pallas_call(solve_kernel, grid=(1,), in_specs=specs, out_specs=part(sh...  7.58 us
  transfers between devices with their start and end apart: 10, of which 8 were waited for; matrix products, arithmetic and copies ran while one was open for 3% of the time, Pallas kernels for 21%

profile of v4, /device:TPU:1, one launch (start us, length us, event | category | flops | bytes accessed | tf_op | source)
XLA Modules:
  0.0 206.8 jit_solution(10626036516677411975)
XLA Ops:
  0.0 0.0 copy-start.23
  0.0 0.0 copy-start.9
  0.0 3.3 %plan_rounds.1 = (s32[32]{0:T(128)S(1)}, f32[8,128,128]{2,1,0:T(8,128)}) custom-call(s32[128]{0:T(128)} %spin.1, s32[512,1,128]{2,1,0:T(1,128)} %constant.66.clone.table_ref, f32[4,8,128,128]{3,2,1,0:T(8,128)} %orbitals_ref.1), custom_call_target="tpu_custom_call" | custom-call | tf_op jit(solution)/shard_map/plan_rounds/pallas_call | solution.py:100
  3.4 0.0 copy-start.14
  3.4 5.9 %collective-permute-start.12 = (f32[8,128,128]{2,1,0:T(8,128)}, f32[8,128,128]{2,1,0:T(8,128)S(1)}, u32[]{:S(2)}, u32[]{:S(2)}) collective-permute-start(f32[8,128,128]{2,1,0:T(8,128)} %get-tuple-element.113), channel_id=1, source_target_pairs={{0,64},{16,80},{32,96},{48,112},{64,0},{80,16},{96,32},{112,48},{1... | collective-permute-start | bytes 1572872 | tf_op jit(solution)/shard_map/ppermute | solution.py:405
  9.2 0.0 copy-done.23
  9.2 0.1 reshape.64
  9.4 0.7 fusion.6
  13.9 0.1 reduce_sum.9
  14.1 0.7 or_reduce_fusion
  16.7 0.0 copy-done.9
  16.7 1.2 dynamic-slice_bitcast_fusion
  17.9 0.1 broadcast_add_fusion
  18.0 1.0 fusion.3
  19.7 11.9 %collective-permute-done.12 = f32[8,128,128]{2,1,0:T(8,128)S(1)} collective-permute-done((f32[8,128,128]{2,1,0:T(8,128)}, f32[8,128,128]{2,1,0:T(8,128)S(1)}, u32[]{:S(2)}, u32[]{:S(2)}) %collective-permute-start.12) | collective-permute-done | bytes 524320 | tf_op jit(solution)/shard_map/ppermute | solution.py:405
  31.6 0.0 copy-done.14
  31.6 175.2 %conditional.1 = (f32[4,8,128,128]{3,2,1,0:T(8,128)}) conditional(s32[]{:T(128)} %convert_element_type.7, (f32[8,128,128]{2,1,0:T(8,128)}, f32[8,128,128]{2,1,0:T(8,128)S(1)}, s32[32]{0:T(128)S(1)}, f32[4,8,128,128]{3,2,1,0:T(8,128)S(1)}, bf16[2,256,256]{2,1,0:T(8,128)(2,1)S(1)}, /*index=5*/bf16[2,256,256]{2,1,0:T(8,128)(2,1)}, ...), branch_computations={%region_2.3_spmd, %region_3.4_spmd} | conditional | flops 300000116736 | bytes 691750784 | solution.py:462
  31.6 0.0 copy-start.19
  31.6 0.0 copy-start.10
  31.6 1.9 collective-permute-start
  33.6 3.8 %forward_planes.7 = f32[16,2,8,8,128]{4,3,2,1,0:T(8,128)} custom-call(s32[32]{0:T(128)S(1)} %get-tuple-element.50.refs_0_.plan, f32[8,128,128]{2,1,0:T(8,128)S(1)} %get-tuple-element.53.refs_1_.refs_2_, f32[4,8,128,128]{3,2,1,0:T(8,128)S(1)} %get-tuple-element.54.refs_2_.refs_3_.refs_6_.refs_7_.refs_4_, ...), custom_call_target="tpu_custom_call" | custom-call | tf_op jit(solution)/shard_map/cond/branch_0_fun/forward_planes/pallas_call | solution.py:271
  37.3 8.9 %all-to-all-start = ((f32[16,2,8,8,128]{4,3,2,1,0:T(8,128)}), f32[16,2,8,8,128]{4,3,2,1,0:T(8,128)}, u32[]{:S(2)}, u32[]{:S(2)}) async-start(f32[16,2,8,8,128]{4,3,2,1,0:T(8,128)} %forward_planes.7), calls=%async_computation | async-start | bytes 2097152 | tf_op jit(solution)/shard_map/cond/branch_0_fun/all_to_all | solution.py:400
  46.2 11.3 %collective-permute-done.refs_1_.refs_5_ = f32[8,128,128]{2,1,0:T(8,128)S(1)} collective-permute-done((f32[8,128,128]{2,1,0:T(8,128)}, f32[8,128,128]{2,1,0:T(8,128)S(1)}, u32[]{:S(2)}, u32[]{:S(2)}) %collective-permute-start) | collective-permute-done | bytes 524320 | tf_op jit(solution)/shard_map/cond/branch_0_fun/ppermute | solution.py:405
  57.5 0.0 copy-done.19
  57.5 1.9 collective-permute-start.1
  59.4 3.8 %forward_planes.8.rest_0_ = f32[16,4,8,8,128]{4,3,2,1,0:T(8,128)} custom-call(s32[32]{0:T(128)S(1)} %get-tuple-element.50.refs_0_.plan, f32[8,128,128]{2,1,0:T(8,128)S(1)} %collective-permute-done.refs_1_.refs_5_, f32[4,8,128,128]{3,2,1,0:T(8,128)S(1)} %get-tuple-element.54.refs_2_.refs_3_.refs_6_.refs_7_.refs_4_, ...), custom_call_target="tpu_custom_call" | custom-call | flops 99999997952 | bytes 200000000 | tf_op jit(solution)/shard_map/cond/branch_0_fun/forward_planes/pallas_call | solution.py:271
  63.2 0.3 all-to-all-done.in_ref
  63.5 3.8 %solve_columns.5 = f32[16,4,8,8,128]{4,3,2,1,0:T(8,128)} custom-call(f32[16,2,8,8,128]{4,3,2,1,0:T(8,128)} %all-to-all-done.in_ref, f32[8,128,128]{2,1,0:T(8,128)} %get-tuple-element.57.kernel_ref.refs_2_, bf16[2,256,256]{2,1,0:T(8,128)(2,1)} %get-tuple-element.58.left_ref.refs_3_, ...), custom_call_target="tpu_custom_call", output_to_operand_aliasing={{}: (4, {})} | custom-call | tf_op jit(solution)/shard_map/cond/branch_0_fun/solve_columns/pallas_call | solution.py:302
  67.3 10.0 %all-to-all-start.1 = ((f32[16,4,8,8,128]{4,3,2,1,0:T(8,128)}), f32[16,4,8,8,128]{4,3,2,1,0:T(8,128)}, u32[]{:S(2)}, u32[]{:S(2)}) async-start(f32[16,4,8,8,128]{4,3,2,1,0:T(8,128)} %solve_columns.5), calls=%async_computation.1 | async-start | bytes 4194304 | tf_op jit(solution)/shard_map/cond/branch_0_fun/all_to_all | solution.py:400
  77.3 7.4 %collective-permute-done.1.refs_1_.refs_2_ = f32[8,128,128]{2,1,0:T(8,128)S(1)} collective-permute-done((f32[8,128,128]{2,1,0:T(8,128)}, f32[8,128,128]{2,1,0:T(8,128)S(1)}, u32[]{:S(2)}, u32[]{:S(2)}) %collective-permute-start.1) | collective-permute-done | bytes 524320 | tf_op jit(solution)/shard_map/cond/branch_0_fun/ppermute | solution.py:405
  84.7 3.8 %forward_planes.9.rest_0_ = f32[16,4,8,8,128]{4,3,2,1,0:T(8,128)} custom-call(s32[32]{0:T(128)S(1)} %get-tuple-element.50.refs_0_.plan, f32[8,128,128]{2,1,0:T(8,128)S(1)} %collective-permute-done.1.refs_1_.refs_2_, f32[4,8,128,128]{3,2,1,0:T(8,128)S(1)} %get-tuple-element.54.refs_2_.refs_3_.refs_6_.refs_7_.refs_4_, ...), custom_call_target="tpu_custom_call" | custom-call | flops 99999997952 | bytes 200000000 | tf_op jit(solution)/shard_map/cond/branch_0_fun/forward_planes/pallas_call | solution.py:271
  88.5 17.3 %all-to-all-done.1.in_ref.refs_1_ = f32[16,4,8,8,128]{4,3,2,1,0:T(8,128)} async-done(((f32[16,4,8,8,128]{4,3,2,1,0:T(8,128)}), f32[16,4,8,8,128]{4,3,2,1,0:T(8,128)}, u32[]{:S(2)}, u32[]{:S(2)}) %all-to-all-start.1) | async-done | bytes 2097184 | tf_op jit(solution)/shard_map/cond/branch_0_fun/all_to_all | solution.py:400
  105.8 3.8 %solve_columns.6 = f32[16,4,8,8,128]{4,3,2,1,0:T(8,128)} custom-call(f32[16,4,8,8,128]{4,3,2,1,0:T(8,128)} %all-to-all-done.1.in_ref.refs_1_, f32[8,128,128]{2,1,0:T(8,128)} %get-tuple-element.57.kernel_ref.refs_2_, bf16[2,256,256]{2,1,0:T(8,128)(2,1)} %get-tuple-element.58.left_ref.refs_3_, ...), custom_call_target="tpu_custom_call", output_to_operand_aliasing={{}: (4, {})} | custom-call | tf_op jit(solution)/shard_map/cond/branch_0_fun/solve_columns/pallas_call | solution.py:302
  109.7 5.7 %all-to-all-start.2 = ((f32[16,4,8,8,128]{4,3,2,1,0:T(8,128)}), f32[16,4,8,8,128]{4,3,2,1,0:T(8,128)}, u32[]{:S(2)}, u32[]{:S(2)}) async-start(f32[16,4,8,8,128]{4,3,2,1,0:T(8,128)} %solve_columns.6), calls=%async_computation.2 | async-start | bytes 4194304 | tf_op jit(solution)/shard_map/cond/branch_0_fun/all_to_all | solution.py:400
  115.3 0.0 copy-done.10
  115.3 4.4 %inverse_planes.5 = (f32[2,8,128,128]{3,2,1,0:T(8,128)}, f32[8,128,128]{2,1,0:T(8,128)}) custom-call(s32[32]{0:T(128)S(1)} %get-tuple-element.50.refs_0_.plan, f32[16,4,8,8,128]{4,3,2,1,0:T(8,128)} %all-to-all-done.1.in_ref.refs_1_, f32[8,128,128]{2,1,0:T(8,128)} %copy-done.19, ...), custom_call_target="tpu_custom_call" | custom-call | tf_op jit(solution)/shard_map/cond/branch_0_fun/inverse_planes/pallas_call | solution.py:316
  119.8 4.5 %collective-permute-start.3 = (f32[8,128,128]{2,1,0:T(8,128)}, f32[8,128,128]{2,1,0:T(8,128)S(1)}, u32[]{:S(2)}, u32[]{:S(2)}) collective-permute-start(f32[8,128,128]{2,1,0:T(8,128)} %get-tuple-element.66), channel_id=1, source_target_pairs={{0,64},{16,80},{32,96},{48,112},{64,0},{80,16},{96,32},{112,48},{1... | collective-permute-start | bytes 1572872 | tf_op jit(solution)/shard_map/cond/branch_0_fun/ppermute | solution.py:405
  124.3 19.6 %all-to-all-done.2.refs_1_ = f32[16,4,8,8,128]{4,3,2,1,0:T(8,128)} async-done(((f32[16,4,8,8,128]{4,3,2,1,0:T(8,128)}), f32[16,4,8,8,128]{4,3,2,1,0:T(8,128)}, u32[]{:S(2)}, u32[]{:S(2)}) %all-to-all-start.2) | async-done | bytes 2097184 | tf_op jit(solution)/shard_map/cond/branch_0_fun/all_to_all | solution.py:400
  143.9 6.0 %solve_and_inverse.2 = (f32[16,2,8,8,128]{4,3,2,1,0:T(8,128)}, f32[2,8,128,128]{3,2,1,0:T(8,128)}, f32[8,128,128]{2,1,0:T(8,128)}) custom-call(s32[32]{0:T(128)S(1)} %get-tuple-element.50.refs_0_.plan, f32[16,4,8,8,128]{4,3,2,1,0:T(8,128)} %all-to-all-done.2.refs_1_, f32[8,128,128]{2,1,0:T(8,128)} %get-tuple-element.57.kernel_ref.refs_2_, ...), custom_call_target="tpu_custom_call" | custom-call | tf_op jit(solution)/shard_map/cond/branch_0_fun/solve_and_inverse/pallas_call | solution.py:340
  149.9 0.0 copy-start.15
  149.9 0.0 collective-permute-done.3
  149.9 5.8 %all-to-all-start.3 = ((f32[16,2,8,8,128]{4,3,2,1,0:T(8,128)}), f32[16,2,8,8,128]{4,3,2,1,0:T(8,128)S(1)}, u32[]{:S(2)}, u32[]{:S(2)}) async-start(f32[16,2,8,8,128]{4,3,2,1,0:T(8,128)} %get-tuple-element.67), calls=%async_computation.3 | async-start | bytes 2097152 | tf_op jit(solution)/shard_map/cond/branch_0_fun/all_to_all | solution.py:400
  155.7 4.6 %collective-permute-start.2 = (f32[8,128,128]{2,1,0:T(8,128)}, f32[8,128,128]{2,1,0:T(8,128)S(1)}, u32[]{:S(2)}, u32[]{:S(2)}) collective-permute-start(f32[8,128,128]{2,1,0:T(8,128)} %get-tuple-element.64), channel_id=1, source_target_pairs={{0,64},{16,80},{32,96},{48,112},{64,0},{80,16},{96,32},{112,48},{1... | collective-permute-start | bytes 1572872 | tf_op jit(solution)/shard_map/cond/branch_0_fun/ppermute | solution.py:405
  160.3 12.6 %all-to-all-done.3.refs_1_ = f32[16,2,8,8,128]{4,3,2,1,0:T(8,128)S(1)} async-done(((f32[16,2,8,8,128]{4,3,2,1,0:T(8,128)}), f32[16,2,8,8,128]{4,3,2,1,0:T(8,128)S(1)}, u32[]{:S(2)}, u32[]{:S(2)}) %all-to-all-start.3) | async-done | bytes 1048608 | tf_op jit(solution)/shard_map/cond/branch_0_fun/all_to_all | solution.py:400
  172.9 0.0 copy-start.22
  172.9 1.0 copy-done.22
  173.9 0.0 copy-done.15
  173.9 4.5 %inverse_planes.6 = (f32[2,8,128,128]{3,2,1,0:T(8,128)}, f32[8,128,128]{2,1,0:T(8,128)}) custom-call(s32[32]{0:T(128)S(1)} %get-tuple-element.50.refs_0_.plan, f32[16,2,8,8,128]{4,3,2,1,0:T(8,128)} %copy-done.22, f32[8,128,128]{2,1,0:T(8,128)S(1)} %collective-permute-done.1.refs_1_.refs_2_, f32[4,8,128,128]{3,2,1,0:T(8,128)} %copy-done.10, ...), custom_call_target="tpu_custom_call" | custom-call | tf_op jit(solution)/shard_map/cond/branch_0_fun/inverse_planes/pallas_call | solution.py:316
  178.4 0.0 copy-start.2
  178.4 4.7 %collective-permute-start.4 = (f32[8,128,128]{2,1,0:T(8,128)}, f32[8,128,128]{2,1,0:T(8,128)S(1)}, u32[]{:S(2)}, u32[]{:S(2)}) collective-permute-start(f32[8,128,128]{2,1,0:T(8,128)} %get-tuple-element.72), channel_id=1, source_target_pairs={{0,64},{16,80},{32,96},{48,112},{64,0},{80,16},{96,32},{112,48},{1... | collective-permute-start | bytes 1572872 | tf_op jit(solution)/shard_map/cond/branch_0_fun/ppermute | solution.py:405
  183.0 0.6 slice.10
  185.6 1.6 broadcast_5_sum_ref.0.sum_ref
  187.1 0.0 copy-done.2
  187.1 2.6 %add_terms.12.sum_ref = f32[4,8,128,128]{3,2,1,0:T(8,128)} custom-call(s32[32]{0:T(128)S(1)} %get-tuple-element.50.refs_0_.plan, f32[2,8,128,128]{3,2,1,0:T(8,128)S(1)} %copy-done.2, f32[4,8,128,128]{3,2,1,0:T(8,128)} %broadcast_5_sum_ref.0.sum_ref), custom_call_target="tpu_custom_call", output_to_operand_aliasing={{}: (2, {})} | custom-call | tf_op jit(solution)/shard_map/cond/branch_0_fun/add_terms/pallas_call | solution.py:370
  189.8 0.0 copy-done.4
  189.8 2.6 %add_terms.13.sum_ref = f32[4,8,128,128]{3,2,1,0:T(8,128)} custom-call(s32[32]{0:T(128)S(1)} %get-tuple-element.50.refs_0_.plan, f32[2,8,128,128]{3,2,1,0:T(8,128)S(1)} %copy-done.4, f32[4,8,128,128]{3,2,1,0:T(8,128)} %add_terms.12.sum_ref), custom_call_target="tpu_custom_call", output_to_operand_aliasing={{}: (2, {})} | custom-call | tf_op jit(solution)/shard_map/cond/branch_0_fun/add_terms/pallas_call | solution.py:370
  192.4 2.4 %add_terms.14.sum_ref = f32[4,8,128,128]{3,2,1,0:T(8,128)} custom-call(s32[32]{0:T(128)S(1)} %get-tuple-element.50.refs_0_.plan, f32[1,8,128,128]{3,2,1,0:T(8,128)S(1)} %bitcast.30, f32[4,8,128,128]{3,2,1,0:T(8,128)} %add_terms.13.sum_ref), custom_call_target="tpu_custom_call", output_to_operand_aliasing={{}: (2, {})} | custom-call | tf_op jit(solution)/shard_map/cond/branch_0_fun/add_terms/pallas_call | solution.py:370
  194.8 0.0 copy-done.6
  194.8 2.6 %add_terms.15.sum_ref = f32[4,8,128,128]{3,2,1,0:T(8,128)} custom-call(s32[32]{0:T(128)S(1)} %get-tuple-element.50.refs_0_.plan, f32[2,8,128,128]{3,2,1,0:T(8,128)S(1)} %copy-done.6, f32[4,8,128,128]{3,2,1,0:T(8,128)} %add_terms.14.sum_ref), custom_call_target="tpu_custom_call", output_to_operand_aliasing={{}: (2, {})} | custom-call | tf_op jit(solution)/shard_map/cond/branch_0_fun/add_terms/pallas_call | solution.py:370
  197.4 0.0 collective-permute-done.2
  197.4 2.4 %add_terms.16 = f32[4,8,128,128]{3,2,1,0:T(8,128)} custom-call(s32[32]{0:T(128)S(1)} %get-tuple-element.50.refs_0_.plan, f32[1,8,128,128]{3,2,1,0:T(8,128)S(1)} %bitcast.32, f32[4,8,128,128]{3,2,1,0:T(8,128)} %add_terms.15.sum_ref), custom_call_target="tpu_custom_call", output_to_operand_aliasing={{}: (2, {})} | custom-call | tf_op jit(solution)/shard_map/cond/branch_0_fun/add_terms/pallas_call | solution.py:370
  199.9 1.1 constant_dynamic-slice_fusion
  200.9 5.0 %collective-permute-done.4 = f32[8,128,128]{2,1,0:T(8,128)S(1)} collective-permute-done((f32[8,128,128]{2,1,0:T(8,128)}, f32[8,128,128]{2,1,0:T(8,128)S(1)}, u32[]{:S(2)}, u32[]{:S(2)}) %collective-permute-start.4) | collective-permute-done | bytes 524320 | tf_op jit(solution)/shard_map/cond/branch_0_fun/ppermute | solution.py:405
  205.9 0.9 bitcast_dynamic-update-slice_fusion
  (4 shorter events, 0.0 us)
Async XLA Ops:
  0.0 9.2 %copy-start.23 = (s32[128]{0:T(128)S(1)}, s32[128]{0:T(128)}, u32[]{:S(2)}) copy-start(s32[128]{0:T(128)} %spin.1) | copy-start | bytes 1540
  0.0 16.7 %copy-start.9 = (f32[4,8,128,128]{3,2,1,0:T(8,128)S(1)}, f32[4,8,128,128]{3,2,1,0:T(8,128)}, u32[]{:S(2)}) copy-start(f32[4,8,128,128]{3,2,1,0:T(8,128)} %orbitals_ref.1) | copy-start | bytes 6291460
  3.4 28.3 %copy-start.14 = (bf16[2,256,256]{2,1,0:T(8,128)(2,1)S(1)}, bf16[2,256,256]{2,1,0:T(8,128)(2,1)}, u32[]{:S(2)}) copy-start(bf16[2,256,256]{2,1,0:T(8,128)(2,1)} %constant.69.clone) | copy-start | bytes 786436
  3.4 28.3 %collective-permute-start.12 = (f32[8,128,128]{2,1,0:T(8,128)}, f32[8,128,128]{2,1,0:T(8,128)S(1)}, u32[]{:S(2)}, u32[]{:S(2)}) collective-permute-start(f32[8,128,128]{2,1,0:T(8,128)} %get-tuple-element.113), channel_id=1, source_target_pairs={{0,64},{16,80},{32,96},{48,112},{64,0},{80,16},{96,32},{112,48},{1... | collective-permute-start | bytes 1572872 | tf_op jit(solution)/shard_map/ppermute | solution.py:405
  31.6 25.9 %copy-start.19 = (f32[8,128,128]{2,1,0:T(8,128)}, f32[8,128,128]{2,1,0:T(8,128)S(1)}, u32[]{:S(2)}) copy-start(f32[8,128,128]{2,1,0:T(8,128)S(1)} %get-tuple-element.53.refs_1_.refs_2_) | copy-start | bytes 1572868 | tf_op jit(solution)/shard_map/cond
  31.6 83.7 %copy-start.10 = (f32[4,8,128,128]{3,2,1,0:T(8,128)}, f32[4,8,128,128]{3,2,1,0:T(8,128)S(1)}, u32[]{:S(2)}) copy-start(f32[4,8,128,128]{3,2,1,0:T(8,128)S(1)} %get-tuple-element.54.refs_2_.refs_3_.refs_6_.refs_7_.refs_4_) | copy-start | bytes 6291460 | tf_op jit(solution)/shard_map/cond
  31.6 25.9 %collective-permute-start = (f32[8,128,128]{2,1,0:T(8,128)}, f32[8,128,128]{2,1,0:T(8,128)S(1)}, u32[]{:S(2)}, u32[]{:S(2)}) collective-permute-start(f32[8,128,128]{2,1,0:T(8,128)} %get-tuple-element.61), channel_id=1, source_target_pairs={{0,64},{16,80},{32,96},{48,112},{64,0},{80,16},{96,32},{112,48},{1... | collective-permute-start | bytes 1572872 | tf_op jit(solution)/shard_map/cond/branch_0_fun/ppermute | solution.py:405
  37.3 26.2 %all-to-all-start = ((f32[16,2,8,8,128]{4,3,2,1,0:T(8,128)}), f32[16,2,8,8,128]{4,3,2,1,0:T(8,128)}, u32[]{:S(2)}, u32[]{:S(2)}) async-start(f32[16,2,8,8,128]{4,3,2,1,0:T(8,128)} %forward_planes.7), calls=%async_computation | async-start | bytes 2097152 | tf_op jit(solution)/shard_map/cond/branch_0_fun/all_to_all | solution.py:400
  57.5 27.2 %collective-permute-start.1 = (f32[8,128,128]{2,1,0:T(8,128)}, f32[8,128,128]{2,1,0:T(8,128)S(1)}, u32[]{:S(2)}, u32[]{:S(2)}) collective-permute-start(f32[8,128,128]{2,1,0:T(8,128)} %get-tuple-element.63), channel_id=1, source_target_pairs={{0,64},{16,80},{32,96},{48,112},{64,0},{80,16},{96,32},{112,48},{1... | collective-permute-start | bytes 1572872 | tf_op jit(solution)/shard_map/cond/branch_0_fun/ppermute | solution.py:405
  67.3 38.6 %all-to-all-start.1 = ((f32[16,4,8,8,128]{4,3,2,1,0:T(8,128)}), f32[16,4,8,8,128]{4,3,2,1,0:T(8,128)}, u32[]{:S(2)}, u32[]{:S(2)}) async-start(f32[16,4,8,8,128]{4,3,2,1,0:T(8,128)} %solve_columns.5), calls=%async_computation.1 | async-start | bytes 4194304 | tf_op jit(solution)/shard_map/cond/branch_0_fun/all_to_all | solution.py:400
  109.7 34.2 %all-to-all-start.2 = ((f32[16,4,8,8,128]{4,3,2,1,0:T(8,128)}), f32[16,4,8,8,128]{4,3,2,1,0:T(8,128)}, u32[]{:S(2)}, u32[]{:S(2)}) async-start(f32[16,4,8,8,128]{4,3,2,1,0:T(8,128)} %solve_columns.6), calls=%async_computation.2 | async-start | bytes 4194304 | tf_op jit(solution)/shard_map/cond/branch_0_fun/all_to_all | solution.py:400
  119.8 30.1 %collective-permute-start.3 = (f32[8,128,128]{2,1,0:T(8,128)}, f32[8,128,128]{2,1,0:T(8,128)S(1)}, u32[]{:S(2)}, u32[]{:S(2)}) collective-permute-start(f32[8,128,128]{2,1,0:T(8,128)} %get-tuple-element.66), channel_id=1, source_target_pairs={{0,64},{16,80},{32,96},{48,112},{64,0},{80,16},{96,32},{112,48},{1... | collective-permute-start | bytes 1572872 | tf_op jit(solution)/shard_map/cond/branch_0_fun/ppermute | solution.py:405
  149.9 24.0 %copy-start.15 = (bf16[2,256,256]{2,1,0:T(8,128)(2,1)S(1)}, bf16[2,256,256]{2,1,0:T(8,128)(2,1)}, u32[]{:S(2)}) copy-start(bf16[2,256,256]{2,1,0:T(8,128)(2,1)} %get-tuple-element.56.refs_5_.refs_9_.refs_6_) | copy-start | bytes 786436 | tf_op jit(solution)/shard_map/cond
  149.9 23.0 %all-to-all-start.3 = ((f32[16,2,8,8,128]{4,3,2,1,0:T(8,128)}), f32[16,2,8,8,128]{4,3,2,1,0:T(8,128)S(1)}, u32[]{:S(2)}, u32[]{:S(2)}) async-start(f32[16,2,8,8,128]{4,3,2,1,0:T(8,128)} %get-tuple-element.67), calls=%async_computation.3 | async-start | bytes 2097152 | tf_op jit(solution)/shard_map/cond/branch_0_fun/all_to_all | solution.py:400
  155.7 41.7 %collective-permute-start.2 = (f32[8,128,128]{2,1,0:T(8,128)}, f32[8,128,128]{2,1,0:T(8,128)S(1)}, u32[]{:S(2)}, u32[]{:S(2)}) collective-permute-start(f32[8,128,128]{2,1,0:T(8,128)} %get-tuple-element.64), channel_id=1, source_target_pairs={{0,64},{16,80},{32,96},{48,112},{64,0},{80,16},{96,32},{112,48},{1... | collective-permute-start | bytes 1572872 | tf_op jit(solution)/shard_map/cond/branch_0_fun/ppermute | solution.py:405
  172.9 1.0 copy-start.22
  178.4 8.8 %copy-start.2 = (f32[2,8,128,128]{3,2,1,0:T(8,128)S(1)}, f32[2,8,128,128]{3,2,1,0:T(8,128)}, u32[]{:S(2)}) copy-start(f32[2,8,128,128]{3,2,1,0:T(8,128)} %get-tuple-element.71.more_ref) | copy-start | bytes 3145732 | tf_op jit(solution)/shard_map/cond
  178.4 27.6 %collective-permute-start.4 = (f32[8,128,128]{2,1,0:T(8,128)}, f32[8,128,128]{2,1,0:T(8,128)S(1)}, u32[]{:S(2)}, u32[]{:S(2)}) collective-permute-start(f32[8,128,128]{2,1,0:T(8,128)} %get-tuple-element.72), channel_id=1, source_target_pairs={{0,64},{16,80},{32,96},{48,112},{64,0},{80,16},{96,32},{112,48},{1... | collective-permute-start | bytes 1572872 | tf_op jit(solution)/shard_map/cond/branch_0_fun/ppermute | solution.py:405
  187.1 2.6 %copy-start.4 = (f32[2,8,128,128]{3,2,1,0:T(8,128)S(1)}, f32[2,8,128,128]{3,2,1,0:T(8,128)}, u32[]{:S(2)}) copy-start(f32[2,8,128,128]{3,2,1,0:T(8,128)} %get-tuple-element.70.more_ref) | copy-start | bytes 3145732 | tf_op jit(solution)/shard_map/cond
  192.4 2.4 %copy-start.6 = (f32[2,8,128,128]{3,2,1,0:T(8,128)S(1)}, f32[2,8,128,128]{3,2,1,0:T(8,128)}, u32[]{:S(2)}) copy-start(f32[2,8,128,128]{3,2,1,0:T(8,128)} %get-tuple-element.68.more_ref) | copy-start | bytes 3145732 | tf_op jit(solution)/shard_map/cond

commit v5 on v4

--- a/solution.py
+++ b/solution.py
@@ -248,6 +248,10 @@
     return pltpu.with_memory_space_constraint(value, pltpu.HBM)
 
 
+def as_it_comes(arrived):
+    return arrived if arrived.shape[1] == 2 else in_hbm(arrived)
+
+
 def params():
     return pltpu.CompilerParams(dimension_semantics=("arbitrary",), vmem_limit_bytes=VMEM_BYTES)
 
@@ -291,7 +295,7 @@
 
 def solve(arrived, kernel, left, right, ahead=None):
     hbm = pl.BlockSpec(memory_space=pl.ANY)
-    operands = [in_hbm(arrived), kernel, left, right]
+    operands = [as_it_comes(arrived), kernel, left, right]
     specs = [part(arrived.shape, 0), whole(kernel.shape), whole(left.shape), whole(right.shape)]
     if ahead is None:
         shape, place, aliases = (arrived.shape[0], 2) + arrived.shape[2:], 0, {}
@@ -331,7 +335,7 @@
         out_shape=[pltpu.HBM(own, jnp.float32), pltpu.HBM(u.shape, jnp.float32)],
         compiler_params=params(),
         name="inverse_planes",
-    )(plan, in_hbm(arrived), u, orbitals, orbitals, left, right)
+    )(plan, as_it_comes(arrived), u, orbitals, orbitals, left, right)
 
 
 def solve_and_inverse(number, plan, arrived, kernel, left_x, right_x, u, orbitals, left, right):

time: 208 us -> 208 us (level)
  waiting for transfers between devices: 85.5 us -> 87.6 us
    ppermute x6, waiting for transfers between devices: 35.6 us -> 38.9 us  [to_partner(): return lax.ppermute(value, 'band', pairs)]
  transfers between devices with their start and end apart: 10 -> 10, of which waited for: 8 -> 7; matrix products, arithmetic and copies ran while one was open for 3% -> 3% of each run, Pallas kernels for 21% -> 20%
where the time goes in v5:
time: 208 us; the launch traced here: 207 us
  waiting for transfers between devices  87.6 us (42%)
  starting transfers between devices  54.5 us (26%)
  Pallas kernels  48.8 us (23%)
  between operations  6.25 us (3%)
  local copies, waits for them, and re-layouts  6.04 us (3%)
    all_to_all x4, waiting for transfers between devices, exchange(): lax.all_to_all(field, 'grid', split_axis=0, concat_axis=0, tiled=True)  48.8 us
    ppermute x6, waiting for transfers between devices, to_partner(): return lax.ppermute(value, 'band', pairs)  38.9 us
    all_to_all x4, starting transfers between devices, exchange(): lax.all_to_all(field, 'grid', split_axis=0, concat_axis=0, tiled=True)  30.9 us
    ppermute x6, starting transfers between devices, to_partner(): return lax.ppermute(value, 'band', pairs)  23.6 us
    pallas_call x5, Pallas kernels, add_into(): pl.pallas_call(add_kernel, grid_spec=pltpu.PrefetchScalarGridSpec(num_sca...  12.7 us
    pallas_call x3, Pallas kernels, forward(): pl.pallas_call(lambda *refs: forward_kernel(number, *refs), grid_spec=plt...  11.9 us
    pallas_call x2, Pallas kernels, inverse(): pl.pallas_call(lambda *refs: inverse_kernel(number, *refs), grid_spec=plt...  8.65 us
    pallas_call x2, Pallas kernels, solve(): pl.pallas_call(solve_kernel, grid=(1,), in_specs=specs, out_specs=part(sh...  6.1 us
  transfers between devices with their start and end apart: 10, of which 7 were waited for; matrix products, arithmetic and copies ran while one was open for 3% of the time, Pallas kernels for 20%

profile of v5, /device:TPU:1, one launch (start us, length us, event | category | flops | bytes accessed | tf_op | source)
XLA Modules:
  0.0 207.2 jit_solution(14828558333644695780)
XLA Ops:
  0.0 0.0 copy-start.26
  0.0 0.0 copy-start.9
  0.0 3.3 %plan_rounds.1 = (s32[32]{0:T(128)S(1)}, f32[8,128,128]{2,1,0:T(8,128)}) custom-call(s32[128]{0:T(128)} %spin.1, s32[512,1,128]{2,1,0:T(1,128)} %constant.66.clone.table_ref, f32[4,8,128,128]{3,2,1,0:T(8,128)} %orbitals_ref.1), custom_call_target="tpu_custom_call" | custom-call | tf_op jit(solution)/shard_map/plan_rounds/pallas_call | solution.py:100
  3.4 0.0 copy-start.15
  3.4 5.9 %collective-permute-start.12 = (f32[8,128,128]{2,1,0:T(8,128)}, f32[8,128,128]{2,1,0:T(8,128)S(1)}, u32[]{:S(2)}, u32[]{:S(2)}) collective-permute-start(f32[8,128,128]{2,1,0:T(8,128)} %get-tuple-element.113), channel_id=1, source_target_pairs={{0,64},{16,80},{32,96},{48,112},{64,0},{80,16},{96,32},{112,48},{1... | collective-permute-start | bytes 1572872 | tf_op jit(solution)/shard_map/ppermute | solution.py:409
  9.2 0.0 copy-done.26
  9.2 0.1 reshape.64
  9.4 0.6 fusion.6
  13.7 0.1 reduce_sum.9
  13.8 0.7 or_reduce_fusion
  16.4 0.0 copy-done.9
  16.4 1.2 dynamic-slice_bitcast_fusion
  17.6 0.1 broadcast_add_fusion
  17.7 0.2 fusion.3
  18.6 13.0 %collective-permute-done.12 = f32[8,128,128]{2,1,0:T(8,128)S(1)} collective-permute-done((f32[8,128,128]{2,1,0:T(8,128)}, f32[8,128,128]{2,1,0:T(8,128)S(1)}, u32[]{:S(2)}, u32[]{:S(2)}) %collective-permute-start.12) | collective-permute-done | bytes 524320 | tf_op jit(solution)/shard_map/ppermute | solution.py:409
  31.6 0.0 copy-done.15
  31.6 175.6 %conditional.1 = (f32[4,8,128,128]{3,2,1,0:T(8,128)}) conditional(s32[]{:T(128)} %convert_element_type.7, (f32[8,128,128]{2,1,0:T(8,128)}, f32[8,128,128]{2,1,0:T(8,128)S(1)}, s32[32]{0:T(128)S(1)}, f32[4,8,128,128]{3,2,1,0:T(8,128)S(1)}, bf16[2,256,256]{2,1,0:T(8,128)(2,1)S(1)}, /*index=5*/bf16[2,256,256]{2,1,0:T(8,128)(2,1)}, ...), branch_computations={%region_2.3_spmd, %region_3.4_spmd} | conditional | flops 300000116736 | bytes 690702208 | solution.py:466
  31.6 0.0 copy-start.23
  31.6 0.0 copy-start.10
  31.6 0.8 copy-done.23
  32.4 1.9 collective-permute-start
  34.3 4.0 %forward_planes.7 = f32[16,2,8,8,128]{4,3,2,1,0:T(8,128)} custom-call(s32[32]{0:T(128)S(1)} %get-tuple-element.50.refs_0_.plan, f32[8,128,128]{2,1,0:T(8,128)} %copy-done.23, f32[4,8,128,128]{3,2,1,0:T(8,128)S(1)} %get-tuple-element.54.refs_2_.refs_3_.refs_6_.refs_7_.refs_4_, ...), custom_call_target="tpu_custom_call" | custom-call | tf_op jit(solution)/shard_map/cond/branch_0_fun/forward_planes/pallas_call | solution.py:275
  38.3 0.0 copy-done.10
  38.3 8.9 %all-to-all-start = ((f32[16,2,8,8,128]{4,3,2,1,0:T(8,128)}), f32[16,2,8,8,128]{4,3,2,1,0:T(8,128)S(1)}, u32[]{:S(2)}, u32[]{:S(2)}) async-start(f32[16,2,8,8,128]{4,3,2,1,0:T(8,128)} %forward_planes.7), calls=%async_computation | async-start | bytes 2097152 | tf_op jit(solution)/shard_map/cond/branch_0_fun/all_to_all | solution.py:404
  47.2 11.0 %collective-permute-done.refs_1_.refs_5_ = f32[8,128,128]{2,1,0:T(8,128)S(1)} collective-permute-done((f32[8,128,128]{2,1,0:T(8,128)}, f32[8,128,128]{2,1,0:T(8,128)S(1)}, u32[]{:S(2)}, u32[]{:S(2)}) %collective-permute-start) | collective-permute-done | bytes 524320 | tf_op jit(solution)/shard_map/cond/branch_0_fun/ppermute | solution.py:409
  58.2 2.0 collective-permute-start.1
  60.2 4.1 %forward_planes.8.rest_0_ = f32[16,4,8,8,128]{4,3,2,1,0:T(8,128)} custom-call(s32[32]{0:T(128)S(1)} %get-tuple-element.50.refs_0_.plan, f32[8,128,128]{2,1,0:T(8,128)S(1)} %collective-permute-done.refs_1_.refs_5_, f32[4,8,128,128]{3,2,1,0:T(8,128)} %copy-done.10, f32[4,8,128,128]{3,2,1,0:T(8,128)} %copy-done.10, ...), custom_call_target="tpu_custom_call" | custom-call | flops 99999997952 | bytes 200000000 | tf_op jit(solution)/shard_map/cond/branch_0_fun/forward_planes/pallas_call | solution.py:275
  64.4 0.0 all-to-all-done.in_ref
  64.4 0.0 copy-done.14
  64.4 0.0 copy-done.18
  64.4 0.0 copy-done.20
  64.4 2.3 %solve_columns.5 = f32[16,4,8,8,128]{4,3,2,1,0:T(8,128)} custom-call(f32[16,2,8,8,128]{4,3,2,1,0:T(8,128)S(1)} %all-to-all-done.in_ref, f32[8,128,128]{2,1,0:T(8,128)S(1)} %get-tuple-element.57.kernel_ref.refs_2_, bf16[2,256,256]{2,1,0:T(8,128)(2,1)S(1)} %copy-done.18, bf16[2,256,256]{2,1,0:T(8,128)(2,1)S(1)} %copy-done.20, ...), custom_call_target="tpu_custom_call", output_to_operand_aliasing={{}: (4, {})} | custom-call | tf_op jit(solution)/shard_map/cond/branch_0_fun/solve_columns/pallas_call | solution.py:306
  66.7 10.6 %all-to-all-start.1 = ((f32[16,4,8,8,128]{4,3,2,1,0:T(8,128)}), f32[16,4,8,8,128]{4,3,2,1,0:T(8,128)}, u32[]{:S(2)}, u32[]{:S(2)}) async-start(f32[16,4,8,8,128]{4,3,2,1,0:T(8,128)} %solve_columns.5), calls=%async_computation.1 | async-start | bytes 4194304 | tf_op jit(solution)/shard_map/cond/branch_0_fun/all_to_all | solution.py:404
  77.3 8.2 %collective-permute-done.1.refs_1_.refs_2_ = f32[8,128,128]{2,1,0:T(8,128)S(1)} collective-permute-done((f32[8,128,128]{2,1,0:T(8,128)}, f32[8,128,128]{2,1,0:T(8,128)S(1)}, u32[]{:S(2)}, u32[]{:S(2)}) %collective-permute-start.1) | collective-permute-done | bytes 524320 | tf_op jit(solution)/shard_map/cond/branch_0_fun/ppermute | solution.py:409
  85.5 0.0 copy-done.11
  85.5 3.8 %forward_planes.9.rest_0_ = f32[16,4,8,8,128]{4,3,2,1,0:T(8,128)} custom-call(s32[32]{0:T(128)S(1)} %get-tuple-element.50.refs_0_.plan, f32[8,128,128]{2,1,0:T(8,128)S(1)} %collective-permute-done.1.refs_1_.refs_2_, f32[4,8,128,128]{3,2,1,0:T(8,128)S(1)} %copy-done.11, f32[4,8,128,128]{3,2,1,0:T(8,128)S(1)} %copy-done.11, ...), custom_call_target="tpu_custom_call" | custom-call | flops 99999997952 | bytes 200000000 | tf_op jit(solution)/shard_map/cond/branch_0_fun/forward_planes/pallas_call | solution.py:275
  89.3 16.5 %all-to-all-done.1.in_ref.refs_1_ = f32[16,4,8,8,128]{4,3,2,1,0:T(8,128)} async-done(((f32[16,4,8,8,128]{4,3,2,1,0:T(8,128)}), f32[16,4,8,8,128]{4,3,2,1,0:T(8,128)}, u32[]{:S(2)}, u32[]{:S(2)}) %all-to-all-start.1) | async-done | bytes 2097184 | tf_op jit(solution)/shard_map/cond/branch_0_fun/all_to_all | solution.py:404
  105.8 3.8 %solve_columns.6 = f32[16,4,8,8,128]{4,3,2,1,0:T(8,128)} custom-call(f32[16,4,8,8,128]{4,3,2,1,0:T(8,128)} %all-to-all-done.1.in_ref.refs_1_, f32[8,128,128]{2,1,0:T(8,128)} %copy-done.14, bf16[2,256,256]{2,1,0:T(8,128)(2,1)} %get-tuple-element.58.left_ref.refs_3_, ...), custom_call_target="tpu_custom_call", output_to_operand_aliasing={{}: (4, {})} | custom-call | tf_op jit(solution)/shard_map/cond/branch_0_fun/solve_columns/pallas_call | solution.py:306
  109.6 5.7 %all-to-all-start.2 = ((f32[16,4,8,8,128]{4,3,2,1,0:T(8,128)}), f32[16,4,8,8,128]{4,3,2,1,0:T(8,128)}, u32[]{:S(2)}, u32[]{:S(2)}) async-start(f32[16,4,8,8,128]{4,3,2,1,0:T(8,128)} %solve_columns.6), calls=%async_computation.2 | async-start | bytes 4194304 | tf_op jit(solution)/shard_map/cond/branch_0_fun/all_to_all | solution.py:404
  115.3 4.4 %inverse_planes.5 = (f32[2,8,128,128]{3,2,1,0:T(8,128)}, f32[8,128,128]{2,1,0:T(8,128)}) custom-call(s32[32]{0:T(128)S(1)} %get-tuple-element.50.refs_0_.plan, f32[16,4,8,8,128]{4,3,2,1,0:T(8,128)} %all-to-all-done.1.in_ref.refs_1_, f32[8,128,128]{2,1,0:T(8,128)} %copy-done.23, f32[4,8,128,128]{3,2,1,0:T(8,128)S(1)} %copy-done.11, ...), custom_call_target="tpu_custom_call" | custom-call | tf_op jit(solution)/shard_map/cond/branch_0_fun/inverse_planes/pallas_call | solution.py:320
  119.7 4.5 %collective-permute-start.3 = (f32[8,128,128]{2,1,0:T(8,128)}, f32[8,128,128]{2,1,0:T(8,128)S(1)}, u32[]{:S(2)}, u32[]{:S(2)}) collective-permute-start(f32[8,128,128]{2,1,0:T(8,128)} %get-tuple-element.66), channel_id=1, source_target_pairs={{0,64},{16,80},{32,96},{48,112},{64,0},{80,16},{96,32},{112,48},{1... | collective-permute-start | bytes 1572872 | tf_op jit(solution)/shard_map/cond/branch_0_fun/ppermute | solution.py:409
  124.2 19.6 %all-to-all-done.2.refs_1_ = f32[16,4,8,8,128]{4,3,2,1,0:T(8,128)} async-done(((f32[16,4,8,8,128]{4,3,2,1,0:T(8,128)}), f32[16,4,8,8,128]{4,3,2,1,0:T(8,128)}, u32[]{:S(2)}, u32[]{:S(2)}) %all-to-all-start.2) | async-done | bytes 2097184 | tf_op jit(solution)/shard_map/cond/branch_0_fun/all_to_all | solution.py:404
  143.8 6.1 %solve_and_inverse.2 = (f32[16,2,8,8,128]{4,3,2,1,0:T(8,128)}, f32[2,8,128,128]{3,2,1,0:T(8,128)}, f32[8,128,128]{2,1,0:T(8,128)}) custom-call(s32[32]{0:T(128)S(1)} %get-tuple-element.50.refs_0_.plan, f32[16,4,8,8,128]{4,3,2,1,0:T(8,128)} %all-to-all-done.2.refs_1_, f32[8,128,128]{2,1,0:T(8,128)} %copy-done.14, ...), custom_call_target="tpu_custom_call" | custom-call | tf_op jit(solution)/shard_map/cond/branch_0_fun/solve_and_inverse/pallas_call | solution.py:344
  149.9 0.0 collective-permute-done.3
  149.9 5.8 %all-to-all-start.3 = ((f32[16,2,8,8,128]{4,3,2,1,0:T(8,128)}), f32[16,2,8,8,128]{4,3,2,1,0:T(8,128)S(1)}, u32[]{:S(2)}, u32[]{:S(2)}) async-start(f32[16,2,8,8,128]{4,3,2,1,0:T(8,128)} %get-tuple-element.67), calls=%async_computation.3 | async-start | bytes 2097152 | tf_op jit(solution)/shard_map/cond/branch_0_fun/all_to_all | solution.py:404
  155.7 4.6 %collective-permute-start.2 = (f32[8,128,128]{2,1,0:T(8,128)}, f32[8,128,128]{2,1,0:T(8,128)S(1)}, u32[]{:S(2)}, u32[]{:S(2)}) collective-permute-start(f32[8,128,128]{2,1,0:T(8,128)} %get-tuple-element.64), channel_id=1, source_target_pairs={{0,64},{16,80},{32,96},{48,112},{64,0},{80,16},{96,32},{112,48},{1... | collective-permute-start | bytes 1572872 | tf_op jit(solution)/shard_map/cond/branch_0_fun/ppermute | solution.py:409
  160.3 12.6 %all-to-all-done.3.refs_1_ = f32[16,2,8,8,128]{4,3,2,1,0:T(8,128)S(1)} async-done(((f32[16,2,8,8,128]{4,3,2,1,0:T(8,128)}), f32[16,2,8,8,128]{4,3,2,1,0:T(8,128)S(1)}, u32[]{:S(2)}, u32[]{:S(2)}) %all-to-all-start.3) | async-done | bytes 1048608 | tf_op jit(solution)/shard_map/cond/branch_0_fun/all_to_all | solution.py:404
  172.9 0.0 copy-done.16
  172.9 4.3 %inverse_planes.6 = (f32[2,8,128,128]{3,2,1,0:T(8,128)}, f32[8,128,128]{2,1,0:T(8,128)}) custom-call(s32[32]{0:T(128)S(1)} %get-tuple-element.50.refs_0_.plan, f32[16,2,8,8,128]{4,3,2,1,0:T(8,128)S(1)} %all-to-all-done.3.refs_1_, f32[8,128,128]{2,1,0:T(8,128)S(1)} %collective-permute-done.1.refs_1_.refs_2_, f32[4,8,128,128]{3,2,1,0:T(8,128)} %copy-done.10, ...), custom_call_target="tpu_custom_call" | custom-call | tf_op jit(solution)/shard_map/cond/branch_0_fun/inverse_planes/pallas_call | solution.py:320
  177.2 4.7 %collective-permute-start.4 = (f32[8,128,128]{2,1,0:T(8,128)}, f32[8,128,128]{2,1,0:T(8,128)S(1)}, u32[]{:S(2)}, u32[]{:S(2)}) collective-permute-start(f32[8,128,128]{2,1,0:T(8,128)} %get-tuple-element.72), channel_id=1, source_target_pairs={{0,64},{16,80},{32,96},{48,112},{64,0},{80,16},{96,32},{112,48},{1... | collective-permute-start | bytes 1572872 | tf_op jit(solution)/shard_map/cond/branch_0_fun/ppermute | solution.py:409
  181.9 0.6 slice.10
  184.4 1.6 broadcast_5_sum_ref.0.sum_ref
  186.0 0.0 copy-done.2
  186.0 2.6 %add_terms.12.sum_ref = f32[4,8,128,128]{3,2,1,0:T(8,128)} custom-call(s32[32]{0:T(128)S(1)} %get-tuple-element.50.refs_0_.plan, f32[2,8,128,128]{3,2,1,0:T(8,128)S(1)} %copy-done.2, f32[4,8,128,128]{3,2,1,0:T(8,128)} %broadcast_5_sum_ref.0.sum_ref), custom_call_target="tpu_custom_call", output_to_operand_aliasing={{}: (2, {})} | custom-call | tf_op jit(solution)/shard_map/cond/branch_0_fun/add_terms/pallas_call | solution.py:374
  188.6 0.0 copy-done.4
  188.6 2.6 %add_terms.13.sum_ref = f32[4,8,128,128]{3,2,1,0:T(8,128)} custom-call(s32[32]{0:T(128)S(1)} %get-tuple-element.50.refs_0_.plan, f32[2,8,128,128]{3,2,1,0:T(8,128)S(1)} %copy-done.4, f32[4,8,128,128]{3,2,1,0:T(8,128)} %add_terms.12.sum_ref), custom_call_target="tpu_custom_call", output_to_operand_aliasing={{}: (2, {})} | custom-call | tf_op jit(solution)/shard_map/cond/branch_0_fun/add_terms/pallas_call | solution.py:374
  191.2 2.4 %add_terms.14.sum_ref = f32[4,8,128,128]{3,2,1,0:T(8,128)} custom-call(s32[32]{0:T(128)S(1)} %get-tuple-element.50.refs_0_.plan, f32[1,8,128,128]{3,2,1,0:T(8,128)S(1)} %bitcast.30, f32[4,8,128,128]{3,2,1,0:T(8,128)} %add_terms.13.sum_ref), custom_call_target="tpu_custom_call", output_to_operand_aliasing={{}: (2, {})} | custom-call | tf_op jit(solution)/shard_map/cond/branch_0_fun/add_terms/pallas_call | solution.py:374
  193.6 0.0 copy-done.6
  193.6 2.6 %add_terms.15.sum_ref = f32[4,8,128,128]{3,2,1,0:T(8,128)} custom-call(s32[32]{0:T(128)S(1)} %get-tuple-element.50.refs_0_.plan, f32[2,8,128,128]{3,2,1,0:T(8,128)S(1)} %copy-done.6, f32[4,8,128,128]{3,2,1,0:T(8,128)} %add_terms.14.sum_ref), custom_call_target="tpu_custom_call", output_to_operand_aliasing={{}: (2, {})} | custom-call | tf_op jit(solution)/shard_map/cond/branch_0_fun/add_terms/pallas_call | solution.py:374
  196.3 0.0 collective-permute-done.2
  196.3 2.4 %add_terms.16 = f32[4,8,128,128]{3,2,1,0:T(8,128)} custom-call(s32[32]{0:T(128)S(1)} %get-tuple-element.50.refs_0_.plan, f32[1,8,128,128]{3,2,1,0:T(8,128)S(1)} %bitcast.32, f32[4,8,128,128]{3,2,1,0:T(8,128)} %add_terms.15.sum_ref), custom_call_target="tpu_custom_call", output_to_operand_aliasing={{}: (2, {})} | custom-call | tf_op jit(solution)/shard_map/cond/branch_0_fun/add_terms/pallas_call | solution.py:374
  198.7 1.1 constant_dynamic-slice_fusion
  199.8 6.6 %collective-permute-done.4 = f32[8,128,128]{2,1,0:T(8,128)S(1)} collective-permute-done((f32[8,128,128]{2,1,0:T(8,128)}, f32[8,128,128]{2,1,0:T(8,128)S(1)}, u32[]{:S(2)}, u32[]{:S(2)}) %collective-permute-start.4) | collective-permute-done | bytes 524320 | tf_op jit(solution)/shard_map/cond/branch_0_fun/ppermute | solution.py:409
  206.4 0.9 bitcast_dynamic-update-slice_fusion
  (10 shorter events, 0.0 us)
Async XLA Ops:
  0.0 9.2 %copy-start.26 = (s32[128]{0:T(128)S(1)}, s32[128]{0:T(128)}, u32[]{:S(2)}) copy-start(s32[128]{0:T(128)} %spin.1) | copy-start | bytes 1540
  0.0 16.4 %copy-start.9 = (f32[4,8,128,128]{3,2,1,0:T(8,128)S(1)}, f32[4,8,128,128]{3,2,1,0:T(8,128)}, u32[]{:S(2)}) copy-start(f32[4,8,128,128]{3,2,1,0:T(8,128)} %orbitals_ref.1) | copy-start | bytes 6291460
  3.4 28.3 %copy-start.15 = (bf16[2,256,256]{2,1,0:T(8,128)(2,1)S(1)}, bf16[2,256,256]{2,1,0:T(8,128)(2,1)}, u32[]{:S(2)}) copy-start(bf16[2,256,256]{2,1,0:T(8,128)(2,1)} %constant.69.clone) | copy-start | bytes 786436
  3.4 28.3 %collective-permute-start.12 = (f32[8,128,128]{2,1,0:T(8,128)}, f32[8,128,128]{2,1,0:T(8,128)S(1)}, u32[]{:S(2)}, u32[]{:S(2)}) collective-permute-start(f32[8,128,128]{2,1,0:T(8,128)} %get-tuple-element.113), channel_id=1, source_target_pairs={{0,64},{16,80},{32,96},{48,112},{64,0},{80,16},{96,32},{112,48},{1... | collective-permute-start | bytes 1572872 | tf_op jit(solution)/shard_map/ppermute | solution.py:409
  31.6 0.8 copy-start.23
  31.6 6.7 %copy-start.10 = (f32[4,8,128,128]{3,2,1,0:T(8,128)}, f32[4,8,128,128]{3,2,1,0:T(8,128)S(1)}, u32[]{:S(2)}) copy-start(f32[4,8,128,128]{3,2,1,0:T(8,128)S(1)} %get-tuple-element.54.refs_2_.refs_3_.refs_6_.refs_7_.refs_4_) | copy-start | bytes 6291460 | tf_op jit(solution)/shard_map/cond
  31.6 32.7 %copy-start.14 = (f32[8,128,128]{2,1,0:T(8,128)}, f32[8,128,128]{2,1,0:T(8,128)S(1)}, u32[]{:S(2)}) copy-start(f32[8,128,128]{2,1,0:T(8,128)S(1)} %get-tuple-element.57.kernel_ref.refs_2_) | copy-start | bytes 1572868 | tf_op jit(solution)/shard_map/cond
  32.4 25.7 %collective-permute-start = (f32[8,128,128]{2,1,0:T(8,128)}, f32[8,128,128]{2,1,0:T(8,128)S(1)}, u32[]{:S(2)}, u32[]{:S(2)}) collective-permute-start(f32[8,128,128]{2,1,0:T(8,128)} %get-tuple-element.61), channel_id=1, source_target_pairs={{0,64},{16,80},{32,96},{48,112},{64,0},{80,16},{96,32},{112,48},{1... | collective-permute-start | bytes 1572872 | tf_op jit(solution)/shard_map/cond/branch_0_fun/ppermute | solution.py:409
  38.3 26.1 %all-to-all-start = ((f32[16,2,8,8,128]{4,3,2,1,0:T(8,128)}), f32[16,2,8,8,128]{4,3,2,1,0:T(8,128)S(1)}, u32[]{:S(2)}, u32[]{:S(2)}) async-start(f32[16,2,8,8,128]{4,3,2,1,0:T(8,128)} %forward_planes.7), calls=%async_computation | async-start | bytes 2097152 | tf_op jit(solution)/shard_map/cond/branch_0_fun/all_to_all | solution.py:404
  58.2 6.2 %copy-start.18 = (bf16[2,256,256]{2,1,0:T(8,128)(2,1)S(1)}, bf16[2,256,256]{2,1,0:T(8,128)(2,1)}, u32[]{:S(2)}) copy-start(bf16[2,256,256]{2,1,0:T(8,128)(2,1)} %get-tuple-element.58.left_ref.refs_3_) | copy-start | bytes 786436 | tf_op jit(solution)/shard_map/cond
  58.2 6.2 %copy-start.20 = (bf16[2,256,256]{2,1,0:T(8,128)(2,1)S(1)}, bf16[2,256,256]{2,1,0:T(8,128)(2,1)}, u32[]{:S(2)}) copy-start(bf16[2,256,256]{2,1,0:T(8,128)(2,1)} %get-tuple-element.59.right_ref.refs_4_) | copy-start | bytes 786436 | tf_op jit(solution)/shard_map/cond
  58.2 27.3 %collective-permute-start.1 = (f32[8,128,128]{2,1,0:T(8,128)}, f32[8,128,128]{2,1,0:T(8,128)S(1)}, u32[]{:S(2)}, u32[]{:S(2)}) collective-permute-start(f32[8,128,128]{2,1,0:T(8,128)} %get-tuple-element.63), channel_id=1, source_target_pairs={{0,64},{16,80},{32,96},{48,112},{64,0},{80,16},{96,32},{112,48},{1... | collective-permute-start | bytes 1572872 | tf_op jit(solution)/shard_map/cond/branch_0_fun/ppermute | solution.py:409
  66.7 18.8 %copy-start.11 = (f32[4,8,128,128]{3,2,1,0:T(8,128)S(1)}, f32[4,8,128,128]{3,2,1,0:T(8,128)}, u32[]{:S(2)}) copy-start(f32[4,8,128,128]{3,2,1,0:T(8,128)} %copy-done.10) | copy-start | bytes 6291460 | tf_op jit(solution)/shard_map/cond
  66.7 39.1 %all-to-all-start.1 = ((f32[16,4,8,8,128]{4,3,2,1,0:T(8,128)}), f32[16,4,8,8,128]{4,3,2,1,0:T(8,128)}, u32[]{:S(2)}, u32[]{:S(2)}) async-start(f32[16,4,8,8,128]{4,3,2,1,0:T(8,128)} %solve_columns.5), calls=%async_computation.1 | async-start | bytes 4194304 | tf_op jit(solution)/shard_map/cond/branch_0_fun/all_to_all | solution.py:404
  109.6 34.2 %all-to-all-start.2 = ((f32[16,4,8,8,128]{4,3,2,1,0:T(8,128)}), f32[16,4,8,8,128]{4,3,2,1,0:T(8,128)}, u32[]{:S(2)}, u32[]{:S(2)}) async-start(f32[16,4,8,8,128]{4,3,2,1,0:T(8,128)} %solve_columns.6), calls=%async_computation.2 | async-start | bytes 4194304 | tf_op jit(solution)/shard_map/cond/branch_0_fun/all_to_all | solution.py:404
  119.7 30.2 %collective-permute-start.3 = (f32[8,128,128]{2,1,0:T(8,128)}, f32[8,128,128]{2,1,0:T(8,128)S(1)}, u32[]{:S(2)}, u32[]{:S(2)}) collective-permute-start(f32[8,128,128]{2,1,0:T(8,128)} %get-tuple-element.66), channel_id=1, source_target_pairs={{0,64},{16,80},{32,96},{48,112},{64,0},{80,16},{96,32},{112,48},{1... | collective-permute-start | bytes 1572872 | tf_op jit(solution)/shard_map/cond/branch_0_fun/ppermute | solution.py:409
  149.9 23.0 %copy-start.16 = (bf16[2,256,256]{2,1,0:T(8,128)(2,1)S(1)}, bf16[2,256,256]{2,1,0:T(8,128)(2,1)}, u32[]{:S(2)}) copy-start(bf16[2,256,256]{2,1,0:T(8,128)(2,1)} %get-tuple-element.56.refs_5_.refs_9_.refs_6_) | copy-start | bytes 786436 | tf_op jit(solution)/shard_map/cond
  149.9 23.0 %all-to-all-start.3 = ((f32[16,2,8,8,128]{4,3,2,1,0:T(8,128)}), f32[16,2,8,8,128]{4,3,2,1,0:T(8,128)S(1)}, u32[]{:S(2)}, u32[]{:S(2)}) async-start(f32[16,2,8,8,128]{4,3,2,1,0:T(8,128)} %get-tuple-element.67), calls=%async_computation.3 | async-start | bytes 2097152 | tf_op jit(solution)/shard_map/cond/branch_0_fun/all_to_all | solution.py:404
  155.7 40.5 %collective-permute-start.2 = (f32[8,128,128]{2,1,0:T(8,128)}, f32[8,128,128]{2,1,0:T(8,128)S(1)}, u32[]{:S(2)}, u32[]{:S(2)}) collective-permute-start(f32[8,128,128]{2,1,0:T(8,128)} %get-tuple-element.64), channel_id=1, source_target_pairs={{0,64},{16,80},{32,96},{48,112},{64,0},{80,16},{96,32},{112,48},{1... | collective-permute-start | bytes 1572872 | tf_op jit(solution)/shard_map/cond/branch_0_fun/ppermute | solution.py:409
  177.2 8.8 %copy-start.2 = (f32[2,8,128,128]{3,2,1,0:T(8,128)S(1)}, f32[2,8,128,128]{3,2,1,0:T(8,128)}, u32[]{:S(2)}) copy-start(f32[2,8,128,128]{3,2,1,0:T(8,128)} %get-tuple-element.71.more_ref) | copy-start | bytes 3145732 | tf_op jit(solution)/shard_map/cond
  177.2 29.2 %collective-permute-start.4 = (f32[8,128,128]{2,1,0:T(8,128)}, f32[8,128,128]{2,1,0:T(8,128)S(1)}, u32[]{:S(2)}, u32[]{:S(2)}) collective-permute-start(f32[8,128,128]{2,1,0:T(8,128)} %get-tuple-element.72), channel_id=1, source_target_pairs={{0,64},{16,80},{32,96},{48,112},{64,0},{80,16},{96,32},{112,48},{1... | collective-permute-start | bytes 1572872 | tf_op jit(solution)/shard_map/cond/branch_0_fun/ppermute | solution.py:409
  186.0 2.6 %copy-start.4 = (f32[2,8,128,128]{3,2,1,0:T(8,128)S(1)}, f32[2,8,128,128]{3,2,1,0:T(8,128)}, u32[]{:S(2)}) copy-start(f32[2,8,128,128]{3,2,1,0:T(8,128)} %get-tuple-element.70.more_ref) | copy-start | bytes 3145732 | tf_op jit(solution)/shard_map/cond
  191.2 2.4 %copy-start.6 = (f32[2,8,128,128]{3,2,1,0:T(8,128)S(1)}, f32[2,8,128,128]{3,2,1,0:T(8,128)}, u32[]{:S(2)}) copy-start(f32[2,8,128,128]{3,2,1,0:T(8,128)} %get-tuple-element.68.more_ref) | copy-start | bytes 3145732 | tf_op jit(solution)/shard_map/cond
